TPU v7x, 32 devices: a whole 2x2x4 slice. The times are simulated.
32 devices in a mesh: grp: 2 (over core), dp: 16 (over z, y, x).
Axes of the slice: x: 2, y: 2, z: 4, core: 2. Of those that a mesh axis runs over, the one named last changes fastest.
Arguments:
- params: float32 [2, 8888320], P('grp', 'dp'), may hold values from -8 to 8
- first_moment: float32 [2, 8888320], P('grp', 'dp'), may hold values from -1 to 1
- second_moment: float32 [2, 8888320], P('grp', 'dp'), may hold values from 0 to 1, as said below
- average: float32 [2, 8888320], P('grp', 'dp'), may hold values from -8 to 8
- pixels: bfloat16 [25088, 768], P('dp'), may hold values from -6 to 6
- visible_index: int32 [128, 64], P('dp'), may hold values from 0 to 195, as said below
- visible_count: int32 [128], P('dp'), may hold values from 32 to 64, as said below
- gsd_id: int32 [128], P('dp'), may hold values from 0 to 6
Outputs:
- new_params: float32 [2, 8888320], P('grp', 'dp')
- new_first_moment: float32 [2, 8888320], P('grp', 'dp')
- new_second_moment: float32 [2, 8888320], P('grp', 'dp')
- new_average: float32 [2, 8888320], P('grp', 'dp')
- loss_sum: float32 [], replicated
- masked_total: float32 [], replicated
- grad_norm: float32 [], replicated
Inputs may be any that keep to these rules, and one draw needn't show every extreme that they name: `visible_count`: the first image of every block of 8 images has 64 visible patches. `visible_index`: the entries of a row are different positions; the first visible_count entries are the visible patches, the others are not read. `second_moment`: positive.
All inputs are finite; a program needn't handle non-finite values.
Results may differ from a plain program's by a relative error of at most 0.00045.
The roundings to bfloat16 on the way count: a program that leaves them out, or rounds other values in their place, can miss the bound.
Values may be sent and summed in bfloat16 or wider, within the bound.
A program may use at most 448 MiB of HBM per device.

v0:
```python
import math

import jax
import jax.numpy as jnp
from jax import lax
from jax.sharding import PartitionSpec as P

DE = 1024
HE = 16
FE = 4096
DD = 512
HD = 16
FD = 2048
PSIDE = 16
GSIDE = 14
VMAX = 64
STEP = 10
PIX = 768
LOWPIX = 192
GRID = 196
NDEC = 3644352


HIGHEST = lax.Precision.HIGHEST
CLIP = 0.05
RATE = 0.01
BETA_ONE = 0.5
BETA_TWO = 0.5
ADAM_EPS = 1e-08
DECAY_WEIGHT = 0.05
AVERAGE_KEEP = 0.9
NORM_EPS = 1e-06
MASK_FILL = -1000000000.0


def shifted_2(block, axis, distance):
    devices = range(lax.axis_size(axis))
    route = [(i - distance, i) for i in devices if i - distance in devices]
    return lax.ppermute(block, axis, route)


def shortened(array):
    return jax.tree.map(lambda a: a.astype(jnp.bfloat16) if a.dtype == jnp.float32 else a, array)


def encoder_row_layout():
    return [
        ("pe_w", (PIX, DE)),
        ("pe_b", (DE,)),
        ("ln1_g", (DE,)),
        ("ln1_b", (DE,)),
        ("qkv_w", (DE, 3 * DE)),
        ("ln2_g", (DE,)),
        ("ln2_b", (DE,)),
        ("fc1_w", (DE, FE)),
        ("fc1_b", (FE,)),
        ("fc2_b", (DE,)),
        ("lnf_g", (DE,)),
        ("lnf_b", (DE,)),
        ("emb_w", (DE, DD)),
        ("emb_b", (DD,)),
    ]


def decoder_layout():
    return [
        ("mask_tok", (DD,)),
        ("ln1_g", (DD,)),
        ("ln1_b", (DD,)),
        ("qkv_w", (DD, 3 * DD)),
        ("out_w", (DD, DD)),
        ("ln2_g", (DD,)),
        ("ln2_b", (DD,)),
        ("fc1_w", (DD, FD)),
        ("fc1_b", (FD,)),
        ("fc2_w", (FD, DD)),
        ("fc2_b", (DD,)),
        ("lnf_g", (DD,)),
        ("lnf_b", (DD,)),
        ("head_w", (DD, LOWPIX + PIX)),
        ("head_b", (LOWPIX + PIX,)),
    ]


def unpack(flat, layout):
    tensors = {}
    offset = 0
    for section_name, section_shape in layout:
        extent = math.prod(section_shape)
        tensors[section_name] = flat[offset : offset + extent].reshape(section_shape)
        offset += extent
    return tensors


def flatten(grads, layout, flat_length):
    pieces = [grads[section_name].reshape(-1) for section_name, section_shape in layout]
    used = jnp.concatenate(pieces)
    return jnp.concatenate([used, jnp.zeros((flat_length - used.shape[0],), jnp.float32)])


def packing(counts, index_rows):
    images = counts.shape[0]
    starts = (jnp.cumsum(counts) - counts).astype(jnp.int32)
    row_ids = jnp.arange(images * VMAX, dtype=jnp.int32)
    owner_image = (
        jnp.sum((row_ids[:, None] >= starts[None, :]).astype(jnp.int32), axis=1) - 1
    ).astype(jnp.int32)
    within = row_ids - starts[owner_image]
    is_valid = row_ids < jnp.sum(counts).astype(jnp.int32)
    position = index_rows[owner_image, jnp.clip(within, 0, VMAX - 1)].astype(jnp.int32)
    grid_row = jnp.where(is_valid, owner_image * GRID + position, images * GRID).astype(jnp.int32)
    segment = jnp.where(is_valid, owner_image, -1).astype(jnp.int32)
    return (grid_row, segment, is_valid, position)


def position_code(position, scales, width):
    quarter = width // 4
    frequency = jnp.exp(jnp.arange(quarter, dtype=jnp.float32) * (-math.log(10000.0) / quarter))
    row_angle = ((position // GSIDE).astype(jnp.float32) * scales)[:, None] * frequency[None, :]
    col_angle = ((position % GSIDE).astype(jnp.float32) * scales)[:, None] * frequency[None, :]
    return jnp.concatenate(
        [jnp.sin(row_angle), jnp.cos(row_angle), jnp.sin(col_angle), jnp.cos(col_angle)], axis=1
    )


def bands(pixel_rows):
    pixel_ids = jnp.arange(PIX, dtype=jnp.int32)
    coarse = (
        pixel_ids // (3 * PSIDE) // 2 * (PSIDE // 2) + pixel_ids // 3 % PSIDE // 2
    ) * 3 + pixel_ids % 3
    pool_table = (coarse[:, None] == jnp.arange(LOWPIX, dtype=jnp.int32)[None, :]).astype(
        jnp.float32
    )
    low_band = jnp.dot(pixel_rows, pool_table, precision=HIGHEST) * 0.25
    high_band = pixel_rows - jnp.dot(low_band, pool_table.T, precision=HIGHEST)
    return (low_band, high_band)


def linear(left, right):
    return jnp.einsum("blk,kn->bln", left, right, preferred_element_type=jnp.float32)


def weight_grad(left, grad_rows):
    return jnp.einsum("blk,bln->kn", left, grad_rows, preferred_element_type=jnp.float32)


def input_grad(grad_rows, right):
    return jnp.einsum("bln,kn->blk", grad_rows, right, preferred_element_type=jnp.float32)


def norm_forward(state, gain, shift):
    centered = state - jnp.mean(state, axis=-1, keepdims=True)
    inverse = lax.rsqrt(jnp.mean(centered * centered, axis=-1, keepdims=True) + NORM_EPS)
    unit_rows = centered * inverse
    return (unit_rows * gain.astype(jnp.float32) + shift.astype(jnp.float32), unit_rows, inverse)


def norm_backward(grad_out, unit_rows, inverse, gain):
    grad_unit = grad_out * gain.astype(jnp.float32)
    grad_in = inverse * (
        grad_unit
        - jnp.mean(grad_unit, axis=-1, keepdims=True)
        - unit_rows * jnp.mean(grad_unit * unit_rows, axis=-1, keepdims=True)
    )
    return (grad_in, jnp.sum(grad_out * unit_rows, axis=(0, 1)), jnp.sum(grad_out, axis=(0, 1)))


def attention_scores(query_part, key_part, bias):
    head_dim = query_part.shape[-1]
    return (
        jnp.einsum("blhd,bmhd->bhlm", query_part, key_part, preferred_element_type=jnp.float32)
        * head_dim ** (-0.5)
        + bias
    )


def gelu_exact(values):
    return jax.nn.gelu(values, approximate=False)


def block_forward(state, weights, heads, bias):
    batch, length, width = state.shape
    normed_one, unit_one, inverse_one = norm_forward(state, weights["ln1_g"], weights["ln1_b"])
    normed_one = normed_one.astype(jnp.bfloat16)
    qkv = (
        linear(normed_one, weights["qkv_w"])
        .astype(jnp.bfloat16)
        .reshape(batch, length, 3, heads, width // heads)
    )
    scores = attention_scores(qkv[:, :, 0], qkv[:, :, 1], bias)
    row_max = jnp.max(scores, axis=-1, keepdims=True)
    shifted = jnp.exp(scores - row_max)
    totals = jnp.sum(shifted, axis=-1, keepdims=True)
    attend = (shifted / totals).astype(jnp.bfloat16)
    logsum = row_max + jnp.log(totals)
    mixed = jnp.einsum("bhlm,bmhd->blhd", attend, qkv[:, :, 2], preferred_element_type=jnp.float32)
    mixed = mixed.astype(jnp.bfloat16).reshape(batch, length, width)
    middle = state + linear(mixed, weights["out_w"])
    normed_two, unit_two, inverse_two = norm_forward(middle, weights["ln2_g"], weights["ln2_b"])
    normed_two = normed_two.astype(jnp.bfloat16)
    pre_act = linear(normed_two, weights["fc1_w"]) + weights["fc1_b"].astype(jnp.float32)
    active = gelu_exact(pre_act).astype(jnp.bfloat16)
    output = middle + linear(active, weights["fc2_w"]) + weights["fc2_b"].astype(jnp.float32)
    kept = {
        "normed_one": normed_one,
        "unit_one": unit_one,
        "inverse_one": inverse_one,
        "qkv": qkv,
        "logsum": logsum,
        "mixed": mixed,
        "unit_two": unit_two,
        "inverse_two": inverse_two,
        "normed_two": normed_two,
        "active": active,
    }
    kept["pre_act"] = pre_act
    return (output, kept)


def block_backward(grad_out, kept, weights, heads, bias):
    batch, length, width = grad_out.shape
    grads = {}
    grad_low = grad_out.astype(jnp.bfloat16)
    grads["fc2_w"] = weight_grad(kept["active"], grad_low)
    grads["fc2_b"] = jnp.sum(grad_out, axis=(0, 1))
    pre_act = kept["pre_act"]
    _, gelu_back = jax.vjp(gelu_exact, pre_act)
    grad_pre = gelu_back(input_grad(grad_low, weights["fc2_w"]))[0]
    grads["fc1_b"] = jnp.sum(grad_pre, axis=(0, 1))
    grad_pre_low = grad_pre.astype(jnp.bfloat16)
    grads["fc1_w"] = weight_grad(kept["normed_two"], grad_pre_low)
    grad_norm_in, grads["ln2_g"], grads["ln2_b"] = norm_backward(
        input_grad(grad_pre_low, weights["fc1_w"]),
        kept["unit_two"],
        kept["inverse_two"],
        weights["ln2_g"],
    )
    grad_mid = grad_out + grad_norm_in
    grad_mid_low = grad_mid.astype(jnp.bfloat16)
    grads["out_w"] = weight_grad(kept["mixed"], grad_mid_low)
    grad_mixed = (
        input_grad(grad_mid_low, weights["out_w"])
        .astype(jnp.bfloat16)
        .reshape(batch, length, heads, width // heads)
    )
    qkv = kept["qkv"]
    query_part, key_part, value_part = (qkv[:, :, 0], qkv[:, :, 1], qkv[:, :, 2])
    attend = jnp.exp(attention_scores(query_part, key_part, bias) - kept["logsum"])
    grad_value = jnp.einsum(
        "bhlm,blhd->bmhd",
        attend.astype(jnp.bfloat16),
        grad_mixed,
        preferred_element_type=jnp.float32,
    )
    grad_attend = jnp.einsum(
        "blhd,bmhd->bhlm", grad_mixed, value_part, preferred_element_type=jnp.float32
    )
    grad_scores = (
        attend * (grad_attend - jnp.sum(grad_attend * attend, axis=-1, keepdims=True))
    ).astype(jnp.bfloat16)
    score_scale = (width // heads) ** (-0.5)
    grad_query = (
        jnp.einsum("bhlm,bmhd->blhd", grad_scores, key_part, preferred_element_type=jnp.float32)
        * score_scale
    )
    grad_key = (
        jnp.einsum("bhlm,blhd->bmhd", grad_scores, query_part, preferred_element_type=jnp.float32)
        * score_scale
    )
    grad_qkv = (
        jnp.stack([grad_query, grad_key, grad_value], axis=2)
        .reshape(batch, length, 3 * width)
        .astype(jnp.bfloat16)
    )
    grads["qkv_w"] = weight_grad(kept["normed_one"], grad_qkv)
    grad_norm_in, grads["ln1_g"], grads["ln1_b"] = norm_backward(
        input_grad(grad_qkv, weights["qkv_w"]),
        kept["unit_one"],
        kept["inverse_one"],
        weights["ln1_g"],
    )
    return (grad_mid + grad_norm_in, grads)


def encoder_bias(segment):
    return jnp.where(segment[:, None] == segment[None, :], 0.0, MASK_FILL)[None, None]


def encoder_forward(weights, pixel_rows, grid_row, segment, is_valid, position, image_scale):
    total_rows = pixel_rows.shape[0]
    width = weights["pe_w"].shape[1]
    patches = jnp.where(is_valid[:, None], pixel_rows[jnp.minimum(grid_row, total_rows - 1)], 0)[
        None
    ]
    state = (
        linear(patches, weights["pe_w"])
        + weights["pe_b"].astype(jnp.float32)
        + position_code(position, image_scale[jnp.maximum(segment, 0)], width)[None]
    )
    state, kept = block_forward(state, weights, HE, encoder_bias(segment))
    normed, unit_rows, inverse = norm_forward(state, weights["lnf_g"], weights["lnf_b"])
    normed = normed.astype(jnp.bfloat16)
    sent = (linear(normed, weights["emb_w"]) + weights["emb_b"].astype(jnp.float32)).astype(
        jnp.bfloat16
    )[0]
    return (sent, (patches, kept, normed, unit_rows, inverse))


def encoder_backward(weights, saved, grad_sent, segment, flat_length):
    patches, kept, normed, unit_rows, inverse = saved
    grads = {}
    grad_rows = grad_sent[None]
    grads["emb_w"] = weight_grad(normed, grad_rows)
    grads["emb_b"] = jnp.sum(grad_sent.astype(jnp.float32), axis=0)
    grad_state, grads["lnf_g"], grads["lnf_b"] = norm_backward(
        input_grad(grad_rows, weights["emb_w"]), unit_rows, inverse, weights["lnf_g"]
    )
    grad_state, block_grads = block_backward(grad_state, kept, weights, HE, encoder_bias(segment))
    grads.update(block_grads)
    grads["pe_w"] = weight_grad(patches, grad_state.astype(jnp.bfloat16))
    grads["pe_b"] = jnp.sum(grad_state, axis=(0, 1))
    borrowed_flat = jnp.concatenate([grads["out_w"].reshape(-1), grads["fc2_w"].reshape(-1)])
    return (flatten(grads, encoder_row_layout(), flat_length), borrowed_flat)


def decoder_step(
    weights, pixel_rows, received, grid_row, is_valid, image_scale, masked_total, flat_length
):
    total_rows = pixel_rows.shape[0]
    images = total_rows // GRID
    width = weights["mask_tok"].shape[0]
    placed = jnp.zeros((total_rows, width), jnp.bfloat16).at[grid_row].set(received, mode="drop")
    seen = jnp.zeros((total_rows,), jnp.float32).at[grid_row].set(1.0, mode="drop")
    grid_ids = jnp.arange(total_rows, dtype=jnp.int32)
    state = jnp.where(
        seen[:, None] > 0.5, placed.astype(jnp.float32), weights["mask_tok"].astype(jnp.float32)
    ) + position_code(grid_ids % GRID, image_scale[grid_ids // GRID], width)
    state, kept = block_forward(state.reshape(images, GRID, width), weights, HD, 0.0)
    normed, unit_rows, inverse = norm_forward(state, weights["lnf_g"], weights["lnf_b"])
    normed = normed.astype(jnp.bfloat16)
    predicted = (linear(normed, weights["head_w"]) + weights["head_b"].astype(jnp.float32)).reshape(
        total_rows, -1
    )
    low_band, high_band = bands(pixel_rows.astype(jnp.float32))
    miss_low = predicted[:, :LOWPIX] - low_band
    miss_high = predicted[:, LOWPIX:] - high_band
    unseen = 1.0 - seen
    per_patch = jnp.sum(miss_low * miss_low, axis=1) + jnp.sum(
        jnp.sqrt(miss_high * miss_high + 1.0) - 1.0, axis=1
    )
    loss_local = jnp.sum(per_patch * unseen)
    row_weight = unseen / masked_total
    grad_pred = (
        jnp.concatenate(
            [2.0 * miss_low, miss_high * lax.rsqrt(miss_high * miss_high + 1.0)], axis=1
        )
        * row_weight[:, None]
    )
    grad_low = grad_pred.astype(jnp.bfloat16).reshape(images, GRID, -1)
    grads = {
        "head_w": weight_grad(normed, grad_low),
        "head_b": jnp.sum(grad_low.astype(jnp.float32), axis=(0, 1)),
    }
    grad_state, grads["lnf_g"], grads["lnf_b"] = norm_backward(
        input_grad(grad_low, weights["head_w"]), unit_rows, inverse, weights["lnf_g"]
    )
    grad_state, block_grads = block_backward(grad_state, kept, weights, HD, 0.0)
    grads.update(block_grads)
    grad_state = grad_state.reshape(total_rows, width)
    grads["mask_tok"] = jnp.sum(grad_state * unseen[:, None], axis=0)
    grad_sent = jnp.where(
        is_valid[:, None], grad_state[jnp.minimum(grid_row, total_rows - 1)], 0.0
    ).astype(jnp.bfloat16)
    return (grad_sent, flatten(grads, decoder_layout(), flat_length), loss_local)


def body(
    params, first_moment, second_moment, average, pixels, visible_index, visible_count, gsd_id
):
    copies = lax.all_gather(params.astype(jnp.bfloat16), "dp", axis=1, tiled=True)[0]
    flat_length = copies.shape[0]
    borrow_start = NDEC
    borrow_length = DE * DE + FE * DE
    borrowed = shifted_2(copies[borrow_start : borrow_start + borrow_length], "grp", -1)
    masked_total = lax.psum(jnp.sum(GRID - visible_count).astype(jnp.float32), "dp")
    encoder_weights = unpack(copies, encoder_row_layout())
    encoder_weights["out_w"] = borrowed[: DE * DE].reshape(DE, DE)
    encoder_weights["fc2_w"] = borrowed[DE * DE :].reshape(FE, DE)
    decoder_weights = unpack(copies, decoder_layout())
    grid_row, segment, is_valid, position = packing(visible_count, visible_index)
    image_scale = 0.5 + 0.25 * gsd_id.astype(jnp.float32)
    encoder_side = lax.axis_index("grp") == 0

    def run_encoder():
        return encoder_forward(
            encoder_weights, pixels, grid_row, segment, is_valid, position, image_scale
        )

    sent, saved = lax.cond(
        encoder_side, run_encoder, lambda: jax.tree.map(jnp.zeros_like, run_encoder())
    )
    received = jax.tree.map(
        lambda part, own: part.astype(own.dtype), shifted_2(shortened(sent), "grp", 1), sent
    )

    def run_decoder():
        return decoder_step(
            decoder_weights,
            pixels,
            received,
            grid_row,
            is_valid,
            image_scale,
            masked_total,
            flat_length,
        )

    grad_sent, decoder_flat, loss_local = lax.cond(
        encoder_side, lambda: jax.tree.map(jnp.zeros_like, run_decoder()), run_decoder
    )
    returned = jax.tree.map(
        lambda part, own: part.astype(own.dtype),
        shifted_2(shortened(grad_sent), "grp", -1),
        grad_sent,
    )
    encoder_flat, borrowed_grad = lax.cond(
        encoder_side,
        lambda: encoder_backward(encoder_weights, saved, returned, segment, flat_length),
        lambda: (jnp.zeros((flat_length,), jnp.float32), jnp.zeros((borrow_length,), jnp.float32)),
    )
    arrived = jax.tree.map(
        lambda part, own: part.astype(own.dtype),
        shifted_2(shortened(borrowed_grad), "grp", 1),
        borrowed_grad,
    )
    flat_grad = (
        encoder_flat
        + decoder_flat
        + jnp.pad(arrived, (borrow_start, flat_length - borrow_start - borrow_length))
    )
    owned = lax.psum_scatter(flat_grad, "dp", scatter_dimension=0, tiled=True)[None]
    squares, loss_sum = lax.psum((jnp.sum(owned * owned), loss_local), ("grp", "dp"))
    grad_norm = jnp.sqrt(squares)
    clipped = owned * jnp.minimum(1.0, CLIP / grad_norm)
    new_first = BETA_ONE * first_moment + (1.0 - BETA_ONE) * clipped
    new_second = BETA_TWO * second_moment + (1.0 - BETA_TWO) * clipped * clipped
    direction = (
        new_first
        / (1.0 - BETA_ONE**STEP)
        / (jnp.sqrt(new_second / (1.0 - BETA_TWO**STEP)) + ADAM_EPS)
    )
    new_params = params - RATE * (direction + DECAY_WEIGHT * params)
    new_average = AVERAGE_KEEP * average + (1.0 - AVERAGE_KEEP) * new_params
    return (new_params, new_first, new_second, new_average, loss_sum, masked_total, grad_norm)


def solution(mesh):
    return jax.shard_map(
        body,
        mesh=mesh,
        in_specs=(
            P("grp", "dp"),
            P("grp", "dp"),
            P("grp", "dp"),
            P("grp", "dp"),
            P("dp", None),
            P("dp", None),
            P("dp"),
            P("dp"),
        ),
        out_specs=(P("grp", "dp"), P("grp", "dp"), P("grp", "dp"), P("grp", "dp"), P(), P(), P()),
        check_vma=False,
    )
```

profile of v0, /device:TPU:0, one launch (start us, length us, event | category | flops | bytes accessed | tf_op | source)
XLA Modules:
  0.0 3215.4 jit_solution(4225243616548101441)
XLA Ops:
  12.4 372.5 %all-gather.2.cloned.1.call-done = bf16[1,8888320]{1,0:T(2,128)(2,1)} async-done(((bf16[1,555520]{1,0:T(2,128)(2,1)}), bf16[1,8888320]{1,0:T(2,128)(2,1)}) %all-gather.2.cloned.1.call-update) | async-done | bytes 17776656 | tf_op jit(solution)/shard_map/all_gather | solution.py:380
  384.9 224.6 %slice_reduce_fusion.6 = bf16[5242880]{0:T(1024)(128)(2,1)} fusion(bf16[1,8888320]{1,0:T(2,128)(2,1)} %all-gather.2.cloned.1.call-done), kind=kLoop, calls=%fused_computation.434 | loop fusion | bytes 20971520 | tf_op jit(solution)/shard_map/slice | solution.py:384
  621.7 144.5 %slice_reduce_fusion.7 = bf16[4194304]{0:T(1024)(128)(2,1)} fusion(bf16[1,8888320]{1,0:T(2,128)(2,1)} %all-gather.2.cloned.1.call-done), kind=kLoop, calls=%fused_computation.435 | loop fusion | bytes 16777216 | tf_op jit(solution)/shard_map/slice | solution.py:90
  766.2 13.3 reshape.1198
  779.5 109.0 %slice_reduce_fusion.8 = bf16[3145728]{0:T(1024)(128)(2,1)} fusion(bf16[1,8888320]{1,0:T(2,128)(2,1)} %all-gather.2.cloned.1.call-done), kind=kLoop, calls=%fused_computation.436 | loop fusion | bytes 12582912 | tf_op jit(solution)/shard_map/slice | solution.py:90
  888.6 10.3 reshape.1197
  898.9 18.5 slice_reduce_fusion.9
  926.8 13.3 slice.224
  947.5 137.5 %conditional.3 = (bf16[512,512]{1,0:T(8,128)(2,1)}, bf16[1,512,768]{2,1,0:T(8,128)(2,1)}, bf16[1,512,4096]{2,1,0:T(8,128)(2,1)}, f32[1,512,1]{1,2,0:T(1,128)S(1)...) conditional(s32[]{:T(128)} %convert_element_type.339, () %tuple.33, ...), branch_computations={%region_3.4_spmd, %region_4.13_spmd} | conditional | flops 15517378560 | bytes 269761248 | solution.py:399
  959.6 28.4 slice_reduce_fusion
  1017.0 9.6 fusion.64
  1044.7 25.3 add_bitcast_fusion
  1087.0 39.4 %psum.21 = f32[]{:T(128)} all-reduce(f32[]{:T(128)S(6)} %convert_element_type.343), channel_id=1, replica_groups=mesh['grp'=2,'dp'=16] {'dp'}, use_global_device_ids=true, to_apply=%region_14.15 | all-reduce | flops 1 | bytes 8 | tf_op jit(solution)/shard_map/psum | solution.py:385
  1126.4 14.8 conditional.4
  1129.0 11.6 broadcast.1176
  1142.5 741.9 %collective-permute-done.2 = bf16[512,512]{1,0:T(8,128)(2,1)S(1)} collective-permute-done((bf16[512,512]{1,0:T(8,128)(2,1)S(1)}, bf16[512,512]{1,0:T(8,128)(2,1)S(1)}, u32[]{:S(2)}, u32[]{:S(2)}) %collective-permute-start.2) | collective-permute-done | bytes 524320 | tf_op jit(solution)/shard_map/ppermute | solution.py:39
  1884.4 273.9 %conditional.5 = (f32[8888320]{0:T(1024)}, bf16[5242880]{0:T(1024)(128)(2,1)}) conditional(s32[]{:T(128)} %convert_element_type.339, () %tuple.32, (f32[1,512,1]{1,2,0:T(1,128)}, bf16[512,512]{1,0:T(8,128)(2,1)S(1)}, bf16[1024,512]{1,0:T(8,128)(2,1)}, bf16[1024]{0:T(1024)(128)(2,1)}, f32[1,512,1024]{2,1,0:T(8,128)}, ...), branch_computations={%region_47.48_spmd, %region_48.66_spmd} | conditional | flops 30576979968 | bytes 755667456 | solution.py:426
  1892.4 26.8 fusion.191
  1943.6 10.9 multiply_reduce_fusion
  1954.5 11.5 multiply_convert_fusion
  2008.6 12.6 copy.121
  2021.2 12.1 copy.170
  2033.3 10.2 constant_dynamic-update-slice_fusion.9
  2054.0 17.5 copy.122
  2104.6 10.6 convolution_bitcast_fusion
  2115.3 11.9 copy.124
  2136.0 22.0 pad_maximum_fusion
  2163.4 12.3 collective-permute-done.3
  2175.6 39.1 %convert_add_fusion = f32[8888320]{0:T(1024)} fusion(f32[8888320]{0:T(1024)} %get-tuple-element.253, f32[8888320]{0:T(1024)} %get-tuple-element.254, bf16[5242880]{0:T(1024)(128)(2,1)} %collective-permute-done.3), kind=kLoop, calls=%fused_computation.433 | loop fusion | flops 26664960 | bytes 117145600 | tf_op jit(solution)/shard_map/add | solution.py:437
  2216.6 924.3 %all-reduce.5.cloned.1.call-done = f32[8888320]{0:T(1024)} async-done(((f32[8888320]{0:T(1024)}), f32[8888320]{0:T(1024)}) %all-reduce.5.cloned.1.call-update) | async-done | bytes 35553296
  3143.8 39.6 %all-reduce.2 = (f32[]{:T(128)}, f32[]{:T(128)}) all-reduce(f32[]{:T(128)} %multiply_reduce_fusion.24, f32[]{:T(128)} %get-tuple-element.256), channel_id=1, replica_groups=mesh['grp'=2,'dp'=16] {'grp','dp'}, use_global_device_ids=true, to_apply=%region_68.69 | all-reduce | flops 2 | bytes 16 | tf_op jit(solution)/shard_map/psum | solution.py:442
  3187.8 19.1 multiply_add_fusion.5
  (243 shorter events, 250.0 us)
Async XLA Ops:
  7.2 610.6 %copy-start = (s32[8,64]{1,0:T(8,128)S(1)}, s32[8,64]{1,0:T(8,128)}, u32[]{:S(2)}) copy-start(s32[8,64]{1,0:T(8,128)} %param.19) | copy-start | bytes 6148
  7.2 377.7 %all-gather.2.cloned.1.call-start = ((), (), s32[]{:S(2)}) async-start(), calls=%async_computation | async-start | bytes 37775360 | tf_op jit(solution)/shard_map/all_gather | solution.py:380
  12.3 598.7 %copy-start.94 = (s32[8]{0:T(128)S(1)}, s32[8]{0:T(128)}, u32[]{:S(2)}) copy-start(s32[8]{0:T(128)} %param.20) | copy-start | bytes 100
  12.4 608.7 %copy-start.95 = (s32[8]{0:T(128)S(1)}, s32[8]{0:T(128)}, u32[]{:S(2)}) copy-start(s32[8]{0:T(128)} %param.21) | copy-start | bytes 100
  12.4 3128.6 %all-reduce.5.cloned.1.call-start = ((), (), s32[]{:S(2)}) async-start(), calls=%async_computation.1 | async-start | bytes 71106560
  609.5 310.1 %collective-permute-start = (bf16[5242880]{0:T(1024)(128)(2,1)}, bf16[5242880]{0:T(1024)(128)(2,1)}, u32[]{:S(2)}, u32[]{:S(2)}) collective-permute-start(bf16[5242880]{0:T(1024)(128)(2,1)} %slice_reduce_fusion.6), channel_id=1, source_target_pairs={{16,0},{17,1},{18,2},{19,3},{20,4},{21,5},{22,6},{23,7},{24,8},{25... | collective-permute-start | bytes 31457288 | tf_op jit(solution)/shard_map/ppermute | solution.py:39
  621.1 326.4 %copy-start.91 = (pred[512]{0:T(512)(128)(4,1)}, pred[512]{0:T(512)(128)(4,1)S(1)}, u32[]{:S(2)}) copy-start(pred[512]{0:T(512)(128)(4,1)S(1)} %iota_compare_fusion.3) | copy-start | bytes 1540
  621.7 325.7 %copy-start.54 = (s32[512]{0:T(512)}, s32[512]{0:T(512)S(1)}, u32[]{:S(2)}) copy-start(s32[512]{0:T(512)S(1)} %get-tuple-element.576) | copy-start | bytes 6148
  919.6 27.9 copy-start.71
  919.6 27.9 copy-start.72
  919.6 27.9 copy-start.74
  997.6 41.6 %copy-start.67 = (f32[512]{0:T(512)}, f32[512]{0:T(512)S(1)}, u32[]{:S(2)}) copy-start(f32[512]{0:T(512)S(1)} %add_rsqrt_fusion.2) | copy-start | bytes 6148 | tf_op jit(solution)/shard_map/cond
  1009.5 17.1 copy-start.3
  1026.6 9.4 copy-start.27
  1026.6 9.4 copy-start.40
  1039.2 30.7 slice-start.4
  1044.7 25.3 slice-start.5
  1085.0 41.4 %copy-start.69 = (f32[1,512,1]{1,2,0:T(1,128)}, f32[1,512,1]{1,2,0:T(1,128)S(1)}, u32[]{:S(2)}) copy-start(f32[1,512,1]{1,2,0:T(1,128)S(1)} %get-tuple-element.243) | copy-start | bytes 6148
  1085.0 41.4 %copy-start.50 = (f32[1,16,512,1]{2,1,3,0:T(8,128)}, f32[1,16,512,1]{2,1,3,0:T(8,128)S(1)}, u32[]{:S(2)}) copy-start(f32[1,16,512,1]{2,1,3,0:T(8,128)S(1)} %get-tuple-element.245) | copy-start | bytes 98308
  1085.0 41.4 %copy-start.78 = (f32[1,512,1]{1,2,0:T(1,128)}, f32[1,512,1]{1,2,0:T(1,128)S(1)}, u32[]{:S(2)}) copy-start(f32[1,512,1]{1,2,0:T(1,128)S(1)} %get-tuple-element.240) | copy-start | bytes 6148
  1085.1 41.3 %collective-permute-start.1 = (bf16[512,512]{1,0:T(8,128)(2,1)}, bf16[512,512]{1,0:T(8,128)(2,1)S(1)}, u32[]{:S(2)}, u32[]{:S(2)}) collective-permute-start(bf16[512,512]{1,0:T(8,128)(2,1)} %get-tuple-element.237), channel_id=1, source_target_pairs={{0,16},{1,17},{2,18},{3,19},{4,20},{5,21},{6,22},{7,23},{8,24},{9,... | collective-permute-start | bytes 1572872 | tf_op jit(solution)/shard_map/ppermute | solution.py:39
  1126.4 758.0 %copy-start.55 = (s32[512]{0:T(512)S(1)}, s32[512]{0:T(512)}, u32[]{:S(2)}) copy-start(s32[512]{0:T(512)} %copy-done.54) | copy-start | bytes 6148
  1141.2 743.2 %collective-permute-start.2 = (bf16[512,512]{1,0:T(8,128)(2,1)S(1)}, bf16[512,512]{1,0:T(8,128)(2,1)S(1)}, u32[]{:S(2)}, u32[]{:S(2)}) collective-permute-start(bf16[512,512]{1,0:T(8,128)(2,1)S(1)} %get-tuple-element.238), channel_id=1, source_target_pairs={{16,0},{17,1},{18,2},{19,3},{20,4},{21,5},{22,6},{23,7},{24,8},{25... | collective-permute-start | bytes 1572872 | tf_op jit(solution)/shard_map/ppermute | solution.py:39
  1889.2 30.0 slice-start.2
  1892.3 35.3 %copy-start.25 = (f32[1,512,1024]{2,1,0:T(8,128)}, f32[1,512,1024]{2,1,0:T(8,128)S(1)}, u32[]{:S(2)}) copy-start(f32[1,512,1024]{2,1,0:T(8,128)S(1)} %get-tuple-element.469) | copy-start | bytes 6291460 | tf_op jit(solution)/shard_map/cond
  1892.4 26.8 copy-start.73
  1892.4 26.8 slice-start.3
  2033.3 11.4 copy-start.98
  2080.9 8.7 copy-start.30
  2158.2 17.4 collective-permute-start.3
  2214.8 971.9 %copy-start.19 = (f32[1,555520]{1,0:T(1,128)S(1)}, f32[1,555520]{1,0:T(1,128)}, u32[]{:S(2)}) copy-start(f32[1,555520]{1,0:T(1,128)} %param.14) | copy-start | bytes 6666244
  3187.8 19.1 copy-start.1
  (33 other events, 182.3 us)
Sparse Core Ops, SparseCore 0:
  12.5 372.3 all-gather.1
  2214.9 925.9 all-reduce.4
where the time goes:
time: 3240 us; the launch traced here: 3220 us
  waiting for transfers between devices  2050 us (63%)
  local copies, waits for them, and re-layouts  722 us (22%)
  matrix products  179 us (6%)
  other arithmetic  152 us (5%)
  blocking collectives  79 us (2%)
    unnamed x3, waiting for transfers between devices  924 us
    ppermute x4, waiting for transfers between devices, shifted_2(): return lax.ppermute(block, axis, route)  754 us
    all_gather x1, waiting for transfers between devices, body(): lax.all_gather(params.astype(jnp.bfloat16), 'dp', axis=1, tiled=True)[0]  372 us
    slice x5, local copies, waits for them, and re-layouts, unpack(): tensors[section_name] = flat[offset:offset + extent].reshape(section_shape)  301 us
    slice x1, local copies, waits for them, and re-layouts, body(): copies[borrow_start:borrow_start + borrow_length]  225 us
    cond x100, local copies, waits for them, and re-layouts  65.1 us
  transfers between devices with their start and end apart: 6, of which 4 were waited for; matrix products, arithmetic and copies ran while one was open for 10% of the time, Pallas kernels for 0%

commit v1 on v0

v1 whole, which is shorter than its diff:
```python
import functools
import math
import types

import jax
import jax.numpy as jnp
from jax import lax
from jax.experimental import pallas as pl
from jax.experimental.pallas import tpu as pltpu
from jax.sharding import PartitionSpec as P

DE = 1024
HE = 16
FE = 4096
DD = 512
HD = 16
FD = 2048
PSIDE = 16
GSIDE = 14
VMAX = 64
STEP = 10
PIX = 768
LOWPIX = 192
GRID = 196
GPAD = 208
NENC = 8662528
NDEC = 3644352
LANES = 128
UNIT = 4 * LANES

HIGHEST = lax.Precision.HIGHEST
CLIP = 0.05
RATE = 0.01
BETA_ONE = 0.5
BETA_TWO = 0.5
ADAM_EPS = 1e-08
DECAY_WEIGHT = 0.05
AVERAGE_KEEP = 0.9
NORM_EPS = 1e-06
MASK_FILL = -1000000000.0
F32 = jnp.float32
BF16 = jnp.bfloat16
MESH = pl.DeviceIdType.MESH

WIDTH = 256
SUB = 64
PIECE = 8192
VEC_ROWS = 16
VEC_COLS = (FE, FD)
HEAD = LOWPIX + PIX

ENC_LAYOUT = [
    (PIX, DE),
    (DE,),
    (DE,),
    (DE,),
    (DE, 3 * DE),
    (DE,),
    (DE,),
    (DE, FE),
    (FE,),
    (DE,),
    (DE,),
    (DE,),
    (DE, DD),
    (DD,),
]
DEC_LAYOUT = [
    (DD,),
    (DD,),
    (DD,),
    (DD, 3 * DD),
    (DD, DD),
    (DD,),
    (DD,),
    (DD, FD),
    (FD,),
    (FD, DD),
    (DD,),
    (DD,),
    (DD,),
    (DD, HEAD),
    (HEAD,),
]
LENT = [(DE, DE), (FE, DE)]


DP_GRID = (4, 2, 2)
ORDERS = (("y", "z", "x"), ("x", "z", "y"), ("z", "x", "y"))
WAYS = ("x", "y", "up", "down")
CHUNK = 16
OPPOSITE = {"x": "x", "y": "y", "up": "down", "down": "up"}


def part_ranges(units):
    first = int(units * 0.41)
    second = int(units * 0.26)
    return [(0, first), (first, second), (first + second, units - first - second)]


def relatives():
    places = [(dz, dy, dx) for dz in range(-3, 4) for dy in (0, 1) for dx in (0, 1)]
    places.remove((0, 0, 0))
    return sorted(places, key=lambda r: abs(r[0]) + r[1] + r[2])


def last_axis(order, place):
    differs = {"z": place[0] != 0, "y": place[1] != 0, "x": place[2] != 0}
    return [axis for axis in order if differs[axis]][-1]


def onward(order, place):
    if place == (0, 0, 0):
        return ["up", "down", "x", "y"]
    axis = last_axis(order, place)
    ways = []
    if axis == "z":
        ways.append("up" if place[0] < 0 else "down")
    for later in order[order.index(axis) + 1 :]:
        ways += ["up", "down"] if later == "z" else [later]
    return ways


def when(condition, action):
    if condition is None:
        action()
    else:
        pl.when(condition)(action)


def both(left, right):
    if left is None:
        return right
    return left if right is None else left & right


class Spot:
    def __init__(self):
        self.grp = lax.axis_index("grp")
        self.dp = lax.axis_index("dp")
        self.x = self.dp % 2
        self.y = (self.dp // 2) % 2
        self.z = self.dp // 4
        self.neighbour = {
            "x": (self.grp, self.index(self.z, self.y, 1 - self.x)),
            "y": (self.grp, self.index(self.z, 1 - self.y, self.x)),
            "up": (self.grp, self.index(jnp.minimum(self.z + 1, 3), self.y, self.x)),
            "down": (self.grp, self.index(jnp.maximum(self.z - 1, 0), self.y, self.x)),
            "core": (1 - self.grp, self.dp),
        }
        self.exists = {"x": None, "y": None, "up": self.z < 3, "down": self.z > 0, "core": None}

    def index(self, z, y, x):
        return z * 4 + y * 2 + x

    def at(self, place):
        z = self.z + place[0]
        y = 1 - self.y if place[1] else self.y
        x = 1 - self.x if place[2] else self.x
        inside = None if place[0] == 0 else (z >= 0) & (z <= 3)
        return z, self.index(z, y, x), inside

    def greet(self):
        barrier = pltpu.get_barrier_semaphore()
        me = self.grp * 16 + self.dp

        def signal(step, carry):
            other = (me + step) % 32
            pl.semaphore_signal(
                barrier, inc=1, device_id=(other // 16, other % 16), device_id_type=MESH
            )
            return carry

        lax.fori_loop(1, 32, signal, 0)
        pl.semaphore_wait(barrier, 31)


def tell_all(spot, tiles, send_sem, recv_sem):
    me = spot.grp * 16 + spot.dp

    def copy(number, other):
        return pltpu.make_async_remote_copy(
            src_ref=tiles.at[number],
            dst_ref=tiles.at[number],
            send_sem=send_sem.at[other],
            recv_sem=recv_sem.at[number],
            device_id=(other // 16, other % 16),
            device_id_type=MESH,
        )

    def start(step, carry):
        copy(me, (me + step) % 32).start()
        return carry

    def finish(step, carry):
        other = (me + step) % 32
        copy(other, other).wait_recv()
        copy(me, other).wait_send()
        return carry

    return (
        lambda: lax.fori_loop(1, 32, start, 0),
        lambda: lax.fori_loop(1, 32, finish, 0),
    )


def gather_kernel(
    master_ref,
    masked_ref,
    out_ref,
    masked_out,
    master,
    own_ref,
    tiles,
    local_sem,
    send_sem,
    recv_sem,
    core_send,
    core_recv,
    tile_send,
    tile_recv,
):
    spot = Spot()
    read = pltpu.make_async_copy(master_ref, master, local_sem)
    read.start()
    tiles[spot.grp * 16 + spot.dp] = masked_ref[...]
    spot.greet()
    tell, told = tell_all(spot, tiles, tile_send, tile_recv)
    ranges = part_ranges(own_ref.shape[0])
    read.wait()

    def round_off(start, length):
        block = pl.ds(start, length)
        own_ref[block] = master[block].astype(BF16)

    def step(index, carry):
        round_off(index * CHUNK, CHUNK)
        return carry

    units = own_ref.shape[0]
    lax.fori_loop(0, units // CHUNK, step, 0)
    if units % CHUNK:
        round_off(units - units % CHUNK, units % CHUNK)

    def copy(part, source, way, from_own):
        target = out_ref.at[spot.grp, source, pl.ds(*ranges[part])]
        origin = own_ref.at[pl.ds(*ranges[part])] if from_own else target
        if way == "core":
            sems = (core_send.at[part, source], core_recv.at[part, source])
        else:
            sems = (send_sem.at[part, source, WAYS.index(way)], recv_sem.at[part, source])
        return pltpu.make_async_remote_copy(
            src_ref=origin,
            dst_ref=target,
            send_sem=sems[0],
            recv_sem=sems[1],
            device_id=spot.neighbour[way],
            device_id_type=MESH,
        )

    sent = []
    for part in (2, 0, 1):
        for way in onward(ORDERS[part], (0, 0, 0)):
            when(
                spot.exists[way],
                lambda part=part, way=way: copy(part, spot.dp, way, True).start(),
            )
            sent.append((part, spot.dp, way, spot.exists[way], True))
    local = pltpu.make_async_copy(own_ref, out_ref.at[spot.grp, spot.dp], local_sem)
    local.start()
    tell()
    for part in range(3):
        copy(part, spot.dp, "core", True).start()
        sent.append((part, spot.dp, "core", None, True))
    for place in relatives():
        _, source, inside = spot.at(place)
        for part in range(3):
            ways = onward(ORDERS[part], place)

            def pass_on(part=part, source=source, ways=ways):
                copy(part, source, "x", False).wait_recv()
                for way in ways:
                    when(
                        spot.exists[way],
                        lambda way=way: copy(part, source, way, False).start(),
                    )
                copy(part, source, "core", False).start()

            when(inside, pass_on)
            for way in ways + ["core"]:
                sent.append((part, source, way, both(inside, spot.exists[way]), False))
    for part, source, way, condition, from_own in sent:
        when(condition, lambda: copy(part, source, way, from_own).wait_send())

    def await_core(source, carry):
        for part in range(3):
            landed = out_ref.at[1 - spot.grp, source, pl.ds(*ranges[part])]
            pltpu.make_async_remote_copy(
                src_ref=landed,
                dst_ref=landed,
                send_sem=core_send.at[part, source],
                recv_sem=core_recv.at[part, source],
                device_id=spot.neighbour["core"],
                device_id_type=MESH,
            ).wait_recv()
        return carry

    lax.fori_loop(0, 16, await_core, 0)
    told()
    masked_out[...] = jnp.sum(tiles[pl.ds(0, 16)], axis=0)
    local.wait()


def gather_rows(master, masked):
    units = master.shape[0]
    dma = pltpu.SemaphoreType.DMA
    anywhere = pl.BlockSpec(memory_space=pl.ANY)
    vmem = pl.BlockSpec(memory_space=pltpu.VMEM)
    return pl.pallas_call(
        gather_kernel,
        out_shape=(
            jax.ShapeDtypeStruct((2, 16, units, 4, LANES), BF16),
            jax.ShapeDtypeStruct((8, LANES), F32),
        ),
        in_specs=[anywhere, vmem],
        out_specs=(anywhere, vmem),
        scratch_shapes=[
            pltpu.VMEM((units, 4, LANES), F32),
            pltpu.VMEM((units, 4, LANES), BF16),
            pltpu.VMEM((32, 8, LANES), F32),
            dma,
            dma((3, 16, 4)),
            dma((3, 16)),
            dma((3, 16)),
            dma((3, 16)),
            dma((32,)),
            dma((32,)),
        ],
        compiler_params=pltpu.CompilerParams(collective_id=0, has_side_effects=True),
        name="gather_rows",
    )(master, masked)


def slot_tables():
    tables = []
    for order in ORDERS:
        table = {}
        for way in WAYS:
            keys = []
            along = False
            for place in [(0, 0, 0)] + relatives():
                if way in onward(order, place):
                    if place[1:] not in keys:
                        keys.append(place[1:])
                    along = along or place[0] != 0
            table[way] = (keys, 3 if way in ("up", "down") else (4 if along else 1))
        tables.append(table)
    return tables


SLOTS = slot_tables()
STAGES = 4


def scatter_kernel(grad_ref, loss_ref, out_ref, sums_ref, *refs):
    ranges = part_ranges(grad_ref.shape[1])
    landing = {}
    for part in range(3):
        for number, way in enumerate(WAYS):
            landing[part, way] = refs[part * 4 + number]
    stage, total, tiles, send_sem, recv_sem, stage_sem, out_sem, tile_send, tile_recv = refs[12:]
    spot = Spot()
    spot.greet()

    def slot(part, way, place, z):
        keys, depth = SLOTS[part][way]
        base = keys.index(place[1:]) * depth
        if way == "up":
            return base + z
        if way == "down":
            return base + z - 1
        return base + (z if depth == 4 else 0)

    def parent(part, place):
        axis = last_axis(ORDERS[part], place)
        if axis == "z":
            return "up" if place[0] > 0 else "down"
        return axis

    def seen_from_parent(part, place):
        way = parent(part, place)
        dz, dy, dx = place
        if way == "x":
            return (dz, dy, 0)
        if way == "y":
            return (dz, 0, dx)
        return (dz - 1 if way == "up" else dz + 1, dy, dx)

    def send(part, place, origin):
        z, owner, _ = spot.at(place)
        way = parent(part, place)
        back = OPPOSITE[way]
        return pltpu.make_async_remote_copy(
            src_ref=origin,
            dst_ref=landing[part, back].at[slot(part, back, seen_from_parent(part, place), z)],
            send_sem=send_sem.at[part, owner],
            recv_sem=recv_sem.at[part, owner, WAYS.index(back)],
            device_id=spot.neighbour[way],
            device_id_type=MESH,
        )

    def own(part, owner):
        return grad_ref.at[owner, pl.ds(*ranges[part])]

    nodes = [((0, 0, 0), part) for part in (2, 0, 1)]
    nodes += [(place, part) for place in relatives() for part in range(3)]
    nodes.reverse()
    sent = []
    inner = []
    for place, part in nodes:
        ways = onward(ORDERS[part], place)
        z, owner, inside = spot.at(place)
        if ways:
            inner.append((part, place, ways, z, owner, inside))
        else:
            when(inside, lambda: send(part, place, own(part, owner)).start())
        if place != (0, 0, 0):
            sent.append((part, place, owner, inside))

    def staged(number):
        part, _, _, _, owner, _ = inner[number]
        return pltpu.make_async_copy(
            own(part, owner),
            stage.at[number % STAGES, pl.ds(0, ranges[part][1])],
            stage_sem.at[number % STAGES],
        )

    for number in range(STAGES - 1):
        when(inner[number][5], lambda: staged(number).start())
    for number, (part, place, ways, z, owner, inside) in enumerate(inner):
        ahead = number + STAGES - 1
        if ahead < len(inner):
            when(inner[ahead][5], lambda: staged(ahead).start())
        length = ranges[part][1]
        root = place == (0, 0, 0)

        def combine(arriving, number=number, part=part, place=place, z=z, owner=owner):
            slots = []
            for way in arriving:
                spot_of = landing[part, way].at[slot(part, way, place, z)]
                pltpu.make_async_remote_copy(
                    src_ref=spot_of,
                    dst_ref=spot_of,
                    send_sem=send_sem.at[part, owner],
                    recv_sem=recv_sem.at[part, owner, WAYS.index(way)],
                    device_id=spot.neighbour[way],
                    device_id_type=MESH,
                ).wait_recv()
                slots.append(spot_of)
            staged(number).wait()
            if slots:
                target = total.at[pl.ds(*ranges[part])] if root else slots[0]

                def add(start, count):
                    value = stage[number % STAGES, pl.ds(start, count)]
                    for item in slots:
                        value = value + item[pl.ds(start, count)]
                    target[pl.ds(start, count)] = value

                def step(index, carry):
                    add(index * CHUNK, CHUNK)
                    return carry

                lax.fori_loop(0, length // CHUNK, step, 0)
                if length % CHUNK:
                    add(length - length % CHUNK, length % CHUNK)
            if not root:
                send(part, place, slots[0] if slots else own(part, owner)).start()

        def choose(ways=ways, combine=combine):
            flat = [way for way in ways if way in ("x", "y")]
            along = [way for way in ways if way in ("up", "down")]
            if not along:
                combine(flat)
            elif len(along) == 1:
                there = spot.exists[along[0]]
                pl.when(there)(lambda: combine(flat + along))
                pl.when(jnp.logical_not(there))(lambda: combine(flat))
            else:
                up, down = spot.exists["up"], spot.exists["down"]
                pl.when(up & down)(lambda: combine(flat + ["up", "down"]))
                pl.when(jnp.logical_not(down))(lambda: combine(flat + ["up"]))
                pl.when(jnp.logical_not(up))(lambda: combine(flat + ["down"]))

        when(inside, choose)
    out = pltpu.make_async_copy(total, out_ref, out_sem)
    out.start()
    units = total.shape[0]

    def square(start, count, running):
        value = total[pl.ds(start, count)]
        return running + jnp.sum(value * value, axis=0)

    squares = lax.fori_loop(
        0,
        units // CHUNK,
        lambda index, running: square(index * CHUNK, CHUNK, running),
        jnp.zeros((4, LANES), F32),
    )
    if units % CHUNK:
        squares = square(units - units % CHUNK, units % CHUNK, squares)
    me = spot.grp * 16 + spot.dp
    tiles[me, pl.ds(0, 4)] = squares
    tiles[me, pl.ds(4, 4)] = loss_ref[pl.ds(4, 4)]
    tell, told = tell_all(spot, tiles, tile_send, tile_recv)
    tell()
    for part, place, owner, inside in sent:
        when(inside, lambda: send(part, place, own(part, owner)).wait_send())
    told()
    sums_ref[...] = jnp.sum(tiles[...], axis=0)
    out.wait()


def scatter_sums(grads, loss):
    units = grads.shape[1]
    ranges = part_ranges(units)
    scratch = []
    for part in range(3):
        for way in WAYS:
            keys, depth = SLOTS[part][way]
            scratch.append(pltpu.VMEM((len(keys) * depth, ranges[part][1], 4, LANES), F32))
    largest = max(length for _, length in ranges)
    dma = pltpu.SemaphoreType.DMA
    scratch += [
        pltpu.VMEM((STAGES, largest, 4, LANES), F32),
        pltpu.VMEM((units, 4, LANES), F32),
        pltpu.VMEM((32, 8, LANES), F32),
        dma((3, 16)),
        dma((3, 16, 4)),
        dma((STAGES,)),
        dma,
        dma((32,)),
        dma((32,)),
    ]
    anywhere = pl.BlockSpec(memory_space=pl.ANY)
    vmem = pl.BlockSpec(memory_space=pltpu.VMEM)
    return pl.pallas_call(
        scatter_kernel,
        out_shape=(
            jax.ShapeDtypeStruct((units, 4, LANES), F32),
            jax.ShapeDtypeStruct((8, LANES), F32),
        ),
        in_specs=[anywhere, vmem],
        out_specs=(anywhere, vmem),
        scratch_shapes=scratch,
        compiler_params=pltpu.CompilerParams(
            collective_id=1, has_side_effects=True, vmem_limit_bytes=63 * 2**20
        ),
        name="scatter_sums",
    )(grads, loss)


def update_values(owned, squares, params, first_moment, second_moment, average):
    clipped = owned * jnp.minimum(1.0, CLIP / jnp.sqrt(squares))
    new_first = BETA_ONE * first_moment + (1.0 - BETA_ONE) * clipped
    new_second = BETA_TWO * second_moment + (1.0 - BETA_TWO) * clipped * clipped
    direction = (
        new_first
        / (1.0 - BETA_ONE**STEP)
        / (jnp.sqrt(new_second / (1.0 - BETA_TWO**STEP)) + ADAM_EPS)
    )
    new_params = params - RATE * (direction + DECAY_WEIGHT * params)
    new_average = AVERAGE_KEEP * average + (1.0 - AVERAGE_KEEP) * new_params
    return new_params, new_first, new_second, new_average


def update_kernel(squares_ref, owned, params, first, second, average, *outs):
    squares = squares_ref[0]

    def step(index, carry):
        block = pl.ds(index * 5, 5)
        values = update_values(
            owned[block], squares, params[block], first[block], second[block], average[block]
        )
        for out, value in zip(outs, values):
            out[block] = value
        return carry

    lax.fori_loop(0, owned.shape[0] // 5, step, 0)


def update(squares, arrays):
    units = arrays[0].shape[0]
    depth = 155
    spec = pl.BlockSpec((depth, 4, LANES), lambda i: (i, 0, 0))
    return pl.pallas_call(
        update_kernel,
        grid=(units // depth,),
        out_shape=[jax.ShapeDtypeStruct((units, 4, LANES), F32)] * 4,
        in_specs=[pl.BlockSpec(memory_space=pltpu.SMEM)] + [spec] * 5,
        out_specs=[spec] * 4,
        name="update",
    )(squares.reshape(1), *arrays)


def sections(layout, base):
    matrices, vectors = [], []
    offset = base
    for shape in layout:
        (matrices if len(shape) == 2 else vectors).append((offset, shape))
        offset += math.prod(shape)
    return matrices, vectors


def matrix_plan(rows):
    enc_matrices, enc_vectors = sections(ENC_LAYOUT, 0)
    dec_matrices, dec_vectors = sections(DEC_LAYOUT, rows * LANES)
    lent = rows * LANES + NDEC
    matrices = enc_matrices + sections(LENT, lent)[0] + dec_matrices
    return matrices, enc_vectors, dec_vectors


def padded(columns):
    return -(-columns // LANES) * LANES


def block_depth(shape):
    if shape[1] % LANES:
        return shape[0]
    depth = shape[0]
    while depth * shape[1] > PIECE * LANES:
        depth //= 2
    return depth


def matrix_kernel(rows, flat_ref, *refs):
    matrices, enc_vectors, dec_vectors = matrix_plan(rows)
    count = len(matrices)
    out_refs = refs[:count]
    vector_refs = refs[count : count + 2]
    blocks = refs[count + 2 : 2 * count + 2]
    flat_in, wide, pairs, vector_in, in_sem, out_sem, vector_sem = refs[2 * count + 2 :]
    lane = lax.broadcasted_iota(jnp.int32, (1, LANES), 1)

    chunks = []
    for number, (offset, shape) in enumerate(matrices):
        depth = block_depth(shape)
        for start in range(0, shape[0], depth):
            place = offset + start * shape[1]
            chunks.append((number, start, depth, place // LANES, place % LANES))

    def load(index):
        number, _, depth, first, shift = chunks[index]
        length = depth * matrices[number][1][1] // LANES
        begin = first // 16 * 16
        end = -(-(first + length + (1 if shift else 0)) // 16) * 16
        copy = pltpu.make_async_copy(
            flat_ref.at[pl.ds(begin, end - begin)],
            flat_in.at[index % 2, pl.ds(0, end - begin)],
            in_sem.at[index % 2],
        )
        return copy, first - begin, end - begin

    def store(index):
        number, start, depth, _, _ = chunks[index]
        slot = start // depth % 2
        return pltpu.make_async_copy(
            blocks[number].at[slot], out_refs[number].at[pl.ds(start, depth)], out_sem.at[number, slot]
        )

    def widen(index, length):
        step = 256

        def one(start, size):
            wide[pl.ds(start, size)] = flat_in[index % 2, pl.ds(start, size)].astype(F32)

        def loop(i, carry):
            one(pl.multiple_of(i * step, step), step)
            return carry

        lax.fori_loop(0, length // step, loop, 0)
        if length % step:
            one(length - length % step, length % step)

    def turned(first, second):
        return pltpu.roll(jnp.where(lane < LANES // 2, second, first), LANES // 2, 1)

    def arrange(index, phase):
        number, start, depth, _, shift = chunks[index]
        columns = matrices[number][1][1]
        block = blocks[number].at[start // depth % 2]
        tiles = columns // LANES

        def plain(i, carry):
            row = pl.multiple_of(i * SUB, SUB)
            for tile in range(tiles):
                value = wide[pl.ds(phase + row * tiles + tile, SUB, stride=tiles)]
                if shift:
                    after = wide[pl.ds(phase + row * tiles + tile + 1, SUB, stride=tiles)]
                    value = turned(value, after)
                block[pl.ds(row, SUB), pl.ds(tile * LANES, LANES)] = value.astype(BF16)
            return carry

        def paired(i, carry):
            stride = 2 * columns // LANES
            half = SUB // 2
            row = pl.multiple_of(i * half, half)
            for tile in range(tiles + 1):
                even = wide[pl.ds(phase + row * stride + tile, half, stride=stride)]
                odd = wide[pl.ds(phase + row * stride + tiles + tile, half, stride=stride)]
                if tile < tiles:
                    after = wide[pl.ds(phase + row * stride + tiles + tile + 1, half, stride=stride)]
                    odd = turned(odd, after)
                else:
                    even = jnp.where(lane < LANES // 2, even, 0.0)
                    odd = jnp.where(lane < LANES // 2, pltpu.roll(odd, LANES // 2, 1), 0.0)
                lanes = pl.ds(tile * LANES, LANES)
                pairs[tile, pl.ds(0, half, stride=2)] = even
                pairs[tile, pl.ds(1, half, stride=2)] = odd
                block[pl.ds(pl.multiple_of(i * SUB, SUB), SUB), lanes] = pairs[tile].astype(BF16)
            return carry

        lax.fori_loop(0, depth // SUB, paired if columns % LANES else plain, 0)

    windows = []
    wanted = [(0, n, v) for n, v in enumerate(enc_vectors)]
    wanted += [(1, n, v) for n, v in enumerate(dec_vectors)]
    for _, _, (offset, shape) in wanted:
        first = offset // LANES // 16 * 16
        end = -(-(offset // LANES + -(-shape[0] // LANES)) // 16) * 16
        if windows and first <= windows[-1][1]:
            windows[-1][1] = max(windows[-1][1], end)
        else:
            windows.append([first, end])
    bases = [sum(e - f for f, e in windows[:n]) for n in range(len(windows))]

    def vector_copy(n):
        first, end = windows[n]
        return pltpu.make_async_copy(
            flat_ref.at[pl.ds(first, end - first)],
            vector_in.at[pl.ds(bases[n], end - first)],
            vector_sem.at[n],
        )

    load(0)[0].start()
    for n in range(len(windows)):
        vector_copy(n).start()
    for index, (number, start, depth, _, _) in enumerate(chunks):
        copy, phase, length = load(index)
        copy.wait()
        if index + 1 < len(chunks):
            load(index + 1)[0].start()
        widen(index, length)
        if start // depth >= 2:
            store(index - 2).wait()
        arrange(index, phase)
        store(index).start()
    for n in range(len(windows)):
        vector_copy(n).wait()
    total = bases[-1] + windows[-1][1] - windows[-1][0]
    wide[pl.ds(0, total)] = vector_in[...].astype(F32)
    for group, n, (offset, shape) in wanted:
        first = offset // LANES
        window = [k for k, (f, e) in enumerate(windows) if f <= first < e][0]
        base = bases[window] + first - windows[window][0]
        for tile in range(-(-shape[0] // LANES)):
            value = wide[pl.ds(base + tile, 1)]
            if shape[0] - tile * LANES < LANES:
                value = jnp.where(lane < shape[0] - tile * LANES, value, 0.0)
            vector_refs[group][pl.ds(n, 1), pl.ds(tile * LANES, LANES)] = value
    for index, (number, start, depth, _, _) in enumerate(chunks):
        if start + 2 * depth >= matrices[number][1][0]:
            store(index).wait()


def weight_matrices(flat):
    rows = flat.shape[0] // 2
    matrices, enc_vectors, dec_vectors = matrix_plan(rows)
    shapes = [(shape[0], padded(shape[1])) for _, shape in matrices]
    buffers = []
    for (_, shape), (_, columns) in zip(matrices, shapes):
        depth = block_depth(shape)
        buffers.append(pltpu.VMEM((min(2, shape[0] // depth), depth, columns), BF16))
    dma = pltpu.SemaphoreType.DMA
    windows = 0
    last = -1
    total = 0
    for offset, shape in enc_vectors + dec_vectors:
        first = offset // LANES // 16 * 16
        end = -(-(offset // LANES + -(-shape[0] // LANES)) // 16) * 16
        if first <= last:
            total += max(0, end - last)
            last = max(last, end)
        else:
            windows += 1
            total += end - first
            last = end
    anywhere = pl.BlockSpec(memory_space=pl.ANY)
    vmem = pl.BlockSpec(memory_space=pltpu.VMEM)
    return pl.pallas_call(
        functools.partial(matrix_kernel, rows),
        out_shape=[jax.ShapeDtypeStruct(shape, BF16) for shape in shapes]
        + [jax.ShapeDtypeStruct((VEC_ROWS, columns), F32) for columns in VEC_COLS],
        in_specs=[anywhere],
        out_specs=[anywhere] * len(shapes) + [vmem, vmem],
        scratch_shapes=buffers
        + [
            pltpu.VMEM((2, PIECE + 32, LANES), BF16),
            pltpu.VMEM((PIECE + 32, LANES), F32),
            pltpu.VMEM((padded(HEAD) // LANES, SUB, LANES), F32),
            pltpu.VMEM((total, LANES), BF16),
            dma((2,)),
            dma((len(shapes), 2)),
            dma((windows,)),
        ],
        compiler_params=pltpu.CompilerParams(vmem_limit_bytes=56 * 2**20),
        name="weight_matrices",
    )(flat)


def stream_items(layout, lent):
    items = []
    offset = 0
    numbers = [0, 0]
    for shape in layout + lent:
        matrix = len(shape) == 2
        number = numbers[matrix]
        numbers[matrix] += 1
        depth = block_depth(shape) if matrix else 0
        for start in range(0, shape[0] if matrix else 1, max(depth, 1)):
            items.append((matrix, number, shape, start, depth, offset))
            offset += depth * shape[1] if matrix else shape[0]
    return items, offset


def product_kernel(rows, layout, lent, count, *refs):
    factors = [refs[4 * n : 4 * n + 4] for n in range(count)]
    mine_ref, other_ref, out_ref = refs[4 * count : 4 * count + 3]
    refs = refs[4 * count + 3 :]
    lefts, rights = refs[:count], refs[count : 2 * count]
    turned_left, tall, rows_out, in_sem, out_sem = refs[2 * count :]
    lane = lax.broadcasted_iota(jnp.int32, (1, LANES), 1)
    half = LANES // 2

    def load(n):
        copies = []
        for side, buffer in ((0, lefts[n]), (1, rights[n])):
            length = factors[n][2 * side].shape[0]
            for part in range(2):
                copies.append(
                    pltpu.make_async_copy(
                        factors[n][2 * side + part],
                        buffer.at[pl.ds(part * length, length)],
                        in_sem.at[n, 2 * side + part],
                    )
                )
        return copies

    for n in range(count):
        for copy in load(n):
            copy.start()

    items, used = stream_items(layout, lent)
    groups = []
    current = []
    for item in items:
        current.append(item)
        if item[0]:
            groups.append(current)
            current = []
    groups.append(current)

    def vector(item, buffer, base):
        _, number, shape, _, _, _ = item
        for tile in range(-(-shape[0] // LANES)):
            lanes = pl.ds(tile * LANES, LANES)
            buffer[pl.ds(base + tile, 1)] = (
                mine_ref[pl.ds(number, 1), lanes] + other_ref[pl.ds(number, 1), lanes]
            )

    def matrix(item, buffer, base):
        _, number, shape, start, depth, offset = item
        columns = shape[1]
        shifted = offset % LANES
        tiles = -(-columns // LANES)
        width = min(WIDTH, columns)
        if start == 0:
            for copy in load(number):
                copy.wait()
            if shifted:
                length = rights[number].shape[0]

                def turn(i, carry):
                    block = pl.ds(pl.multiple_of(i * 64, 64), 64)
                    value = rights[number][block].astype(F32)
                    rights[number][block] = pltpu.roll(value, half, 1).astype(BF16)
                    return carry

                lax.fori_loop(0, length // 64, turn, 0)
        length = lefts[number].shape[0]
        sub = min(256, depth)

        def loop(step, carry):
            k = pl.multiple_of(start + step * sub, sub)
            turned_left[pl.ds(0, sub), pl.ds(0, length)] = lefts[number][:, pl.ds(k, sub)].T

            def across(c, carry):
                column = pl.multiple_of(c * width, width)
                value = jnp.dot(
                    turned_left[pl.ds(0, sub), pl.ds(0, length)],
                    rights[number][:, pl.ds(column, width)],
                    preferred_element_type=F32,
                )
                row = base + step * sub * tiles
                for piece in range(width // LANES):
                    part = value[:, piece * LANES : (piece + 1) * LANES]
                    tile = c * (width // LANES) + piece
                    if columns % LANES:
                        tall[tile, pl.ds(step * sub, sub)] = part
                    elif shifted and piece == 0:
                        first = row + tile

                        @pl.when(c == 0)
                        def _():
                            before = pltpu.roll(part, 1, 0)
                            index = lax.broadcasted_iota(jnp.int32, (sub, LANES), 0)
                            held = buffer[pl.ds(row, 1)]
                            before = jnp.where(index == 0, held, before)
                            merged = jnp.where(lane < half, before, part)
                            buffer[pl.ds(row, sub, stride=tiles)] = merged
                            buffer[pl.ds(row + sub * tiles, 1)] = part[sub - 1 :]

                        @pl.when(c > 0)
                        def _():
                            buffer[pl.ds(first, sub, stride=tiles)] = part
                    else:
                        buffer[pl.ds(row + tile, sub, stride=tiles)] = part
                return carry

            lax.fori_loop(0, tiles * LANES // width, across, 0)
            return carry

        lax.fori_loop(0, depth // sub, loop, 0)
        if columns % LANES:
            stride = 2 * columns // LANES
            pair = 64

            def weave(i, carry):
                k = pl.multiple_of(i * 2 * pair, 2 * pair)
                row = base + i * pair * stride
                evens = [tall[t, pl.ds(k, pair, stride=2)] for t in range(tiles)]
                odds = [tall[t, pl.ds(k + 1, pair, stride=2)] for t in range(tiles)]
                for t in range(tiles - 1):
                    buffer[pl.ds(row + t, pair, stride=stride)] = evens[t]
                middle = jnp.where(lane < half, evens[-1], pltpu.roll(odds[0], half, 1))
                buffer[pl.ds(row + tiles - 1, pair, stride=stride)] = middle
                for t in range(1, tiles):
                    both_halves = jnp.where(lane < half, odds[t], odds[t - 1])
                    buffer[pl.ds(row + tiles - 1 + t, pair, stride=stride)] = pltpu.roll(
                        both_halves, half, 1
                    )
                return carry

            lax.fori_loop(0, depth // 2 // pair, weave, 0)

    flights = []
    tail = None
    for number, group in enumerate(groups):
        slot = number % 2
        buffer = rows_out.at[slot]
        if number >= 2:
            flights[number - 2].wait()
        first = group[0][5] // LANES if group else used // LANES
        begin = first // 8 * 8
        if tail is not None:
            buffer[pl.ds(0, 8)] = rows_out[1 - slot, pl.ds(tail, 8)]
        for item in group:
            (matrix if item[0] else vector)(item, buffer, item[5] // LANES - begin)
        last = number == len(groups) - 1
        if last:
            at = used // LANES - begin
            if used % LANES:
                buffer[pl.ds(at, 1)] = jnp.where(lane < used % LANES, buffer[pl.ds(at, 1)], 0.0)
                at += 1
            length = rows - begin
            if length > at:
                buffer[pl.ds(at, length - at)] = jnp.zeros((length - at, LANES), F32)
        else:
            end = groups[number + 1][0][5] if groups[number + 1] else used
            tail = (end // LANES - begin) // 8 * 8
            length = tail
        flight = pltpu.make_async_copy(
            buffer.at[pl.ds(0, length)], out_ref.at[pl.ds(begin, length)], out_sem.at[slot]
        )
        flight.start()
        flights.append(flight)
    for flight in flights[-2:]:
        flight.wait()


def flat_gradient(rows, layout, lent, factors, mine, other):
    shapes = [shape for shape in layout if len(shape) == 2] + lent
    lefts = [pltpu.VMEM((2 * f[0].shape[0], f[0].shape[1]), BF16) for f in factors]
    rights = [pltpu.VMEM((2 * f[2].shape[0], f[2].shape[1]), BF16) for f in factors]
    longest = max(2 * f[0].shape[0] for f in factors)
    dma = pltpu.SemaphoreType.DMA
    anywhere = pl.BlockSpec(memory_space=pl.ANY)
    vmem = pl.BlockSpec(memory_space=pltpu.VMEM)
    return pl.pallas_call(
        functools.partial(product_kernel, rows, layout, lent, len(shapes)),
        out_shape=jax.ShapeDtypeStruct((rows, LANES), F32),
        in_specs=[anywhere] * (4 * len(shapes)) + [vmem, vmem],
        out_specs=anywhere,
        scratch_shapes=lefts
        + rights
        + [
            pltpu.VMEM((256, longest), BF16),
            pltpu.VMEM((padded(HEAD) // LANES, DD, LANES), F32),
            pltpu.VMEM((2, PIECE + 128, LANES), F32),
            dma((len(shapes), 4)),
            dma((2,)),
        ],
        compiler_params=pltpu.CompilerParams(vmem_limit_bytes=62 * 2**20),
        name="flat_gradient",
    )(*[a for f in factors for a in f], mine, other)


Bag = types.SimpleNamespace


def position_code(position, scales, width):
    quarter = width // 4
    frequency = jnp.exp(jnp.arange(quarter, dtype=F32) * (-math.log(10000.0) / quarter))
    row_angle = ((position // GSIDE).astype(F32) * scales)[..., None] * frequency
    col_angle = ((position % GSIDE).astype(F32) * scales)[..., None] * frequency
    return jnp.concatenate(
        [jnp.sin(row_angle), jnp.cos(row_angle), jnp.sin(col_angle), jnp.cos(col_angle)], axis=-1
    )


def bands(pixel_rows):
    pixel_ids = jnp.arange(PIX, dtype=jnp.int32)
    coarse = (
        pixel_ids // (3 * PSIDE) // 2 * (PSIDE // 2) + pixel_ids // 3 % PSIDE // 2
    ) * 3 + pixel_ids % 3
    pool_table = (coarse[:, None] == jnp.arange(LOWPIX, dtype=jnp.int32)[None, :]).astype(F32)
    low_band = jnp.dot(pixel_rows, pool_table, precision=HIGHEST) * 0.25
    high_band = pixel_rows - jnp.dot(low_band, pool_table.T, precision=HIGHEST)
    return (low_band, high_band)


def linear(left, right):
    return jnp.einsum("...k,kn->...n", left, right, preferred_element_type=F32)


def input_grad(grad_rows, right):
    return jnp.einsum("...n,kn->...k", grad_rows, right, preferred_element_type=F32)


def norm_forward(state, gain, shift):
    centered = state - jnp.mean(state, axis=-1, keepdims=True)
    inverse = lax.rsqrt(jnp.mean(centered * centered, axis=-1, keepdims=True) + NORM_EPS)
    unit_rows = centered * inverse
    return (unit_rows * gain.astype(F32) + shift.astype(F32), unit_rows, inverse)


def norm_backward(grad_out, unit_rows, inverse, gain):
    grad_unit = grad_out * gain.astype(F32)
    grad_in = inverse * (
        grad_unit
        - jnp.mean(grad_unit, axis=-1, keepdims=True)
        - unit_rows * jnp.mean(grad_unit * unit_rows, axis=-1, keepdims=True)
    )
    return (grad_in, jnp.sum(grad_out * unit_rows, axis=(0, 1)), jnp.sum(grad_out, axis=(0, 1)))


def attention_scores(query_part, key_part, bias):
    head_dim = query_part.shape[-1]
    return (
        jnp.einsum("blhd,bmhd->bhlm", query_part, key_part, preferred_element_type=F32)
        * head_dim ** (-0.5)
        + bias
    )


def gelu_exact(values):
    return jax.nn.gelu(values, approximate=False)


def block_forward(state, weights, heads, bias):
    batch, length, width = state.shape
    normed_one, unit_one, inverse_one = norm_forward(state, weights.ln1_g, weights.ln1_b)
    normed_one = normed_one.astype(BF16)
    qkv = (
        linear(normed_one, weights.qkv_w)
        .astype(BF16)
        .reshape(batch, length, 3, heads, width // heads)
    )
    scores = attention_scores(qkv[:, :, 0], qkv[:, :, 1], bias)
    row_max = jnp.max(scores, axis=-1, keepdims=True)
    shifted = jnp.exp(scores - row_max)
    totals = jnp.sum(shifted, axis=-1, keepdims=True)
    attend = (shifted / totals).astype(BF16)
    logsum = row_max + jnp.log(totals)
    mixed = jnp.einsum("bhlm,bmhd->blhd", attend, qkv[:, :, 2], preferred_element_type=F32)
    mixed = mixed.astype(BF16).reshape(batch, length, width)
    middle = state + linear(mixed, weights.out_w)
    normed_two, unit_two, inverse_two = norm_forward(middle, weights.ln2_g, weights.ln2_b)
    normed_two = normed_two.astype(BF16)
    pre_act = linear(normed_two, weights.fc1_w) + weights.fc1_b.astype(F32)
    active = gelu_exact(pre_act).astype(BF16)
    output = middle + linear(active, weights.fc2_w) + weights.fc2_b.astype(F32)
    kept = Bag(
        normed_one=normed_one,
        unit_one=unit_one,
        inverse_one=inverse_one,
        qkv=qkv,
        logsum=logsum,
        mixed=mixed,
        unit_two=unit_two,
        inverse_two=inverse_two,
        normed_two=normed_two,
        active=active,
        pre_act=pre_act,
    )
    return (output, kept)


def block_backward(grad_out, kept, weights, heads, bias):
    batch, length, width = grad_out.shape
    grads = Bag()
    pairs = Bag()
    grad_low = grad_out.astype(BF16)
    pairs.fc2_w = (kept.active, grad_low)
    grads.fc2_b = jnp.sum(grad_out, axis=(0, 1))
    _, gelu_back = jax.vjp(gelu_exact, kept.pre_act)
    grad_pre = gelu_back(input_grad(grad_low, weights.fc2_w))[0]
    grads.fc1_b = jnp.sum(grad_pre, axis=(0, 1))
    grad_pre_low = grad_pre.astype(BF16)
    pairs.fc1_w = (kept.normed_two, grad_pre_low)
    grad_norm_in, grads.ln2_g, grads.ln2_b = norm_backward(
        input_grad(grad_pre_low, weights.fc1_w),
        kept.unit_two,
        kept.inverse_two,
        weights.ln2_g,
    )
    grad_mid = grad_out + grad_norm_in
    grad_mid_low = grad_mid.astype(BF16)
    pairs.out_w = (kept.mixed, grad_mid_low)
    grad_mixed = (
        input_grad(grad_mid_low, weights.out_w)
        .astype(BF16)
        .reshape(batch, length, heads, width // heads)
    )
    qkv = kept.qkv
    query_part, key_part, value_part = (qkv[:, :, 0], qkv[:, :, 1], qkv[:, :, 2])
    attend = jnp.exp(attention_scores(query_part, key_part, bias) - kept.logsum)
    grad_value = jnp.einsum(
        "bhlm,blhd->bmhd", attend.astype(BF16), grad_mixed, preferred_element_type=F32
    )
    grad_attend = jnp.einsum("blhd,bmhd->bhlm", grad_mixed, value_part, preferred_element_type=F32)
    grad_scores = (
        attend * (grad_attend - jnp.sum(grad_attend * attend, axis=-1, keepdims=True))
    ).astype(BF16)
    score_scale = (width // heads) ** (-0.5)
    grad_query = (
        jnp.einsum("bhlm,bmhd->blhd", grad_scores, key_part, preferred_element_type=F32)
        * score_scale
    )
    grad_key = (
        jnp.einsum("bhlm,blhd->bmhd", grad_scores, query_part, preferred_element_type=F32)
        * score_scale
    )
    grad_qkv = (
        jnp.stack([grad_query, grad_key, grad_value], axis=2)
        .reshape(batch, length, 3 * width)
        .astype(BF16)
    )
    pairs.qkv_w = (kept.normed_one, grad_qkv)
    grad_norm_in, grads.ln1_g, grads.ln1_b = norm_backward(
        input_grad(grad_qkv, weights.qkv_w),
        kept.unit_one,
        kept.inverse_one,
        weights.ln1_g,
    )
    return (grad_mid + grad_norm_in, grads, pairs)


def forward_backward(enc, dec, pixels, index_rows, counts, scales, masked_total):
    images = counts.shape[0]
    slots = jnp.arange(VMAX, dtype=jnp.int32)
    valid = slots[None, :] < counts[:, None]
    position = jnp.where(valid, index_rows, 0)
    pixel_images = jnp.pad(pixels.reshape(images, GRID, PIX), ((0, 0), (0, GPAD - GRID), (0, 0)))
    grid = jnp.arange(GPAD, dtype=jnp.int32)
    chosen = ((position[:, :, None] == grid[None, None, :]) & valid[:, :, None]).astype(BF16)
    patches = jnp.einsum("ivg,igp->ivp", chosen, pixel_images, preferred_element_type=F32)
    patches = patches.astype(BF16)
    enc_bias = jnp.where(valid, 0.0, MASK_FILL)[:, None, None, :]
    state = (
        linear(patches, enc.pe_w)
        + enc.pe_b.astype(F32)
        + position_code(position, scales[:, None], DE)
    )
    state, enc_kept = block_forward(state, enc, HE, enc_bias)
    enc_normed, enc_unit, enc_inverse = norm_forward(state, enc.lnf_g, enc.lnf_b)
    enc_normed = enc_normed.astype(BF16)
    sent = (linear(enc_normed, enc.emb_w) + enc.emb_b.astype(F32)).astype(BF16)

    placed = jnp.einsum("ivg,ivd->igd", chosen, sent, preferred_element_type=F32)
    seen = jnp.sum(chosen.astype(F32), axis=1)
    dec_bias = jnp.where(grid < GRID, 0.0, MASK_FILL)[None, None, None, :]
    state = jnp.where(
        seen[:, :, None] > 0.5, placed, dec.mask_tok.astype(F32)
    ) + position_code(jnp.broadcast_to(grid[None], (images, GPAD)), scales[:, None], DD)
    state, dec_kept = block_forward(state, dec, HD, dec_bias)
    normed, unit_rows, inverse = norm_forward(state, dec.lnf_g, dec.lnf_b)
    normed = normed.astype(BF16)
    predicted = linear(normed, dec.head_w[:, :HEAD]) + dec.head_b[:HEAD].astype(F32)
    low_band, high_band = bands(pixel_images.reshape(-1, PIX).astype(F32))
    low_band = low_band.reshape(images, GPAD, -1)
    high_band = high_band.reshape(images, GPAD, -1)
    miss_low = predicted[..., :LOWPIX] - low_band
    miss_high = predicted[..., LOWPIX:] - high_band
    unseen = jnp.where(grid[None] < GRID, 1.0 - seen, 0.0)
    per_patch = jnp.sum(miss_low * miss_low, axis=-1) + jnp.sum(
        jnp.sqrt(miss_high * miss_high + 1.0) - 1.0, axis=-1
    )
    loss_local = jnp.sum(per_patch * unseen)
    row_weight = unseen / masked_total
    grad_pred = (
        jnp.concatenate(
            [2.0 * miss_low, miss_high * lax.rsqrt(miss_high * miss_high + 1.0)], axis=-1
        )
        * row_weight[:, :, None]
    )
    grad_low = jnp.pad(grad_pred, ((0, 0), (0, 0), (0, padded(HEAD) - HEAD))).astype(BF16)
    dec_pairs = Bag(head_w=(normed, grad_low))
    dec_grads = Bag(head_b=jnp.sum(grad_low.astype(F32), axis=(0, 1)))
    grad_state, dec_grads.lnf_g, dec_grads.lnf_b = norm_backward(
        input_grad(grad_low, dec.head_w), unit_rows, inverse, dec.lnf_g
    )
    grad_state, block_grads, block_pairs = block_backward(grad_state, dec_kept, dec, HD, dec_bias)
    vars(dec_grads).update(vars(block_grads))
    vars(dec_pairs).update(vars(block_pairs))
    dec_grads.mask_tok = jnp.sum(grad_state * unseen[:, :, None], axis=(0, 1))
    grad_sent = jnp.einsum(
        "ivg,igd->ivd", chosen, grad_state.astype(BF16), preferred_element_type=F32
    ).astype(BF16)

    enc_pairs = Bag(emb_w=(enc_normed, grad_sent))
    enc_grads = Bag(emb_b=jnp.sum(grad_sent.astype(F32), axis=(0, 1)))
    grad_state, enc_grads.lnf_g, enc_grads.lnf_b = norm_backward(
        input_grad(grad_sent, enc.emb_w), enc_unit, enc_inverse, enc.lnf_g
    )
    grad_state, block_grads, block_pairs = block_backward(grad_state, enc_kept, enc, HE, enc_bias)
    vars(enc_grads).update(vars(block_grads))
    vars(enc_pairs).update(vars(block_pairs))
    enc_pairs.pe_w = (patches, grad_state.astype(BF16))
    enc_grads.pe_b = jnp.sum(grad_state, axis=(0, 1))
    return loss_local, enc_grads, enc_pairs, dec_grads, dec_pairs


def vector_rows(vectors, columns):
    rows = [jnp.pad(vector, (0, columns - vector.shape[0])) for vector in vectors]
    rows += [jnp.zeros((columns,), F32)] * (VEC_ROWS - len(rows))
    return jnp.stack(rows)


def to_core(array, core):
    return lax.ppermute(array, "grp", [(1 - core, core)])


def factor_list(pairs, core):
    factors = []
    for left, right in pairs:
        left = left.reshape(-1, left.shape[-1])
        right = right.reshape(-1, right.shape[-1])
        factors.append((left, to_core(left, core), right, to_core(right, core)))
    return factors


def gradient_row(rows, enc_grads, enc_pairs, dec_grads, dec_pairs):
    e, d = enc_grads, dec_grads
    enc_vectors = vector_rows(
        [e.pe_b, e.ln1_g, e.ln1_b, e.ln2_g, e.ln2_b, e.fc1_b, e.fc2_b, e.lnf_g, e.lnf_b, e.emb_b],
        VEC_COLS[0],
    )
    dec_vectors = vector_rows(
        [d.mask_tok, d.ln1_g, d.ln1_b, d.ln2_g, d.ln2_b]
        + [d.fc1_b, d.fc2_b, d.lnf_g, d.lnf_b, d.head_b],
        VEC_COLS[1],
    )
    e, d = enc_pairs, dec_pairs
    first = factor_list([e.pe_w, e.qkv_w, e.fc1_w, e.emb_w], 0)
    second = factor_list([d.qkv_w, d.out_w, d.fc1_w, d.fc2_w, d.head_w, e.out_w, e.fc2_w], 1)
    enc_other = to_core(enc_vectors, 0)
    dec_other = to_core(dec_vectors, 1)
    return lax.cond(
        lax.axis_index("grp") == 0,
        lambda: flat_gradient(rows, ENC_LAYOUT, [], first, enc_vectors, enc_other),
        lambda: flat_gradient(rows, DEC_LAYOUT, LENT, second, dec_vectors, dec_other),
    )


def bags(parts):
    enc, dec = Bag(), Bag()
    enc.pe_w, enc.qkv_w, enc.fc1_w, enc.emb_w, enc.out_w, enc.fc2_w = parts[:6]
    dec.qkv_w, dec.out_w, dec.fc1_w, dec.fc2_w, dec.head_w = parts[6:11]
    e, d = parts[11:]
    enc.pe_b, enc.ln1_g, enc.ln1_b, enc.ln2_g, enc.ln2_b = [e[n, :DE] for n in range(5)]
    enc.fc1_b = e[5]
    enc.fc2_b, enc.lnf_g, enc.lnf_b = [e[n, :DE] for n in range(6, 9)]
    enc.emb_b = e[9, :DD]
    dec.mask_tok, dec.ln1_g, dec.ln1_b, dec.ln2_g, dec.ln2_b = [d[n, :DD] for n in range(5)]
    dec.fc1_b = d[5]
    dec.fc2_b, dec.lnf_g, dec.lnf_b = [d[n, :DD] for n in range(6, 9)]
    dec.head_b = d[9, : padded(HEAD)]
    return enc, dec


def body(
    params, first_moment, second_moment, average, pixels, visible_index, visible_count, gsd_id
):
    chips = lax.axis_size("dp")
    rows = params.shape[1] // LANES
    special = chips == math.prod(DP_GRID) and rows % 4 == 0
    masked = jnp.sum(GRID - visible_count).astype(F32)
    if special:
        shards = [a.reshape(-1, 4, LANES) for a in (params, first_moment, second_moment, average)]
        copies, masked_tile = gather_rows(shards[0], jnp.full((8, LANES), masked))
        masked_total = masked_tile[0, 0]
    else:
        copies = lax.all_gather(params.astype(BF16).reshape(-1, LANES), "dp", axis=0, tiled=True)
        copies = lax.all_gather(copies, "grp", axis=0, tiled=True)
        masked_total = lax.psum(masked, "dp")
    enc, dec = bags(weight_matrices(copies.reshape(-1, LANES)))

    half = visible_count.shape[0] // 2
    core = lax.axis_index("grp")

    def mine(array, count):
        return lax.dynamic_slice_in_dim(array, core * count, count, 0)

    scales = 0.5 + 0.25 * mine(gsd_id, half).astype(F32)
    loss_local, enc_grads, enc_pairs, dec_grads, dec_pairs = forward_backward(
        enc,
        dec,
        mine(pixels, half * GRID),
        mine(visible_index, half),
        mine(visible_count, half),
        scales,
        masked_total,
    )
    gradient = gradient_row(chips * rows, enc_grads, enc_pairs, dec_grads, dec_pairs)
    if special:
        owned, sums = scatter_sums(
            gradient.reshape(chips, rows // 4, 4, LANES), jnp.full((8, LANES), loss_local)
        )
        squares = jnp.sum(sums[:4])
        loss_sum = sums[4, 0]
        outs = update(squares, [owned] + shards)
        outs = [out.reshape(params.shape) for out in outs]
    else:
        owned = lax.psum_scatter(gradient, "dp", scatter_dimension=0, tiled=True)
        owned = owned.reshape(params.shape)
        squares, loss_sum = lax.psum((jnp.sum(owned * owned), loss_local), ("grp", "dp"))
        outs = update_values(owned, squares, params, first_moment, second_moment, average)
    return (*outs, loss_sum, masked_total, jnp.sqrt(squares))


def solution(mesh):
    return jax.shard_map(
        body,
        mesh=mesh,
        in_specs=(P("grp", "dp"),) * 4 + (P("dp", None), P("dp", None), P("dp"), P("dp")),
        out_specs=(P("grp", "dp"),) * 4 + (P(), P(), P()),
        check_vma=False,
    )
```

time: 3240 us -> 1050 us (0.32)
  waiting for transfers between devices: 2050 us -> 2.43 us
  Pallas kernels: 0 us -> 690 us
  local copies, waits for them, and re-layouts: 722 us -> 101 us
  other arithmetic: 152 us -> 68.7 us
  blocking collectives: 79 us -> 0 us
  matrix products: 179 us -> 109 us
  starting transfers between devices: 9.32 us -> 58.6 us
    unnamed x3 -> x0, waiting for transfers between devices: 924 us -> none
    ppermute x4 -> x24, waiting for transfers between devices: 754 us -> 2.43 us  [to_core(): return lax.ppermute(array, 'grp', [(1 - core, core)])]
    pallas_call x0 -> x5, Pallas kernels: none -> 690 us  [the longest x1 423 us: scatter_sums(): pl.pallas_call(scatter_kernel, out_shape=(jax.ShapeDtypeStruct((units, 4,...]
    slice x10 -> x9, local copies, waits for them, and re-layouts: 554 us -> 12.8 us  [the longest x1 3.8 us: block_forward(): scores = attention_scores(qkv[:, :, 0], qkv[:, :, 1], bias)]
    all_gather x1 -> x0, waiting for transfers between devices: 372 us -> none  [body(): lax.all_gather(params.astype(jnp.bfloat16), 'dp', axis=1, tiled=True)[0]]
    psum x2 -> x0, blocking collectives: 79 us -> none  [the longest x1 39.6 us: body(): lax.psum((jnp.sum(owned * owned), loss_local), ('grp', 'dp'))]
    cond x100 -> x0, local copies, waits for them, and re-layouts: 65.1 us -> none
    dot_general x18 -> x27, matrix products: 139 us -> 76.4 us  [the longest x10 40.7 us: input_grad(): jnp.einsum('...n,kn->...k', grad_rows, right, preferred_element_type=F32)]
  transfers between devices with their start and end apart: 6 -> 24, of which waited for: 4 -> 1; matrix products, arithmetic and copies ran while one was open for 10% -> 4% of each run, Pallas kernels for 0% -> 0%
where the time goes in v1:
time: 1050 us; the launch traced here: 1030 us
  Pallas kernels  690 us (66%)
  matrix products  109 us (10%)
  local copies, waits for them, and re-layouts  101 us (10%)
  other arithmetic  68.7 us (7%)
  starting transfers between devices  58.6 us (6%)
    pallas_call x1, Pallas kernels, scatter_sums(): pl.pallas_call(scatter_kernel, out_shape=(jax.ShapeDtypeStruct((units, 4,...  423 us
    pallas_call x1, Pallas kernels, gather_rows(): pl.pallas_call(gather_kernel, out_shape=(jax.ShapeDtypeStruct((2, 16, uni...  149 us
    ppermute x24, starting transfers between devices, to_core(): return lax.ppermute(array, 'grp', [(1 - core, core)])  58.6 us
    pallas_call x1, Pallas kernels, flat_gradient(): pl.pallas_call(functools.partial(product_kernel, rows, layout, lent, len(...  45.3 us
    pallas_call x1, Pallas kernels, weight_matrices(): pl.pallas_call(functools.partial(matrix_kernel, rows), out_shape=[jax.Sha...  44.8 us
    dot_general x10, matrix products, input_grad(): jnp.einsum('...n,kn->...k', grad_rows, right, preferred_element_type=F32)  40.7 us
    pallas_call x1, Pallas kernels, update(): pl.pallas_call(update_kernel, grid=(units // depth,), out_shape=[jax.Shap...  27.7 us
    convert_element_type x2, other arithmetic, block_forward(): active = gelu_exact(pre_act).astype(BF16)  26.3 us
  transfers between devices with their start and end apart: 24, of which 1 were waited for; matrix products, arithmetic and copies ran while one was open for 4% of the time, Pallas kernels for 0%

profile of v1, /device:TPU:0, one launch (start us, length us, event | category | flops | bytes accessed | tf_op | source)
XLA Modules:
  0.0 1033.9 jit_solution(4586898018773566013)
XLA Ops:
  3.2 148.9 %gather_rows.1 = (bf16[2,16,1085,4,128]{4,3,2,1,0:T(4,128)(2,1)}, f32[8,128]{1,0:T(8,128)}) custom-call(f32[1085,4,128]{2,1,0:T(4,128)} %bitcast.319, f32[8,128]{1,0:T(8,128)} %broadcast_in_dim.58.masked_ref), custom_call_target="tpu_custom_call" | custom-call | tf_op jit(solution)/shard_map/gather_rows/pallas_call | solution.py:319
  152.1 44.8 %weight_matrices.1 = (bf16[768,1024]{1,0:T(8,128)(2,1)}, bf16[1024,3072]{1,0:T(8,128)(2,1)}, bf16[1024,4096]{1,0:T(8,128)(2,1)}, bf16[1024,512]{1,0:T(8,128)(2,1...) custom-call(bf16[138880,128]{1,0:T(8,128)(2,1)} %bitcast.304), custom_call_target="tpu_custom_call" | custom-call | tf_op jit(solution)/shard_map/weight_matrices/pallas_call | solution.py:800
  209.8 4.6 fusion.35
  214.4 3.3 reshape.568
  217.7 3.8 fusion.152
  231.7 3.6 fusion.99
  235.4 10.3 %multiply_convert_fusion.2 = (bf16[4,64,4096]{2,1,0:T(8,128)(2,1)S(1)}, f32[4,64,4096]{2,1,0:T(8,128)}) fusion(f32[4,64,4096]{2,1,0:T(8,128)S(1)} %get-tuple-element.353, u8[64,4096]{1,0:T(8,128)(4,1)S(1)} %get-tuple-element.260, u8[64,4096]{1,0:T(8,128)(4,1)S(1)} %get-tuple-element.259), kind=kLoop, calls=%fused_computation.55 | loop fusion | flops 73400320 | bytes 11010048 | tf_op jit(solution)/shard_map/convert_element_type | solution.py:1111
  251.2 4.0 multiply_sine_fusion.1
  264.2 4.5 copy.87
  268.8 4.5 fusion.162
  278.1 5.2 fusion.62
  289.1 3.6 convert_subtract_fusion
  294.4 3.7 fusion.52
  298.1 15.9 %multiply_convert_fusion.1 = (bf16[4,208,2048]{2,1,0:T(8,128)(2,1)S(1)}, f32[4,208,2048]{2,1,0:T(8,128)S(1)}) fusion(f32[4,208,2048]{2,1,0:T(8,128)S(1)} %get-tuple-element.362, f32[2048]{0:T(1024)S(1)} %bitcast.377, u8[208,2048]{1,0:T(8,128)(4,1)S(1)} %get-tuple-element.258, u8[208,2048]{1,0:T(8,128)(4,1)S(1)} %get-tuple-element.257), kind=kLoop, calls=%fused_computation.25 | loop fusion | flops 120979456 | bytes 17899520 | tf_op jit(solution)/shard_map/convert_element_type | solution.py:1111
  327.6 7.1 fusion.150
  343.9 13.2 %multiply_reduce_fusion = (f32[4,16,208]{2,1,0:T(8,128)S(1)}, f32[4,16,208,208]{2,3,1,0:T(8,128)}) fusion(f32[4,16,208,208]{2,3,1,0:T(8,128)} %copy-done, f32[4,16,208]{2,1,0:T(8,128)S(1)} %log_add_fusion, bf16[4,208,16,32]{1,3,2,0:T(8,128)(2,1)} %bitcast.317, bf16[4,208,3,16,32]{1,4,3,2,0:T(8,128)(2,1)S(1)} %bitcast.307), kind=kOutput, calls=%fused_computation.1 | convolution fusion | flops 185502720 | bytes 24170496 | tf_op jit(solution)/shard_map/blhd,bmhd->bhlm/dot_general | solution.py:1161
  357.1 7.1 multiply_convert_fusion
  382.2 8.1 fusion.151
  390.4 6.8 multiply_reduce_fusion.16
  411.5 3.6 convert_element_type.238
  415.1 5.8 multiply_reduce_fusion.17
  442.4 3.7 collective-permute-start.14
  455.0 7.0 collective-permute-start.11
  486.5 4.9 convert_element_type.240
  492.7 7.7 collective-permute-start.5
  502.5 3.1 collective-permute-start.6
  505.6 4.7 copy.99
  510.3 5.7 convert_element_type.226
  531.9 45.5 %conditional.1 = (f32[16,1085,4,128]{3,2,1,0:T(4,128)}) conditional(s32[]{:T(128)} %convert_element_type.191, (bf16[832,512]{1,0:T(8,128)(2,1)}, bf16[832,512]{1,0:T(8,128)(2,1)}, bf16[832,1536]{0,1:T(8,128)(2,1)S(1)}, bf16[832,1536]{1,0:T(8,128)(2,1)}, bf16[832,512]{0,1:T(8,128)(2,1)}, /*index=5*/bf16[832,512]{1,0:T(8,128)(2,1)}, ...), branch_computations={%region_52.53_spmd, %region_53.54_spmd} | conditional | bytes 7864384 | solution.py:1299
  532.1 45.3 %flat_gradient.3 = f32[69440,128]{1,0:T(8,128)} custom-call(bf16[256,768]{1,0:T(8,128)(2,1)} %get-tuple-element.130.refs_0_, bf16[256,768]{1,0:T(8,128)(2,1)} %get-tuple-element.131.refs_1_, bf16[256,1024]{1,0:T(8,128)(2,1)} %get-tuple-element.132.refs_2_, bf16[256,1024]{1,0:T(8,128)(2,1)} %get-tuple-element.133.refs_3_, ...), custom_call_target="tpu_custom_call" | custom-call | tf_op jit(solution)/shard_map/cond/branch_1_fun/flat_gradient/pallas_call | solution.py:1009
  578.6 423.0 %scatter_sums.1 = (f32[1085,4,128]{2,1,0:T(4,128)}, f32[8,128]{1,0:T(8,128)}) custom-call(f32[16,1085,4,128]{3,2,1,0:T(4,128)} %get-tuple-element.389.grad_ref, f32[8,128]{1,0:T(8,128)} %broadcast_in_dim.76.loss_ref), custom_call_target="tpu_custom_call" | custom-call | tf_op jit(solution)/shard_map/scatter_sums/pallas_call | solution.py:547
  1004.8 27.7 %update.1 = (f32[1085,4,128]{2,1,0:T(4,128)}, f32[1085,4,128]{2,1,0:T(4,128)}, f32[1085,4,128]{2,1,0:T(4,128)}, f32[1085,4,128]{2,1,0:T(4,128)}) custom-call(f32[1]{0:T(128)} %bitcast.103.squares_ref, f32[1085,4,128]{2,1,0:T(4,128)} %get-tuple-element.192.owned, f32[1085,4,128]{2,1,0:T(4,128)} %bitcast.320, f32[1085,4,128]{2,1,0:T(4,128)} %bitcast.341, ...), custom_call_target="tpu_custom_call" | custom-call | tf_op jit(solution)/shard_map/update/pallas_call | solution.py:596
  (401 shorter events, 183.6 us)
Async XLA Ops:
  152.1 49.4 %copy-start.93 = (s32[8]{0:T(128)S(1)}, s32[8]{0:T(128)}, u32[]{:S(2)}) copy-start(s32[8]{0:T(128)} %param.16) | copy-start | bytes 100
  152.1 49.4 %copy-start.94 = (s32[8]{0:T(128)S(1)}, s32[8]{0:T(128)}, u32[]{:S(2)}) copy-start(s32[8]{0:T(128)} %param.17) | copy-start | bytes 100
  152.1 49.6 %copy-start.84 = (s32[8,64]{1,0:T(8,128)S(1)}, s32[8,64]{1,0:T(8,128)}, u32[]{:S(2)}) copy-start(s32[8,64]{1,0:T(8,128)} %param.15) | copy-start | bytes 6148
  208.1 19.5 %copy-start.10 = (f32[4,64,1024]{2,1,0:T(8,128)}, f32[4,64,1024]{2,1,0:T(8,128)S(1)}, u32[]{:S(2)}) copy-start(f32[4,64,1024]{2,1,0:T(8,128)S(1)} %get-tuple-element.348) | copy-start | bytes 3145732
  420.9 31.7 %copy-start.46 = (bf16[4,64,1024]{2,1,0:T(8,128)(2,1)S(1)}, bf16[4,64,1024]{2,1,0:T(8,128)(2,1)}, u32[]{:S(2)}) copy-start(bf16[4,64,1024]{2,1,0:T(8,128)(2,1)} %copy-done.45) | copy-start | bytes 1572868
  420.9 33.0 %copy-start.25 = (bf16[4,16,64,64]{3,2,1,0:T(8,128)(2,1)S(1)}, bf16[4,16,64,64]{3,2,1,0:T(8,128)(2,1)}, u32[]{:S(2)}) copy-start(bf16[4,16,64,64]{3,2,1,0:T(8,128)(2,1)} %copy-done.24) | copy-start | bytes 1572868
  430.3 21.0 %collective-permute-start.23 = (f32[16,4096]{1,0:T(8,128)S(1)}, f32[16,4096]{1,0:T(8,128)}, u32[]{:S(2)}, u32[]{:S(2)}) collective-permute-start(f32[16,4096]{1,0:T(8,128)S(1)} %stack.135), channel_id=1, source_target_pairs={{16,0},{17,1},{18,2},{19,3},{20,4},{21,5},{22,6},{23,7},{24,8},{25... | collective-permute-start | bytes 786440 | tf_op jit(solution)/shard_map/ppermute | solution.py:1271
  442.4 7.6 collective-permute-start.14
  446.1 6.5 collective-permute-start.22
  447.4 16.1 %collective-permute-start.16 = (bf16[256,1024]{1,0:T(8,128)(2,1)}, bf16[256,1024]{1,0:T(8,128)(2,1)S(1)}, u32[]{:S(2)}, u32[]{:S(2)}) collective-permute-start(bf16[256,1024]{1,0:T(8,128)(2,1)} %bitcast.352), channel_id=1, source_target_pairs={{16,0},{17,1},{18,2},{19,3},{20,4},{21,5},{22,6},{23,7},{24,8},{25... | collective-permute-start | bytes 1572872 | tf_op jit(solution)/shard_map/ppermute | solution.py:1271
  448.7 16.9 %collective-permute-start.21 = (bf16[256,1024]{1,0:T(8,128)(2,1)}, bf16[256,1024]{1,0:T(8,128)(2,1)}, u32[]{:S(2)}, u32[]{:S(2)}) collective-permute-start(bf16[256,1024]{1,0:T(8,128)(2,1)} %bitcast.350), channel_id=1, source_target_pairs={{16,0},{17,1},{18,2},{19,3},{20,4},{21,5},{22,6},{23,7},{24,8},{25... | collective-permute-start | bytes 1572872 | tf_op jit(solution)/shard_map/ppermute | solution.py:1271
  450.0 24.2 %copy-start.57 = (f32[16,2048]{1,0:T(8,128)}, f32[16,2048]{1,0:T(8,128)S(1)}, u32[]{:S(2)}) copy-start(f32[16,2048]{1,0:T(8,128)S(1)} %collective-permute-done.14) | copy-start | bytes 393220
  450.0 5.0 collective-permute-start.15
  451.3 16.4 %collective-permute-start.19 = (bf16[256,1024]{1,0:T(8,128)(2,1)}, bf16[256,1024]{1,0:T(8,128)(2,1)}, u32[]{:S(2)}, u32[]{:S(2)}) collective-permute-start(bf16[256,1024]{1,0:T(8,128)(2,1)} %bitcast.348), channel_id=1, source_target_pairs={{16,0},{17,1},{18,2},{19,3},{20,4},{21,5},{22,6},{23,7},{24,8},{25... | collective-permute-start | bytes 1572872 | tf_op jit(solution)/shard_map/ppermute | solution.py:1271
  452.7 17.3 %collective-permute-start.17 = (bf16[256,1024]{1,0:T(8,128)(2,1)S(1)}, bf16[256,1024]{1,0:T(8,128)(2,1)}, u32[]{:S(2)}, u32[]{:S(2)}) collective-permute-start(bf16[256,1024]{1,0:T(8,128)(2,1)S(1)} %bitcast.346), channel_id=1, source_target_pairs={{16,0},{17,1},{18,2},{19,3},{20,4},{21,5},{22,6},{23,7},{24,8},{25... | collective-permute-start | bytes 1572872 | tf_op jit(solution)/shard_map/ppermute | solution.py:1271
  455.0 21.1 %collective-permute-start.11 = (bf16[256,1024]{1,0:T(8,128)(2,1)}, bf16[256,1024]{1,0:T(8,128)(2,1)}, u32[]{:S(2)}, u32[]{:S(2)}) collective-permute-start(bf16[256,1024]{1,0:T(8,128)(2,1)} %bitcast.67), channel_id=1, source_target_pairs={{0,16},{1,17},{2,18},{3,19},{4,20},{5,21},{6,22},{7,23},{8,24},{9,... | collective-permute-start | bytes 1572872 | tf_op jit(solution)/shard_map/ppermute | solution.py:1271
  463.5 17.3 %collective-permute-start.13 = (bf16[256,1024]{1,0:T(8,128)(2,1)}, bf16[256,1024]{1,0:T(8,128)(2,1)}, u32[]{:S(2)}, u32[]{:S(2)}) collective-permute-start(bf16[256,1024]{1,0:T(8,128)(2,1)} %bitcast.69), channel_id=1, source_target_pairs={{0,16},{1,17},{2,18},{3,19},{4,20},{5,21},{6,22},{7,23},{8,24},{9,... | collective-permute-start | bytes 1572872 | tf_op jit(solution)/shard_map/ppermute | solution.py:1271
  465.6 17.3 %collective-permute-start.10 = (bf16[256,1024]{1,0:T(8,128)(2,1)}, bf16[256,1024]{1,0:T(8,128)(2,1)}, u32[]{:S(2)}, u32[]{:S(2)}) collective-permute-start(bf16[256,1024]{1,0:T(8,128)(2,1)} %reshape_reshape.7), channel_id=1, source_target_pairs={{0,16},{1,17},{2,18},{3,19},{4,20},{5,21},{6,22},{7,23},{8,24},{9,... | collective-permute-start | bytes 1572872 | tf_op jit(solution)/shard_map/ppermute | solution.py:1271
  467.7 17.4 %collective-permute-start.3 = (bf16[832,512]{1,0:T(8,128)(2,1)}, bf16[832,512]{1,0:T(8,128)(2,1)}, u32[]{:S(2)}, u32[]{:S(2)}) collective-permute-start(bf16[832,512]{1,0:T(8,128)(2,1)} %bitcast.338), channel_id=1, source_target_pairs={{0,16},{1,17},{2,18},{3,19},{4,20},{5,21},{6,22},{7,23},{8,24},{9,... | collective-permute-start | bytes 2555912 | tf_op jit(solution)/shard_map/ppermute | solution.py:1271
  469.9 21.5 %collective-permute-start.7 = (bf16[832,512]{1,0:T(8,128)(2,1)}, bf16[832,512]{1,0:T(8,128)(2,1)}, u32[]{:S(2)}, u32[]{:S(2)}) collective-permute-start(bf16[832,512]{1,0:T(8,128)(2,1)} %bitcast.336), channel_id=1, source_target_pairs={{0,16},{1,17},{2,18},{3,19},{4,20},{5,21},{6,22},{7,23},{8,24},{9,... | collective-permute-start | bytes 2555912 | tf_op jit(solution)/shard_map/ppermute | solution.py:1271
  476.1 29.5 %copy-start.4 = (bf16[4,208,3,16,32]{1,4,3,0,2:T(8,128)(2,1)S(1)}, bf16[4,208,3,16,32]{1,4,3,0,2:T(8,128)(2,1)}, u32[]{:S(2)}) copy-start(bf16[4,208,3,16,32]{1,4,3,0,2:T(8,128)(2,1)} %copy-done.3) | copy-start | bytes 7667716
  476.1 16.6 %collective-permute-start.8 = (bf16[832,512]{1,0:T(8,128)(2,1)}, bf16[832,512]{1,0:T(8,128)(2,1)}, u32[]{:S(2)}, u32[]{:S(2)}) collective-permute-start(bf16[832,512]{1,0:T(8,128)(2,1)} %bitcast.334), channel_id=1, source_target_pairs={{0,16},{1,17},{2,18},{3,19},{4,20},{5,21},{6,22},{7,23},{8,24},{9,... | collective-permute-start | bytes 2555912 | tf_op jit(solution)/shard_map/ppermute | solution.py:1271
  480.7 19.6 %collective-permute-start.2 = (bf16[832,512]{1,0:T(8,128)(2,1)}, bf16[832,512]{1,0:T(8,128)(2,1)}, u32[]{:S(2)}, u32[]{:S(2)}) collective-permute-start(bf16[832,512]{1,0:T(8,128)(2,1)} %copy.102), channel_id=1, source_target_pairs={{0,16},{1,17},{2,18},{3,19},{4,20},{5,21},{6,22},{7,23},{8,24},{9,... | collective-permute-start | bytes 2555912 | tf_op jit(solution)/shard_map/ppermute | solution.py:1271
  483.0 19.6 %collective-permute-start.4 = (bf16[832,512]{1,0:T(8,128)(2,1)}, bf16[832,512]{1,0:T(8,128)(2,1)}, u32[]{:S(2)}, u32[]{:S(2)}) collective-permute-start(bf16[832,512]{1,0:T(8,128)(2,1)} %bitcast.332), channel_id=1, source_target_pairs={{0,16},{1,17},{2,18},{3,19},{4,20},{5,21},{6,22},{7,23},{8,24},{9,... | collective-permute-start | bytes 2555912 | tf_op jit(solution)/shard_map/ppermute | solution.py:1271
  485.2 41.8 %collective-permute-start.20 = (bf16[256,4096]{1,0:T(8,128)(2,1)}, bf16[256,4096]{1,0:T(8,128)(2,1)}, u32[]{:S(2)}, u32[]{:S(2)}) collective-permute-start(bf16[256,4096]{1,0:T(8,128)(2,1)} %bitcast.344), channel_id=1, source_target_pairs={{16,0},{17,1},{18,2},{19,3},{20,4},{21,5},{22,6},{23,7},{24,8},{25... | collective-permute-start | bytes 6291464 | tf_op jit(solution)/shard_map/ppermute | solution.py:1271
  491.4 30.2 %collective-permute-start.18 = (bf16[256,3072]{1,0:T(8,128)(2,1)}, bf16[256,3072]{1,0:T(8,128)(2,1)}, u32[]{:S(2)}, u32[]{:S(2)}) collective-permute-start(bf16[256,3072]{1,0:T(8,128)(2,1)} %convert_element_type.240), channel_id=1, source_target_pairs={{16,0},{17,1},{18,2},{19,3},{20,4},{21,5},{22,6},{23,7},{24,8},{25... | collective-permute-start | bytes 4718600 | tf_op jit(solution)/shard_map/ppermute | solution.py:1271
  492.7 39.2 %collective-permute-start.5 = (bf16[832,2048]{1,0:T(8,128)(2,1)}, bf16[832,2048]{1,0:T(8,128)(2,1)}, u32[]{:S(2)}, u32[]{:S(2)}) collective-permute-start(bf16[832,2048]{1,0:T(8,128)(2,1)} %bitcast.328), channel_id=1, source_target_pairs={{0,16},{1,17},{2,18},{3,19},{4,20},{5,21},{6,22},{7,23},{8,24},{9,... | collective-permute-start | bytes 10223624 | tf_op jit(solution)/shard_map/ppermute | solution.py:1271
  500.4 18.4 %collective-permute-start = (bf16[832,512]{1,0:T(8,128)(2,1)}, bf16[832,512]{1,0:T(8,128)(2,1)}, u32[]{:S(2)}, u32[]{:S(2)}) collective-permute-start(bf16[832,512]{1,0:T(8,128)(2,1)} %bitcast.330), channel_id=1, source_target_pairs={{0,16},{1,17},{2,18},{3,19},{4,20},{5,21},{6,22},{7,23},{8,24},{9,... | collective-permute-start | bytes 2555912 | tf_op jit(solution)/shard_map/ppermute | solution.py:1271
  502.5 29.3 %collective-permute-start.6 = (bf16[832,2048]{1,0:T(8,128)(2,1)}, bf16[832,2048]{1,0:T(8,128)(2,1)}, u32[]{:S(2)}, u32[]{:S(2)}) collective-permute-start(bf16[832,2048]{1,0:T(8,128)(2,1)} %bitcast.310), channel_id=1, source_target_pairs={{0,16},{1,17},{2,18},{3,19},{4,20},{5,21},{6,22},{7,23},{8,24},{9,... | collective-permute-start | bytes 10223624 | tf_op jit(solution)/shard_map/ppermute | solution.py:1271
  518.8 13.1 %collective-permute-start.1 = (bf16[832,1536]{1,0:T(8,128)(2,1)}, bf16[832,1536]{1,0:T(8,128)(2,1)}, u32[]{:S(2)}, u32[]{:S(2)}) collective-permute-start(bf16[832,1536]{1,0:T(8,128)(2,1)} %copy.100), channel_id=1, source_target_pairs={{0,16},{1,17},{2,18},{3,19},{4,20},{5,21},{6,22},{7,23},{8,24},{9,... | collective-permute-start | bytes 7667720 | tf_op jit(solution)/shard_map/ppermute | solution.py:1271
  521.6 10.3 collective-permute-start.12
  527.0 4.8 collective-permute-start.9
  (93 other events, 476.6 us)

commit v2 on v1

--- a/solution.py
+++ b/solution.py
@@ -86,16 +86,24 @@
 
 
 DP_GRID = (4, 2, 2)
-ORDERS = (("y", "z", "x"), ("x", "z", "y"), ("z", "x", "y"))
+YZX, XZY, ZXY = ("y", "z", "x"), ("x", "z", "y"), ("z", "x", "y")
+SPLIT = 2
+ORDERS = (YZX,) * SPLIT + (XZY,) * SPLIT + (ZXY,) * SPLIT
+PARTS = len(ORDERS)
+OWN_FIRST = tuple(range(2 * SPLIT, 3 * SPLIT)) + tuple(range(2 * SPLIT))
+SHARES = (0.41, 0.26, 0.33)
 WAYS = ("x", "y", "up", "down")
 CHUNK = 16
 OPPOSITE = {"x": "x", "y": "y", "up": "down", "down": "up"}
 
 
 def part_ranges(units):
-    first = int(units * 0.41)
-    second = int(units * 0.26)
-    return [(0, first), (first, second), (first + second, units - first - second)]
+    ends = [0]
+    for share in SHARES:
+        for _ in range(SPLIT):
+            ends.append(ends[-1] + share / SPLIT)
+    ends = [round(end * units) for end in ends[:-1]] + [units]
+    return [(start, end - start) for start, end in zip(ends, ends[1:])]
 
 
 def relatives():
@@ -259,7 +267,7 @@
         )
 
     sent = []
-    for part in (2, 0, 1):
+    for part in OWN_FIRST:
         for way in onward(ORDERS[part], (0, 0, 0)):
             when(
                 spot.exists[way],
@@ -269,12 +277,12 @@
     local = pltpu.make_async_copy(own_ref, out_ref.at[spot.grp, spot.dp], local_sem)
     local.start()
     tell()
-    for part in range(3):
+    for part in range(PARTS):
         copy(part, spot.dp, "core", True).start()
         sent.append((part, spot.dp, "core", None, True))
     for place in relatives():
         _, source, inside = spot.at(place)
-        for part in range(3):
+        for part in range(PARTS):
             ways = onward(ORDERS[part], place)
 
             def pass_on(part=part, source=source, ways=ways):
@@ -293,7 +301,7 @@
         when(condition, lambda: copy(part, source, way, from_own).wait_send())
 
     def await_core(source, carry):
-        for part in range(3):
+        for part in range(PARTS):
             landed = out_ref.at[1 - spot.grp, source, pl.ds(*ranges[part])]
             pltpu.make_async_remote_copy(
                 src_ref=landed,
@@ -329,10 +337,10 @@
             pltpu.VMEM((units, 4, LANES), BF16),
             pltpu.VMEM((32, 8, LANES), F32),
             dma,
-            dma((3, 16, 4)),
-            dma((3, 16)),
-            dma((3, 16)),
-            dma((3, 16)),
+            dma((PARTS, 16, 4)),
+            dma((PARTS, 16)),
+            dma((PARTS, 16)),
+            dma((PARTS, 16)),
             dma((32,)),
             dma((32,)),
         ],
@@ -365,10 +373,10 @@
 def scatter_kernel(grad_ref, loss_ref, out_ref, sums_ref, *refs):
     ranges = part_ranges(grad_ref.shape[1])
     landing = {}
-    for part in range(3):
+    for part in range(PARTS):
         for number, way in enumerate(WAYS):
             landing[part, way] = refs[part * 4 + number]
-    stage, total, tiles, send_sem, recv_sem, stage_sem, out_sem, tile_send, tile_recv = refs[12:]
+    stage, total, tiles, send_sem, recv_sem, stage_sem, out_sem, tile_send, tile_recv = refs[4 * PARTS :]
     spot = Spot()
     spot.greet()
 
@@ -412,23 +420,20 @@
     def own(part, owner):
         return grad_ref.at[owner, pl.ds(*ranges[part])]
 
-    nodes = [((0, 0, 0), part) for part in (2, 0, 1)]
-    nodes += [(place, part) for place in relatives() for part in range(3)]
-    nodes.reverse()
+    nodes = [(place, part) for place in relatives()[::-1] for part in range(PARTS)]
+    nodes += [((0, 0, 0), part) for part in range(PARTS)]
     sent = []
     inner = []
     for place, part in nodes:
+        z, owner, inside = spot.at(place)
         ways = onward(ORDERS[part], place)
-        z, owner, inside = spot.at(place)
-        if ways:
-            inner.append((part, place, ways, z, owner, inside))
-        else:
-            when(inside, lambda: send(part, place, own(part, owner)).start())
         if place != (0, 0, 0):
             sent.append((part, place, owner, inside))
+        inner.append((part, place, ways, z, owner, inside))
+    staged_nodes = [node for node in inner if node[2]]
 
     def staged(number):
-        part, _, _, _, owner, _ = inner[number]
+        part, _, _, _, owner, _ = staged_nodes[number]
         return pltpu.make_async_copy(
             own(part, owner),
             stage.at[number % STAGES, pl.ds(0, ranges[part][1])],
@@ -436,11 +441,16 @@
         )
 
     for number in range(STAGES - 1):
-        when(inner[number][5], lambda: staged(number).start())
-    for number, (part, place, ways, z, owner, inside) in enumerate(inner):
+        when(staged_nodes[number][5], lambda: staged(number).start())
+    number = -1
+    for part, place, ways, z, owner, inside in inner:
+        if not ways:
+            when(inside, lambda: send(part, place, own(part, owner)).start())
+            continue
+        number += 1
         ahead = number + STAGES - 1
-        if ahead < len(inner):
-            when(inner[ahead][5], lambda: staged(ahead).start())
+        if ahead < len(staged_nodes):
+            when(staged_nodes[ahead][5], lambda: staged(ahead).start())
         length = ranges[part][1]
         root = place == (0, 0, 0)
 
@@ -525,7 +535,7 @@
     units = grads.shape[1]
     ranges = part_ranges(units)
     scratch = []
-    for part in range(3):
+    for part in range(PARTS):
         for way in WAYS:
             keys, depth = SLOTS[part][way]
             scratch.append(pltpu.VMEM((len(keys) * depth, ranges[part][1], 4, LANES), F32))
@@ -535,8 +545,8 @@
         pltpu.VMEM((STAGES, largest, 4, LANES), F32),
         pltpu.VMEM((units, 4, LANES), F32),
         pltpu.VMEM((32, 8, LANES), F32),
-        dma((3, 16)),
-        dma((3, 16, 4)),
+        dma((PARTS, 16)),
+        dma((PARTS, 16, 4)),
         dma((STAGES,)),
         dma,
         dma((32,)),
@@ -560,36 +570,33 @@
     )(grads, loss)
 
 
-def update_values(owned, squares, params, first_moment, second_moment, average):
-    clipped = owned * jnp.minimum(1.0, CLIP / jnp.sqrt(squares))
+def update_values(owned, scale, params, first_moment, second_moment, average):
+    clipped = owned * scale
     new_first = BETA_ONE * first_moment + (1.0 - BETA_ONE) * clipped
     new_second = BETA_TWO * second_moment + (1.0 - BETA_TWO) * clipped * clipped
-    direction = (
-        new_first
-        / (1.0 - BETA_ONE**STEP)
-        / (jnp.sqrt(new_second / (1.0 - BETA_TWO**STEP)) + ADAM_EPS)
-    )
+    root = jnp.sqrt(new_second * (1.0 / (1.0 - BETA_TWO**STEP)))
+    direction = new_first * (1.0 / (1.0 - BETA_ONE**STEP)) / (root + ADAM_EPS)
     new_params = params - RATE * (direction + DECAY_WEIGHT * params)
     new_average = AVERAGE_KEEP * average + (1.0 - AVERAGE_KEEP) * new_params
     return new_params, new_first, new_second, new_average
 
 
-def update_kernel(squares_ref, owned, params, first, second, average, *outs):
-    squares = squares_ref[0]
-
-    def step(index, carry):
-        block = pl.ds(index * 5, 5)
-        values = update_values(
-            owned[block], squares, params[block], first[block], second[block], average[block]
-        )
-        for out, value in zip(outs, values):
+def update_kernel(scale_ref, *refs):
+    scale = scale_ref[0]
+    step = 31
+
+    def one(index, carry):
+        block = pl.ds(index * step, step)
+        owned, params, first, second, average = [ref[block] for ref in refs[:5]]
+        values = update_values(owned, scale, params, first, second, average)
+        for out, value in zip(refs[5:], values):
             out[block] = value
         return carry
 
-    lax.fori_loop(0, owned.shape[0] // 5, step, 0)
-
-
-def update(squares, arrays):
+    lax.fori_loop(0, refs[0].shape[0] // step, one, 0)
+
+
+def update(scale, arrays):
     units = arrays[0].shape[0]
     depth = 155
     spec = pl.BlockSpec((depth, 4, LANES), lambda i: (i, 0, 0))
@@ -600,7 +607,7 @@
         in_specs=[pl.BlockSpec(memory_space=pltpu.SMEM)] + [spec] * 5,
         out_specs=[spec] * 4,
         name="update",
-    )(squares.reshape(1), *arrays)
+    )(scale.reshape(1), *arrays)
 
 
 def sections(layout, base):
@@ -833,33 +840,139 @@
     return items, offset
 
 
-def product_kernel(rows, layout, lent, count, *refs):
-    factors = [refs[4 * n : 4 * n + 4] for n in range(count)]
-    mine_ref, other_ref, out_ref = refs[4 * count : 4 * count + 3]
-    refs = refs[4 * count + 3 :]
-    lefts, rights = refs[:count], refs[count : 2 * count]
-    turned_left, tall, rows_out, in_sem, out_sem = refs[2 * count :]
+ROLES = (
+    (ENC_LAYOUT, [], (0, 1, 2, 3)),
+    (DEC_LAYOUT, LENT, (6, 7, 8, 9, 10, 4, 5)),
+)
+PAIRS = 11
+
+
+def factor_buffers(shapes):
+    sizes = []
+    places = {}
+    for role in (1, 0):
+        taken = set()
+        for number in ROLES[role][2]:
+            for side in range(2):
+                length, columns = shapes[2 * number + side]
+                fits = [
+                    n
+                    for n, size in enumerate(sizes)
+                    if n not in taken and size[0] == 2 * length and size[1] >= columns
+                ]
+                if fits:
+                    place = min(fits, key=lambda n: sizes[n][1])
+                else:
+                    place = len(sizes)
+                    sizes.append((2 * length, columns))
+                taken.add(place)
+                places[role, number, side] = place
+    return sizes, places
+
+
+def product_kernel(rows, shapes, *refs):
+    factors, vectors, out_ref = refs[: 2 * PAIRS], refs[2 * PAIRS : 2 * PAIRS + 2], refs[24]
+    sizes, places = factor_buffers(shapes)
+    buffers = refs[25 : 25 + len(sizes)]
+    refs = refs[25 + len(sizes) :]
+    others = refs[:2]
+    turned_left, tall, rows_out, own_sem, send_sem, recv_sem, out_sem = refs[2:]
+    core = lax.axis_index("grp")
+    sibling = (1 - core, lax.axis_index("dp"))
+    barrier = pltpu.get_barrier_semaphore()
+    pl.semaphore_signal(barrier, inc=1, device_id=sibling, device_id_type=MESH)
+    pl.semaphore_wait(barrier, 1)
+
+    def half_of(role, number, side, part):
+        length, columns = shapes[2 * number + side]
+        buffer = buffers[places[role, number, side]]
+        return buffer.at[pl.ds(part * length, length), pl.ds(0, columns)]
+
+    def local(role, number, side):
+        return pltpu.make_async_copy(
+            factors[2 * number + side], half_of(role, number, side, 0), own_sem.at[number, side]
+        )
+
+    def remote(role, number, side):
+        return pltpu.make_async_remote_copy(
+            src_ref=factors[2 * number + side],
+            dst_ref=half_of(role, number, side, 1),
+            send_sem=send_sem.at[number, side],
+            recv_sem=recv_sem.at[number, side],
+            device_id=sibling,
+            device_id_type=MESH,
+        )
+
+    def remote_vectors(role):
+        return pltpu.make_async_remote_copy(
+            src_ref=vectors[role],
+            dst_ref=others[role],
+            send_sem=send_sem.at[PAIRS, role],
+            recv_sem=recv_sem.at[PAIRS, role],
+            device_id=sibling,
+            device_id_type=MESH,
+        )
+
+    def act(role):
+        remote_vectors(1 - role).start()
+        pending = [(number, side) for number in ROLES[role][2] for side in range(2)]
+        for number, side in pending:
+            local(role, number, side).start()
+        given = [(number, side) for number in ROLES[1 - role][2] for side in range(2)]
+        for number, side in given:
+            remote(1 - role, number, side).start()
+        remote_vectors(role).wait_recv()
+
+        def ready(number):
+            for side in range(2):
+                local(role, number, side).wait()
+                remote(role, number, side).wait_recv()
+
+        lefts, rights = [], []
+        for number in ROLES[role][2]:
+            for side, views in ((0, lefts), (1, rights)):
+                length, columns = shapes[2 * number + side]
+                buffer = buffers[places[role, number, side]]
+                views.append(buffer.at[pl.ds(0, 2 * length), pl.ds(0, columns)])
+        fill_row(
+            rows,
+            ROLES[role],
+            ready,
+            lefts,
+            rights,
+            vectors[role],
+            others[role],
+            turned_left,
+            tall,
+            rows_out,
+            out_ref,
+            out_sem,
+        )
+        for number, side in given:
+            remote(1 - role, number, side).wait_send()
+        remote_vectors(1 - role).wait_send()
+
+    for role in range(2):
+        pl.when(core == role)(functools.partial(act, role))
+
+
+def fill_row(
+    rows,
+    role,
+    ready,
+    lefts,
+    rights,
+    mine_ref,
+    other_ref,
+    turned_left,
+    tall,
+    rows_out,
+    out_ref,
+    out_sem,
+):
+    layout, lent, numbers = role
     lane = lax.broadcasted_iota(jnp.int32, (1, LANES), 1)
     half = LANES // 2
-
-    def load(n):
-        copies = []
-        for side, buffer in ((0, lefts[n]), (1, rights[n])):
-            length = factors[n][2 * side].shape[0]
-            for part in range(2):
-                copies.append(
-                    pltpu.make_async_copy(
-                        factors[n][2 * side + part],
-                        buffer.at[pl.ds(part * length, length)],
-                        in_sem.at[n, 2 * side + part],
-                    )
-                )
-        return copies
-
-    for n in range(count):
-        for copy in load(n):
-            copy.start()
-
     items, used = stream_items(layout, lent)
     groups = []
     current = []
@@ -885,8 +998,7 @@
         tiles = -(-columns // LANES)
         width = min(WIDTH, columns)
         if start == 0:
-            for copy in load(number):
-                copy.wait()
+            ready(numbers[number])
             if shifted:
                 length = rights[number].shape[0]
 
@@ -998,31 +1110,35 @@
         flight.wait()
 
 
-def flat_gradient(rows, layout, lent, factors, mine, other):
-    shapes = [shape for shape in layout if len(shape) == 2] + lent
-    lefts = [pltpu.VMEM((2 * f[0].shape[0], f[0].shape[1]), BF16) for f in factors]
-    rights = [pltpu.VMEM((2 * f[2].shape[0], f[2].shape[1]), BF16) for f in factors]
-    longest = max(2 * f[0].shape[0] for f in factors)
+def flat_gradient(rows, factors, enc_vectors, dec_vectors):
+    shapes = [factor.shape for factor in factors]
+    sizes, _ = factor_buffers(shapes)
+    longest = max(length for length, _ in sizes)
     dma = pltpu.SemaphoreType.DMA
     anywhere = pl.BlockSpec(memory_space=pl.ANY)
     vmem = pl.BlockSpec(memory_space=pltpu.VMEM)
     return pl.pallas_call(
-        functools.partial(product_kernel, rows, layout, lent, len(shapes)),
+        functools.partial(product_kernel, rows, shapes),
         out_shape=jax.ShapeDtypeStruct((rows, LANES), F32),
-        in_specs=[anywhere] * (4 * len(shapes)) + [vmem, vmem],
+        in_specs=[anywhere] * (2 * PAIRS) + [vmem, vmem],
         out_specs=anywhere,
-        scratch_shapes=lefts
-        + rights
+        scratch_shapes=[pltpu.VMEM(size, BF16) for size in sizes]
         + [
+            pltpu.VMEM(enc_vectors.shape, F32),
+            pltpu.VMEM(dec_vectors.shape, F32),
             pltpu.VMEM((256, longest), BF16),
             pltpu.VMEM((padded(HEAD) // LANES, DD, LANES), F32),
             pltpu.VMEM((2, PIECE + 128, LANES), F32),
-            dma((len(shapes), 4)),
+            dma((PAIRS, 2)),
+            dma((PAIRS + 1, 2)),
+            dma((PAIRS + 1, 2)),
             dma((2,)),
         ],
-        compiler_params=pltpu.CompilerParams(vmem_limit_bytes=62 * 2**20),
+        compiler_params=pltpu.CompilerParams(
+            collective_id=2, has_side_effects=True, vmem_limit_bytes=63 * 2**20
+        ),
         name="flat_gradient",
-    )(*[a for f in factors for a in f], mine, other)
+    )(*factors, enc_vectors, dec_vectors)
 
 
 Bag = types.SimpleNamespace
@@ -1267,19 +1383,6 @@
     return jnp.stack(rows)
 
 
-def to_core(array, core):
-    return lax.ppermute(array, "grp", [(1 - core, core)])
-
-
-def factor_list(pairs, core):
-    factors = []
-    for left, right in pairs:
-        left = left.reshape(-1, left.shape[-1])
-        right = right.reshape(-1, right.shape[-1])
-        factors.append((left, to_core(left, core), right, to_core(right, core)))
-    return factors
-
-
 def gradient_row(rows, enc_grads, enc_pairs, dec_grads, dec_pairs):
     e, d = enc_grads, dec_grads
     enc_vectors = vector_rows(
@@ -1292,15 +1395,10 @@
         VEC_COLS[1],
     )
     e, d = enc_pairs, dec_pairs
-    first = factor_list([e.pe_w, e.qkv_w, e.fc1_w, e.emb_w], 0)
-    second = factor_list([d.qkv_w, d.out_w, d.fc1_w, d.fc2_w, d.head_w, e.out_w, e.fc2_w], 1)
-    enc_other = to_core(enc_vectors, 0)
-    dec_other = to_core(dec_vectors, 1)
-    return lax.cond(
-        lax.axis_index("grp") == 0,
-        lambda: flat_gradient(rows, ENC_LAYOUT, [], first, enc_vectors, enc_other),
-        lambda: flat_gradient(rows, DEC_LAYOUT, LENT, second, dec_vectors, dec_other),
-    )
+    pairs = [e.pe_w, e.qkv_w, e.fc1_w, e.emb_w, e.out_w, e.fc2_w]
+    pairs += [d.qkv_w, d.out_w, d.fc1_w, d.fc2_w, d.head_w]
+    factors = [factor.reshape(-1, factor.shape[-1]) for pair in pairs for factor in pair]
+    return flat_gradient(rows, factors, enc_vectors, dec_vectors)
 
 
 def bags(parts):
@@ -1317,6 +1415,10 @@
     dec.fc2_b, dec.lnf_g, dec.lnf_b = [d[n, :DD] for n in range(6, 9)]
     dec.head_b = d[9, : padded(HEAD)]
     return enc, dec
+
+
+def clip_scale(squares):
+    return jnp.minimum(1.0, CLIP / jnp.sqrt(squares))
 
 
 def body(
@@ -1359,13 +1461,13 @@
         )
         squares = jnp.sum(sums[:4])
         loss_sum = sums[4, 0]
-        outs = update(squares, [owned] + shards)
+        outs = update(clip_scale(squares), [owned] + shards)
         outs = [out.reshape(params.shape) for out in outs]
     else:
         owned = lax.psum_scatter(gradient, "dp", scatter_dimension=0, tiled=True)
         owned = owned.reshape(params.shape)
         squares, loss_sum = lax.psum((jnp.sum(owned * owned), loss_local), ("grp", "dp"))
-        outs = update_values(owned, squares, params, first_moment, second_moment, average)
+        outs = update_values(owned, clip_scale(squares), params, first_moment, second_moment, average)
     return (*outs, loss_sum, masked_total, jnp.sqrt(squares))
 
 

time: 1050 us -> 815 us (0.78)
  Pallas kernels: 690 us -> 543 us
  starting transfers between devices: 58.6 us -> 0 us
  local copies, waits for them, and re-layouts: 101 us -> 81.2 us
    pallas_call x1, Pallas kernels: 423 us -> 290 us  [scatter_sums(): pl.pallas_call(scatter_kernel, out_shape=(jax.ShapeDtypeStruct((units, 4,...]
    ppermute x24 -> x0, starting transfers between devices: 58.6 us -> none  [to_core(): return lax.ppermute(array, 'grp', [(1 - core, core)])]
    pallas_call x1, Pallas kernels: 27.7 us -> 11.8 us  [update(): pl.pallas_call(update_kernel, grid=(units // depth,), out_shape=[jax.Shap...]
    pad x18, local copies, waits for them, and re-layouts: 13.6 us -> 0.06 us  [vector_rows(): jnp.pad(vector, (0, columns - vector.shape[0]))]
  transfers between devices with their start and end apart: 24 -> 0, of which waited for: 1 -> 0; matrix products, arithmetic and copies ran while one was open for 4% -> 0% of each run, Pallas kernels for 0% -> 0%
where the time goes in v2:
time: 815 us; the launch traced here: 807 us
  Pallas kernels  543 us (67%)
  matrix products  108 us (13%)
  local copies, waits for them, and re-layouts  81.2 us (10%)
  other arithmetic  69.6 us (9%)
    pallas_call x1, Pallas kernels, scatter_sums(): pl.pallas_call(scatter_kernel, out_shape=(jax.ShapeDtypeStruct((units, 4,...  290 us
    pallas_call x1, Pallas kernels, gather_rows(): pl.pallas_call(gather_kernel, out_shape=(jax.ShapeDtypeStruct((2, 16, uni...  149 us
    pallas_call x1, Pallas kernels, flat_gradient(): pl.pallas_call(functools.partial(product_kernel, rows, shapes), out_shape...  47.9 us
    pallas_call x1, Pallas kernels, weight_matrices(): pl.pallas_call(functools.partial(matrix_kernel, rows), out_shape=[jax.Sha...  44.8 us
    dot_general x10, matrix products, input_grad(): jnp.einsum('...n,kn->...k', grad_rows, right, preferred_element_type=F32)  36 us
    dot_general x10, matrix products, linear(): return jnp.einsum('...k,kn->...n', left, right, preferred_element_type=F32)  28.2 us
    convert_element_type x2, other arithmetic, block_forward(): active = gelu_exact(pre_act).astype(BF16)  26.6 us
    convert_element_type x7, local copies, waits for them, and re-layouts, block_backward(): grad_qkv = jnp.stack([grad_query, grad_key, grad_value], axis=2).reshape(...  24.8 us

profile of v2, /device:TPU:0, one launch (start us, length us, event | category | flops | bytes accessed | tf_op | source)
XLA Modules:
  0.0 806.7 jit_solution(12817941351832294635)
XLA Ops:
  7.5 3.0 multiply_sine_fusion.3
  14.6 3.9 convert_subtract_fusion
  18.5 4.0 multiply_sine_fusion.1
  22.5 148.9 %gather_rows.1 = (bf16[2,16,1085,4,128]{4,3,2,1,0:T(4,128)(2,1)}, f32[8,128]{1,0:T(8,128)}) custom-call(f32[1085,4,128]{2,1,0:T(4,128)} %bitcast.316, f32[8,128]{1,0:T(8,128)} %broadcast_in_dim.57.masked_ref), custom_call_target="tpu_custom_call" | custom-call | tf_op jit(solution)/shard_map/gather_rows/pallas_call | solution.py:327
  172.5 44.8 %weight_matrices.1 = (bf16[768,1024]{1,0:T(8,128)(2,1)}, bf16[1024,3072]{1,0:T(8,128)(2,1)}, bf16[1024,4096]{1,0:T(8,128)(2,1)}, bf16[1024,512]{1,0:T(8,128)(2,1...) custom-call(bf16[138880,128]{1,0:T(8,128)(2,1)} %bitcast.302), custom_call_target="tpu_custom_call" | custom-call | tf_op jit(solution)/shard_map/weight_matrices/pallas_call | solution.py:807
  230.5 3.3 reshape.567
  233.8 3.8 fusion.152
  249.9 7.4 fusion.99
  257.4 10.7 %multiply_convert_fusion.2 = (bf16[4,64,4096]{2,1,0:T(8,128)(2,1)S(1)}, f32[4,64,4096]{2,1,0:T(8,128)}) fusion(f32[4,64,4096]{2,1,0:T(8,128)S(1)} %get-tuple-element.145, u8[64,4096]{1,0:T(8,128)(4,1)S(1)} %get-tuple-element.52, u8[64,4096]{1,0:T(8,128)(4,1)S(1)} %get-tuple-element.51), kind=kLoop, calls=%fused_computation.55 | loop fusion | flops 73400320 | bytes 11010048 | tf_op jit(solution)/shard_map/convert_element_type | solution.py:1227
  272.0 3.0 fusion.159
  277.5 3.0 convolution_convert_fusion
  280.5 4.5 copy.52
  285.0 4.5 fusion.162
  289.5 3.0 fusion
  294.4 4.3 fusion.62
  307.5 3.7 fusion.52
  311.2 15.9 %multiply_convert_fusion.1 = (bf16[4,208,2048]{2,1,0:T(8,128)(2,1)S(1)}, f32[4,208,2048]{2,1,0:T(8,128)S(1)}) fusion(f32[4,208,2048]{2,1,0:T(8,128)S(1)} %get-tuple-element.154, f32[2048]{0:T(1024)S(1)} %bitcast.363, u8[208,2048]{1,0:T(8,128)(4,1)S(1)} %get-tuple-element.50, u8[208,2048]{1,0:T(8,128)(4,1)S(1)} %get-tuple-element.49), kind=kLoop, calls=%fused_computation.26 | loop fusion | flops 120979456 | bytes 17899520 | tf_op jit(solution)/shard_map/convert_element_type | solution.py:1227
  341.9 6.4 fusion.150
  354.6 8.1 %fusion.53 = bf16[4,208,1,16,32]{1,4,3,0,2:T(8,128)(2,1)} fusion(bf16[4,208,16,32]{1,3,2,0:T(8,128)(2,1)S(1)} %bitcast.314, f32[4,16,208,208]{2,3,1,0:T(8,128)} %copy-done, f32[4,16,208]{2,1,0:T(8,128)S(1)} %log_add_fusion), kind=kOutput, calls=%fused_computation.121 | convolution fusion | flops 182747136 | bytes 12832768 | tf_op jit(solution)/shard_map/bhlm,blhd->bmhd/dot_general | solution.py:1274
  362.7 9.8 %multiply_reduce_fusion = (f32[4,16,208]{2,1,0:T(8,128)S(1)}, f32[4,16,208,208]{2,3,1,0:T(8,128)}) fusion(f32[4,16,208,208]{2,3,1,0:T(8,128)} %copy-done, f32[4,16,208]{2,1,0:T(8,128)S(1)} %log_add_fusion, bf16[4,208,16,32]{1,3,2,0:T(8,128)(2,1)S(1)} %bitcast.315, bf16[4,208,3,16,32]{1,4,3,2,0:T(8,128)(2,1)S(1)} %bitcast.305), kind=kOutput, calls=%fused_computation.1 | convolution fusion | flops 185502720 | bytes 24367104 | tf_op jit(solution)/shard_map/blhd,bmhd->bhlm/dot_general | solution.py:1277
  372.6 7.3 multiply_convert_fusion
  384.1 4.7 copy.80
  388.8 6.7 convert_element_type.235
  395.5 4.5 copy.82.refs_13_
  411.2 7.5 fusion.151
  418.8 6.8 multiply_reduce_fusion.16
  437.9 3.2 convert_element_type.234.refs_3_
  441.1 3.2 convert_element_type.232
  444.2 5.8 multiply_reduce_fusion.17
  452.9 47.9 %flat_gradient.1 = f32[69440,128]{1,0:T(8,128)} custom-call(bf16[256,768]{1,0:T(8,128)(2,1)} %bitcast.342, bf16[256,1024]{1,0:T(8,128)(2,1)} %bitcast.339, bf16[256,1024]{1,0:T(8,128)(2,1)} %bitcast.335, bf16[256,3072]{1,0:T(8,128)(2,1)} %convert_element_type.234.refs_3_, bf16[256,1024]{1,0:T(8,128)(2,1)} %bitcast.336, bf16[256,4096]{1,0:T(8,128)(2,1)} %bitcast.341, ...), custom_call_target="tpu_custom_call" | custom-call | tf_op jit(solution)/shard_map/flat_gradient/pallas_call | solution.py:1120
  500.8 289.7 %scatter_sums.1 = (f32[1085,4,128]{2,1,0:T(4,128)}, f32[8,128]{1,0:T(8,128)}) custom-call(f32[16,1085,4,128]{3,2,1,0:T(4,128)} %bitcast.301, f32[8,128]{1,0:T(8,128)} %broadcast_in_dim.76.loss_ref), custom_call_target="tpu_custom_call" | custom-call | tf_op jit(solution)/shard_map/scatter_sums/pallas_call | solution.py:557
  793.6 11.8 %update.1 = (f32[1085,4,128]{2,1,0:T(4,128)}, f32[1085,4,128]{2,1,0:T(4,128)}, f32[1085,4,128]{2,1,0:T(4,128)}, f32[1085,4,128]{2,1,0:T(4,128)}) custom-call(f32[1]{0:T(128)} %bitcast.102.scale_ref, f32[1085,4,128]{2,1,0:T(4,128)} %get-tuple-element.44.refs_0_, f32[1085,4,128]{2,1,0:T(4,128)} %bitcast.317, f32[1085,4,128]{2,1,0:T(4,128)} %bitcast.332, ...), custom_call_target="tpu_custom_call" | custom-call | tf_op jit(solution)/shard_map/update/pallas_call | solution.py:603
  (321 shorter events, 106.9 us)
Async XLA Ops:
  4.1 8.4 %copy-start.65 = (pred[4,64]{1,0:T(4,128)(4,1)}, pred[4,64]{1,0:T(4,128)(4,1)S(1)}, u32[]{:S(2)}) copy-start(pred[4,64]{1,0:T(4,128)(4,1)S(1)} %iota_compare_fusion.4) | copy-start | bytes 772
  12.5 212.5 %copy-start.42 = (bf16[4,64,768]{2,1,0:T(8,128)(2,1)}, bf16[4,64,768]{2,1,0:T(8,128)(2,1)S(1)}, u32[]{:S(2)}) copy-start(bf16[4,64,768]{2,1,0:T(8,128)(2,1)S(1)} %convolution_convert_fusion.3) | copy-start | bytes 1179652
  172.5 52.5 %copy-start.49 = (f32[4,64,256]{2,1,0:T(8,128)S(1)}, f32[4,64,256]{2,1,0:T(8,128)}, u32[]{:S(2)}) copy-start(f32[4,64,256]{2,1,0:T(8,128)} %get-tuple-element.132) | copy-start | bytes 786436
  172.5 52.5 %copy-start.50 = (f32[4,64,256]{2,1,0:T(8,128)S(1)}, f32[4,64,256]{2,1,0:T(8,128)}, u32[]{:S(2)}) copy-start(f32[4,64,256]{2,1,0:T(8,128)} %get-tuple-element.133) | copy-start | bytes 786436
  225.0 24.6 %copy-start.53 = (f32[1,1024]{1,0:T(1,128)}, f32[1,1024]{1,0:T(1,128)S(1)}, u32[]{:S(2)}) copy-start(f32[1,1024]{1,0:T(1,128)S(1)} %get-tuple-element.112) | copy-start | bytes 12292
  227.3 19.6 %copy-start.7 = (f32[4,64,1024]{2,1,0:T(8,128)}, f32[4,64,1024]{2,1,0:T(8,128)S(1)}, u32[]{:S(2)}) copy-start(f32[4,64,1024]{2,1,0:T(8,128)S(1)} %get-tuple-element.140) | copy-start | bytes 3145732
  249.3 18.8 %copy-start.9 = (f32[4,64,1024]{2,1,0:T(8,128)}, f32[4,64,1024]{2,1,0:T(8,128)S(1)}, u32[]{:S(2)}) copy-start(f32[4,64,1024]{2,1,0:T(8,128)S(1)} %get-tuple-element.144) | copy-start | bytes 3145732
  249.3 8.0 copy-start.57
  249.6 7.7 copy-start.61
  249.6 18.5 %slice-start.4 = ((s8[8388608]{0:T(1024)(128)(4,1)}), s8[4194304]{0:T(1024)(128)(4,1)S(1)}, s32[]{:S(2)}) async-start(s8[8388608]{0:T(1024)(128)(4,1)} %bitcast.398), calls=%async_computation.4 | async-start | bytes 8388608
  249.9 7.4 copy-start.36
  249.9 18.2 %slice-start.5 = ((s8[8388608]{0:T(1024)(128)(4,1)}), s8[4194304]{0:T(1024)(128)(4,1)S(1)}, s32[]{:S(2)}) async-start(s8[8388608]{0:T(1024)(128)(4,1)} %bitcast.398), calls=%async_computation.5 | async-start | bytes 8388608
  257.3 10.8 %copy-start.19 = (f32[4,64,4096]{2,1,0:T(8,128)}, f32[4,64,4096]{2,1,0:T(8,128)S(1)}, u32[]{:S(2)}) copy-start(f32[4,64,4096]{2,1,0:T(8,128)S(1)} %get-tuple-element.145) | copy-start | bytes 12582916
  257.4 10.8 %copy-start.68 = (f32[1,1024]{1,0:T(1,128)S(1)}, f32[1,1024]{1,0:T(1,128)}, u32[]{:S(2)}) copy-start(f32[1,1024]{1,0:T(1,128)} %get-tuple-element.110) | copy-start | bytes 12292
  298.7 5.8 copy-start.5
  298.7 5.8 copy-start.44
  311.2 15.9 %copy-start.70 = (f32[1,512]{1,0:T(1,128)S(1)}, f32[1,512]{1,0:T(1,128)}, u32[]{:S(2)}) copy-start(f32[1,512]{1,0:T(1,128)} %get-tuple-element.118) | copy-start | bytes 6148
  311.2 15.9 %copy-start.75 = (bf16[2048,512]{1,0:T(8,128)(2,1)S(1)}, bf16[2048,512]{1,0:T(8,128)(2,1)}, u32[]{:S(2)}) copy-start(bf16[2048,512]{1,0:T(8,128)(2,1)} %get-tuple-element.40) | copy-start | bytes 6291460
  341.9 6.5 copy-start.33
  341.9 6.5 copy-start.74
  354.5 8.2 %copy-start.3 = (bf16[4,208,1536]{1,2,0:T(8,128)(2,1)S(1)}, bf16[4,208,1536]{1,2,0:T(8,128)(2,1)}, u32[]{:S(2)}) copy-start(bf16[4,208,1536]{1,2,0:T(8,128)(2,1)} %copy.52) | copy-start | bytes 7667716
  354.6 18.0 %slice-start = ((s8[13631488]{0:T(1024)(128)(4,1)}), s8[4194304]{0:T(1024)(128)(4,1)S(1)}, s32[]{:S(2)}) async-start(s8[13631488]{0:T(1024)(128)(4,1)} %bitcast.299), calls=%async_computation | async-start | bytes 8388608
  354.6 18.0 %slice-start.1 = ((s8[13631488]{0:T(1024)(128)(4,1)}), s8[4194304]{0:T(1024)(128)(4,1)S(1)}, s32[]{:S(2)}) async-start(s8[13631488]{0:T(1024)(128)(4,1)} %bitcast.299), calls=%async_computation.1 | async-start | bytes 8388608
  362.7 9.8 %slice-start.2 = ((s8[13631488]{0:T(1024)(128)(4,1)}), s8[4194304]{0:T(1024)(128)(4,1)S(1)}, s32[]{:S(2)}) async-start(s8[13631488]{0:T(1024)(128)(4,1)} %bitcast.299), calls=%async_computation.2 | async-start | bytes 8388608
  362.7 9.8 %slice-start.3 = ((s8[13631488]{0:T(1024)(128)(4,1)}), s8[1048576]{0:T(1024)(128)(4,1)S(1)}, s32[]{:S(2)}) async-start(s8[13631488]{0:T(1024)(128)(4,1)} %bitcast.299), calls=%async_computation.3 | async-start | bytes 2097152
  411.2 7.6 copy-start.38
  411.2 7.6 copy-start.10
  411.2 7.6 copy-start.54
  411.2 7.6 copy-start.58
  411.2 7.6 copy-start.62
  418.7 6.9 copy-start.41
  444.2 5.8 copy-start.8
  (54 other events, 146.6 us)

commit v3 on v2

--- a/solution.py
+++ b/solution.py
@@ -1,6 +1,5 @@
 import functools
 import math
-import types
 
 import jax
 import jax.numpy as jnp
@@ -1141,280 +1140,751 @@
     )(*factors, enc_vectors, dec_vectors)
 
 
-Bag = types.SimpleNamespace
-
-
-def position_code(position, scales, width):
+LN1_G, LN1_B, LN2_G, LN2_B, FC1_B, FC2_B, LNF_G, LNF_B, LAST_B = range(1, 10)
+GROUP = 256
+TURNS = 16
+BATCH = 2
+
+
+def dot(left, right):
+    return jnp.dot(left, right, preferred_element_type=F32)
+
+
+def dot_nt(left, right):
+    return lax.dot_general(left, right, (((1,), (1,)), ((), ())), preferred_element_type=F32)
+
+
+def dot_tn(left, right):
+    return lax.dot_general(left, right, (((0,), (0,)), ((), ())), preferred_element_type=F32)
+
+
+def blocks(length, size, action):
+    def step(index, carry):
+        action(pl.ds(pl.multiple_of(index * size, size), size))
+        return carry
+
+    lax.fori_loop(0, length // size, step, 0)
+
+
+def row_step(length):
+    return 208 if length % 208 == 0 else 128
+
+
+def score_step(length):
+    return 832 if length % 208 == 0 else 256
+
+
+def normed(state):
+    centered = state - jnp.mean(state, axis=-1, keepdims=True)
+    inverse = lax.rsqrt(jnp.mean(centered * centered, axis=-1, keepdims=True) + NORM_EPS)
+    return centered * inverse, inverse
+
+
+def norm_rows(source, target, vectors, gain):
+    width = source.shape[1]
+
+    def one(rows):
+        unit, _ = normed(source[rows])
+        value = unit * vectors[pl.ds(gain, 1), pl.ds(0, width)]
+        target[rows] = (value + vectors[pl.ds(gain + 1, 1), pl.ds(0, width)]).astype(BF16)
+
+    blocks(source.shape[0], row_step(source.shape[0]), one)
+
+
+def norm_rows_back(source, grad, vectors, sums, gain, finish):
+    width = source.shape[1]
+    lanes = pl.ds(0, width)
+
+    def one(rows):
+        unit, inverse = normed(source[rows])
+        out = grad[rows]
+        sums[pl.ds(gain, 1), lanes] += jnp.sum(out * unit, axis=0, keepdims=True)
+        sums[pl.ds(gain + 1, 1), lanes] += jnp.sum(out, axis=0, keepdims=True)
+        scaled = out * vectors[pl.ds(gain, 1), lanes]
+        mean = jnp.mean(scaled, axis=-1, keepdims=True)
+        along = jnp.mean(scaled * unit, axis=-1, keepdims=True)
+        finish(rows, inverse * (scaled - mean - unit * along))
+
+    blocks(source.shape[0], row_step(source.shape[0]), one)
+
+
+def gelu_parts(value):
+    below = 0.5 * (1.0 + lax.erf(value * math.sqrt(0.5)))
+    return below, value * below
+
+
+def head_masks(depth):
+    lane = lax.broadcasted_iota(jnp.int32, (1, GROUP), 1)
+    return [
+        ((lane >= head * depth) & (lane < (head + 1) * depth)).astype(F32).astype(BF16)
+        for head in range(GROUP // depth)
+    ]
+
+
+def stack_heads(target, value, masks):
+    length = value.shape[0]
+    for head, mask in enumerate(masks):
+        target[pl.ds(head * length, length)] = value * mask
+
+
+def attention_forward(images, length, heads, qkv, bias, attend, attend_low, stacked, mixed):
+    width = mixed.shape[1]
+    depth = width // heads
+    masks = head_masks(depth)
+    groups = width // GROUP
+    scale = depth**-0.5
+
+    def one(index, carry):
+        image, group = index // groups, index % groups
+        rows = pl.ds(pl.multiple_of(image * length, length), length)
+
+        def lanes(part):
+            return pl.ds(pl.multiple_of(part * width + group * GROUP, GROUP), GROUP)
+
+        stack_heads(stacked, qkv[rows, lanes(0)], masks)
+        attend[index] = dot_nt(stacked[...], qkv[rows, lanes(1)])
+        shift = bias[pl.ds(image, 1)]
+
+        def softmax(block):
+            scores = attend[index, block] * scale + shift
+            raised = jnp.exp(scores - jnp.max(scores, axis=-1, keepdims=True))
+            value = raised / jnp.sum(raised, axis=-1, keepdims=True)
+            attend[index, block] = value
+            attend_low[block] = value.astype(BF16)
+
+        blocks(len(masks) * length, score_step(length), softmax)
+        value = qkv[rows, lanes(2)]
+        total = jnp.zeros((length, GROUP), F32)
+        for head, mask in enumerate(masks):
+            total += dot(attend_low[pl.ds(head * length, length)], value * mask)
+        mixed[rows, lanes(0)] = total.astype(BF16)
+        return carry
+
+    lax.fori_loop(0, images * groups, one, 0)
+
+
+def attention_backward(
+    images, length, heads, qkv, grad_mixed, attend, attend_low, grad_low, grads, stacked, other, out
+):
+    width = grad_mixed.shape[1]
+    depth = width // heads
+    masks = head_masks(depth)
+    groups = width // GROUP
+    scale = depth**-0.5
+
+    def one(index, carry):
+        image, group = index // groups, index % groups
+        rows = pl.ds(pl.multiple_of(image * length, length), length)
+
+        def lanes(part):
+            return pl.ds(pl.multiple_of(part * width + group * GROUP, GROUP), GROUP)
+
+        stack_heads(stacked, qkv[rows, lanes(0)], masks)
+        stack_heads(other, grad_mixed[rows, lanes(0)], masks)
+        grads[...] = dot_nt(other[...], qkv[rows, lanes(2)])
+
+        def scores(block):
+            value = attend[index, block]
+            grad = grads[block]
+            total = jnp.sum(grad * value, axis=-1, keepdims=True)
+            grad_low[block] = (value * (grad - total)).astype(BF16)
+            attend_low[block] = value.astype(BF16)
+
+        blocks(len(masks) * length, score_step(length), scores)
+        out[rows, lanes(2)] = dot_tn(attend_low[...], other[...]).astype(BF16)
+        out[rows, lanes(1)] = (dot_tn(grad_low[...], stacked[...]) * scale).astype(BF16)
+        key = qkv[rows, lanes(1)]
+        total = jnp.zeros((length, GROUP), F32)
+        for head, mask in enumerate(masks):
+            total += dot(grad_low[pl.ds(head * length, length)], key * mask)
+        out[rows, lanes(0)] = (total * scale).astype(BF16)
+        return carry
+
+    lax.fori_loop(0, images * groups, one, 0)
+
+
+def columns_loop(columns, size, action):
+    blocks(columns, min(size, columns), action)
+
+
+def feed_forward(normed_two, fc1_w, fc2_w, vectors, middle, pre, active, state):
+    bias = pl.ds(FC1_B, 1)
+
+    def up(lanes):
+        value = dot(normed_two[...], fc1_w[:, lanes]) + vectors[bias, lanes]
+        pre[:, lanes] = value
+        active[:, lanes] = gelu_parts(value)[1].astype(BF16)
+
+    columns_loop(pre.shape[1], 256, up)
+
+    def down(lanes):
+        value = dot(active[...], fc2_w[:, lanes])
+        state[:, lanes] = middle[:, lanes] + value + vectors[pl.ds(FC2_B, 1), lanes]
+
+    columns_loop(state.shape[1], 256, down)
+
+
+def feed_backward(grad_low, fc1_w, fc2_w, pre, sums, grad_pre, out):
+    def up(lanes):
+        value = pre[:, lanes]
+        below, _ = gelu_parts(value)
+        slope = below + value * (jnp.exp(-0.5 * value * value) * (1.0 / math.sqrt(2.0 * math.pi)))
+        grad = dot_nt(grad_low[...], fc2_w[lanes]) * slope
+        sums[pl.ds(FC1_B, 1), lanes] += jnp.sum(grad, axis=0, keepdims=True)
+        grad_pre[:, lanes] = grad.astype(BF16)
+
+    columns_loop(pre.shape[1], 256, up)
+
+    def down(lanes):
+        out[:, lanes] = dot_nt(grad_pre[...], fc1_w[lanes])
+
+    columns_loop(out.shape[1], 256, down)
+
+
+def turn_code(places, table):
+    lane = lax.broadcasted_iota(jnp.int32, (places.shape[0], TURNS), 1)
+    passed = (lane > 0) & (lane < TURNS - 1) & (places >= lane * GSIDE)
+    row = jnp.sum(passed.astype(F32), axis=1, keepdims=True).astype(jnp.int32)
+    parts = []
+    for pick in (row, places - row * GSIDE):
+        chosen = (lane == pick).astype(F32)
+        parts.append(jnp.dot(chosen, table, precision=HIGHEST, preferred_element_type=F32))
+    return jnp.concatenate(parts, axis=1)
+
+
+def decoder_kernel(
+    sent,
+    pixels,
+    spot_rows,
+    spot_columns,
+    table,
+    masked_ref,
+    bands_w,
+    vectors,
+    qkv_w,
+    out_w,
+    fc1_w,
+    fc2_w,
+    head_w,
+    normed_one,
+    grad_qkv,
+    mixed,
+    grad_middle_low,
+    normed_two,
+    grad_pre,
+    active,
+    grad_out_low,
+    normed_last,
+    grad_predicted,
+    grad_sent,
+    sums,
+    loss,
+    seen,
+    bias,
+    state,
+    middle,
+    last,
+    grad,
+    spare,
+    qkv,
+    pre,
+    attend,
+    attend_low,
+    scores_low,
+    scores_grad,
+    stacked,
+    other,
+    grad_mixed,
+):
+    width = state.shape[1]
+    lanes = pl.ds(0, width)
+
+    @pl.when(pl.program_id(0) == 0)
+    def _():
+        sums[...] = jnp.zeros_like(sums)
+        loss[...] = jnp.zeros_like(loss)
+
+    grid = lax.broadcasted_iota(jnp.int32, (GPAD, 1), 0)
+    key = lax.broadcasted_iota(jnp.int32, (1, GPAD), 1)
+    token = vectors[pl.ds(0, 1), lanes]
+    for image in range(BATCH):
+        rows = pl.ds(image * GPAD, GPAD)
+        chosen = (grid == spot_rows[image]).astype(F32)
+        shown = jnp.sum(chosen, axis=1, keepdims=True)
+        placed = dot(chosen.astype(BF16), sent[pl.ds(image * VMAX, VMAX)])
+        seen[rows] = jnp.where(grid < GRID, shown, 1.0)
+        code = turn_code(grid, table[image])
+        state[rows] = jnp.where(shown > 0.5, placed, token) + code
+        bias[pl.ds(image, 1)] = jnp.where(key < GRID, 0.0, MASK_FILL)
+
+    norm_rows(state, normed_one, vectors, LN1_G)
+
+    def project(part):
+        qkv[:, part] = dot(normed_one[...], qkv_w[:, part]).astype(BF16)
+
+    columns_loop(qkv.shape[1], 256, project)
+    attention_forward(
+        BATCH, GPAD, HD, qkv, bias, attend, attend_low, stacked, mixed
+    )
+
+    def output(part):
+        middle[:, part] = state[:, part] + dot(mixed[...], out_w[:, part])
+
+    columns_loop(width, 256, output)
+    norm_rows(middle, normed_two, vectors, LN2_G)
+    feed_forward(normed_two, fc1_w, fc2_w, vectors, middle, pre, active, last)
+    norm_rows(last, normed_last, vectors, LNF_G)
+
+    weight = 1.0 / masked_ref[pl.ds(0, 1), pl.ds(0, 1)]
+
+    def predict(part):
+        value = dot(normed_last[...], head_w[:, part]) + vectors[pl.ds(LAST_B, 1), part]
+        miss = value - dot(pixels[...], bands_w[:, part])
+        index = lax.broadcasted_iota(jnp.int32, (1, GROUP), 1) + part.start
+        low = index < LOWPIX
+        square = miss * miss
+        root = jnp.sqrt(square + 1.0)
+        unseen = 1.0 - seen[...]
+        loss[...] += jnp.sum(jnp.where(low, square, root - 1.0) * unseen).reshape(1, 1)
+        slope = jnp.where(low, 2.0 * miss, miss / root) * (unseen * weight)
+        rounded = slope.astype(BF16)
+        grad_predicted[:, part] = rounded
+        sums[pl.ds(LAST_B, 1), part] += jnp.sum(rounded.astype(F32), axis=0, keepdims=True)
+
+    columns_loop(head_w.shape[1], GROUP, predict)
+
+    def head_back(part):
+        spare[:, part] = dot_nt(grad_predicted[...], head_w[part])
+
+    columns_loop(width, 256, head_back)
+
+    def last_back(rows, value):
+        grad[rows] = value
+        grad_out_low[rows] = value.astype(BF16)
+        sums[pl.ds(FC2_B, 1), lanes] += jnp.sum(value, axis=0, keepdims=True)
+
+    norm_rows_back(last, spare, vectors, sums, LNF_G, last_back)
+    block_backward(
+        BATCH,
+        GPAD,
+        HD,
+        (qkv_w, out_w, fc1_w, fc2_w),
+        vectors,
+        sums,
+        (state, middle, grad, spare, pre, qkv),
+        (grad_out_low, grad_pre, grad_middle_low, grad_mixed, grad_qkv),
+        (attend, attend_low, scores_low, scores_grad, stacked, other),
+    )
+    unseen = 1.0 - seen[...]
+    sums[pl.ds(0, 1), lanes] += jnp.sum(grad[...] * unseen, axis=0, keepdims=True)
+    for image in range(BATCH):
+        chosen = (spot_columns[pl.ds(image * VMAX, VMAX)] == key).astype(F32).astype(BF16)
+        value = dot(chosen, grad[pl.ds(image * GPAD, GPAD)].astype(BF16))
+        grad_sent[pl.ds(image * VMAX, VMAX)] = value.astype(BF16)
+
+
+def block_backward(images, length, heads, weights, vectors, sums, states, lows, scratch):
+    qkv_w, out_w, fc1_w, fc2_w = weights
+    state, middle, grad, spare, pre, qkv = states
+    grad_out_low, grad_pre, grad_middle_low, grad_mixed, grad_qkv = lows
+    attend, attend_low, scores_low, scores_grad, stacked, other = scratch
+    width = state.shape[1]
+    feed_backward(grad_out_low, fc1_w, fc2_w, pre, sums, grad_pre, spare)
+
+    def middle_back(rows, value):
+        total = grad[rows] + value
+        grad[rows] = total
+        grad_middle_low[rows] = total.astype(BF16)
+
+    norm_rows_back(middle, spare, vectors, sums, LN2_G, middle_back)
+
+    def mixed_back(part):
+        grad_mixed[:, part] = dot_nt(grad_middle_low[...], out_w[part]).astype(BF16)
+
+    columns_loop(width, 256, mixed_back)
+    attention_backward(
+        images,
+        length,
+        heads,
+        qkv,
+        grad_mixed,
+        attend,
+        attend_low,
+        scores_low,
+        scores_grad,
+        stacked,
+        other,
+        grad_qkv,
+    )
+
+    def first_back(part):
+        spare[:, part] = dot_nt(grad_qkv[...], qkv_w[part])
+
+    columns_loop(width, 256, first_back)
+
+    def state_back(rows, value):
+        grad[rows] = grad[rows] + value
+
+    norm_rows_back(state, spare, vectors, sums, LN1_G, state_back)
+
+
+def decoder(sent, pixels, spots, tables, masked_tile, vectors, weights):
+    images = spots.shape[0]
+    rows = BATCH * GPAD
+    shown = BATCH * VMAX
+    stack = GROUP // (DD // HD) * GPAD
+    widths = [DD, 3 * DD, DD, DD, DD, FD, FD, DD, DD, padded(HEAD)]
+    whole = lambda array: pl.BlockSpec(array.shape, lambda i: (0,) * array.ndim)
+    by_rows = lambda length, columns: pl.BlockSpec((length, columns), lambda i: (i, 0))
+    bands_w = band_matrix()
+    out_shape = [jax.ShapeDtypeStruct((images * GPAD, columns), BF16) for columns in widths]
+    out_shape.append(jax.ShapeDtypeStruct((images * VMAX, DD), BF16))
+    out_shape.append(jax.ShapeDtypeStruct((VEC_ROWS, VEC_COLS[1]), F32))
+    out_shape.append(jax.ShapeDtypeStruct((1, 1), F32))
+    operands = [masked_tile, bands_w, vectors, *weights]
+    f32 = lambda *shape: pltpu.VMEM(shape, F32)
+    b16 = lambda *shape: pltpu.VMEM(shape, BF16)
+    return pl.pallas_call(
+        decoder_kernel,
+        grid=(images // BATCH,),
+        out_shape=out_shape,
+        in_specs=[
+            by_rows(shown, DD),
+            by_rows(rows, PIX),
+            pl.BlockSpec((BATCH, 1, VMAX), lambda i: (i, 0, 0)),
+            by_rows(shown, 1),
+            pl.BlockSpec((BATCH, TURNS, DD // 2), lambda i: (i, 0, 0)),
+        ]
+        + [whole(operand) for operand in operands],
+        out_specs=[by_rows(rows, columns) for columns in widths]
+        + [by_rows(shown, DD)]
+        + [pl.BlockSpec(shape.shape, lambda i: (0, 0)) for shape in out_shape[-2:]],
+        scratch_shapes=[
+            f32(rows, 1),
+            f32(BATCH, GPAD),
+            f32(rows, DD),
+            f32(rows, DD),
+            f32(rows, DD),
+            f32(rows, DD),
+            f32(rows, DD),
+            b16(rows, 3 * DD),
+            f32(rows, FD),
+            f32(BATCH * DD // GROUP, stack, GPAD),
+            b16(stack, GPAD),
+            b16(stack, GPAD),
+            f32(stack, GPAD),
+            b16(stack, GROUP),
+            b16(stack, GROUP),
+            b16(rows, DD),
+        ],
+        compiler_params=pltpu.CompilerParams(vmem_limit_bytes=62 * 2**20),
+        name="decoder",
+    )(sent, pixels, spots.reshape(images, 1, VMAX), spots.reshape(-1, 1), tables, *operands)
+
+
+def encoder_forward_kernel(
+    pixels,
+    spot_rows,
+    spot_columns,
+    table,
+    vectors,
+    pe_hbm,
+    qkv_hbm,
+    out_hbm,
+    fc1_hbm,
+    fc2_hbm,
+    emb_hbm,
+    sent,
+    patches,
+    state,
+    normed_one,
+    qkv,
+    mixed,
+    middle,
+    normed_two,
+    pre,
+    active,
+    last,
+    normed_last,
+    attend,
+    pe_w,
+    qkv_w,
+    out_w,
+    fc1_w,
+    fc2_w,
+    emb_w,
+    bias,
+    attend_low,
+    stacked,
+    sems,
+):
+    pairs = [
+        (pe_hbm, pe_w),
+        (qkv_hbm, qkv_w),
+        (out_hbm, out_w),
+        (fc1_hbm, fc1_w),
+        (fc2_hbm, fc2_w),
+        (emb_hbm, emb_w),
+    ]
+    copies = [pltpu.make_async_copy(*pair, sems.at[n]) for n, pair in enumerate(pairs)]
+    for copy in copies:
+        copy.start()
+    images = spot_rows.shape[0]
+    key = lax.broadcasted_iota(jnp.int32, (1, GPAD), 1)
+    for image in range(images):
+        rows = pl.ds(image * VMAX, VMAX)
+        place = spot_columns[rows]
+        chosen = (place == key).astype(F32).astype(BF16)
+        patches[rows] = dot(chosen, pixels[pl.ds(image * GPAD, GPAD)]).astype(BF16)
+        code = turn_code(jnp.maximum(place, 0), table[image])
+        state[rows] = code + vectors[pl.ds(0, 1), pl.ds(0, DE)]
+        bias[pl.ds(image, 1)] = jnp.where(spot_rows[image] < 0, MASK_FILL, 0.0)
+    copies[0].wait()
+
+    def embed(part):
+        state[:, part] += dot(patches[...], pe_w[:, part])
+
+    columns_loop(DE, 256, embed)
+    norm_rows(state, normed_one, vectors, LN1_G)
+    copies[1].wait()
+
+    def project(part):
+        qkv[:, part] = dot(normed_one[...], qkv_w[:, part]).astype(BF16)
+
+    columns_loop(3 * DE, 256, project)
+    attention_forward(images, VMAX, HE, qkv, bias, attend, attend_low, stacked, mixed)
+    copies[2].wait()
+
+    def output(part):
+        middle[:, part] = state[:, part] + dot(mixed[...], out_w[:, part])
+
+    columns_loop(DE, 256, output)
+    norm_rows(middle, normed_two, vectors, LN2_G)
+    copies[3].wait()
+    copies[4].wait()
+    feed_forward(normed_two, fc1_w, fc2_w, vectors, middle, pre, active, last)
+    norm_rows(last, normed_last, vectors, LNF_G)
+    copies[5].wait()
+    value = dot(normed_last[...], emb_w[...]) + vectors[pl.ds(LAST_B, 1), pl.ds(0, DD)]
+    sent[...] = value.astype(BF16)
+
+
+def encoder_forward(pixels, spots, tables, vectors, weights):
+    images = spots.shape[0]
+    rows = images * VMAX
+    stack = GROUP // (DE // HE) * VMAX
+    anywhere = pl.BlockSpec(memory_space=pl.ANY)
+    vmem = pl.BlockSpec(memory_space=pltpu.VMEM)
+    kept = [
+        (DD, BF16),
+        (PIX, BF16),
+        (DE, F32),
+        (DE, BF16),
+        (3 * DE, BF16),
+        (DE, BF16),
+        (DE, F32),
+        (DE, BF16),
+        (FE, F32),
+        (FE, BF16),
+        (DE, F32),
+        (DE, BF16),
+    ]
+    out_shape = [jax.ShapeDtypeStruct((rows, columns), kind) for columns, kind in kept]
+    out_shape.append(jax.ShapeDtypeStruct((images * DE // GROUP, stack, VMAX), F32))
+    return pl.pallas_call(
+        encoder_forward_kernel,
+        out_shape=out_shape,
+        in_specs=[vmem] * 5 + [anywhere] * 6,
+        out_specs=[vmem] * len(out_shape),
+        scratch_shapes=[pltpu.VMEM(weight.shape, BF16) for weight in weights]
+        + [
+            pltpu.VMEM((images, VMAX), F32),
+            pltpu.VMEM((stack, VMAX), BF16),
+            pltpu.VMEM((stack, GROUP), BF16),
+            pltpu.SemaphoreType.DMA((6,)),
+        ],
+        compiler_params=pltpu.CompilerParams(vmem_limit_bytes=60 * 2**20),
+        name="encoder_forward",
+    )(pixels, spots.reshape(images, 1, VMAX), spots.reshape(-1, 1), tables, vectors, *weights)
+
+
+def encoder_backward_kernel(
+    grad_sent,
+    vectors,
+    state,
+    qkv,
+    middle,
+    pre,
+    last,
+    attend,
+    qkv_hbm,
+    out_hbm,
+    fc1_hbm,
+    fc2_hbm,
+    emb_hbm,
+    grad_state_low,
+    grad_qkv,
+    grad_middle_low,
+    grad_pre,
+    grad_out_low,
+    sums,
+    qkv_w,
+    out_w,
+    fc1_w,
+    fc2_w,
+    emb_w,
+    grad,
+    spare,
+    grad_mixed,
+    attend_low,
+    scores_low,
+    scores_grad,
+    stacked,
+    other,
+    sems,
+):
+    pairs = [
+        (emb_hbm, emb_w),
+        (fc2_hbm, fc2_w),
+        (fc1_hbm, fc1_w),
+        (out_hbm, out_w),
+        (qkv_hbm, qkv_w),
+    ]
+    copies = [pltpu.make_async_copy(*pair, sems.at[n]) for n, pair in enumerate(pairs)]
+    for copy in copies:
+        copy.start()
+    lanes = pl.ds(0, DE)
+    sums[...] = jnp.zeros_like(sums)
+    summed = jnp.sum(grad_sent[...].astype(F32), axis=0, keepdims=True)
+    sums[pl.ds(LAST_B, 1), pl.ds(0, DD)] = summed
+    copies[0].wait()
+
+    def sent_back(part):
+        spare[:, part] = dot_nt(grad_sent[...], emb_w[part])
+
+    columns_loop(DE, 256, sent_back)
+
+    def last_back(rows, value):
+        grad[rows] = value
+        grad_out_low[rows] = value.astype(BF16)
+        sums[pl.ds(FC2_B, 1), lanes] += jnp.sum(value, axis=0, keepdims=True)
+
+    norm_rows_back(last, spare, vectors, sums, LNF_G, last_back)
+    for copy in copies[1:]:
+        copy.wait()
+    block_backward(
+        state.shape[0] // VMAX,
+        VMAX,
+        HE,
+        (qkv_w, out_w, fc1_w, fc2_w),
+        vectors,
+        sums,
+        (state, middle, grad, spare, pre, qkv),
+        (grad_out_low, grad_pre, grad_middle_low, grad_mixed, grad_qkv),
+        (attend, attend_low, scores_low, scores_grad, stacked, other),
+    )
+
+    def first(rows):
+        value = grad[rows]
+        sums[pl.ds(0, 1), lanes] += jnp.sum(value, axis=0, keepdims=True)
+        grad_state_low[rows] = value.astype(BF16)
+
+    blocks(grad.shape[0], row_step(grad.shape[0]), first)
+
+
+def encoder_backward(grad_sent, vectors, kept, weights):
+    state, qkv, middle, pre, last, attend = kept
+    rows = state.shape[0]
+    stack = attend.shape[1]
+    anywhere = pl.BlockSpec(memory_space=pl.ANY)
+    vmem = pl.BlockSpec(memory_space=pltpu.VMEM)
+    out_shape = [
+        jax.ShapeDtypeStruct((rows, columns), BF16) for columns in (DE, 3 * DE, DE, FE, DE)
+    ]
+    out_shape.append(jax.ShapeDtypeStruct((VEC_ROWS, VEC_COLS[0]), F32))
+    f32 = lambda *shape: pltpu.VMEM(shape, F32)
+    b16 = lambda *shape: pltpu.VMEM(shape, BF16)
+    return pl.pallas_call(
+        encoder_backward_kernel,
+        out_shape=out_shape,
+        in_specs=[vmem] * 8 + [anywhere] * 5,
+        out_specs=[vmem] * len(out_shape),
+        scratch_shapes=[pltpu.VMEM(weight.shape, BF16) for weight in weights]
+        + [
+            f32(rows, DE),
+            f32(rows, DE),
+            b16(rows, DE),
+            b16(stack, VMAX),
+            b16(stack, VMAX),
+            f32(stack, VMAX),
+            b16(stack, GROUP),
+            b16(stack, GROUP),
+            pltpu.SemaphoreType.DMA((5,)),
+        ],
+        compiler_params=pltpu.CompilerParams(vmem_limit_bytes=60 * 2**20),
+        name="encoder_backward",
+    )(grad_sent, vectors, state, qkv, middle, pre, last, attend, *weights)
+
+
+def band_matrix():
+    ids = jnp.arange(PIX, dtype=jnp.int32)
+    coarse = (ids // (3 * PSIDE) // 2 * (PSIDE // 2) + ids // 3 % PSIDE // 2) * 3 + ids % 3
+    low = jnp.where(coarse[:, None] == jnp.arange(LOWPIX, dtype=jnp.int32)[None], 0.25, 0.0)
+    same = jnp.where(coarse[:, None] == coarse[None], 0.25, 0.0)
+    high = jnp.where(ids[:, None] == ids[None], 1.0, 0.0) - same
+    rest = jnp.zeros((PIX, padded(HEAD) - HEAD), F32)
+    return jnp.concatenate([low, high, rest], axis=1).astype(BF16)
+
+
+def turn_table(scales, width):
     quarter = width // 4
     frequency = jnp.exp(jnp.arange(quarter, dtype=F32) * (-math.log(10000.0) / quarter))
-    row_angle = ((position // GSIDE).astype(F32) * scales)[..., None] * frequency
-    col_angle = ((position % GSIDE).astype(F32) * scales)[..., None] * frequency
-    return jnp.concatenate(
-        [jnp.sin(row_angle), jnp.cos(row_angle), jnp.sin(col_angle), jnp.cos(col_angle)], axis=-1
+    angle = (jnp.arange(TURNS, dtype=F32)[None] * scales[:, None])[..., None] * frequency
+    return jnp.concatenate([jnp.sin(angle), jnp.cos(angle)], axis=-1)
+
+
+def forward_backward(parts, pixels, index_rows, counts, scales, masked_tile):
+    pe_w, qkv_w, fc1_w, emb_w, out_w, fc2_w = parts[:6]
+    dec_weights = parts[6:11]
+    enc_vectors, dec_vectors = parts[11:]
+    images = counts.shape[0]
+    valid = jnp.arange(VMAX, dtype=jnp.int32)[None, :] < counts[:, None]
+    spots = jnp.where(valid, index_rows, -1)
+    pixels = jnp.pad(pixels.reshape(images, GRID, PIX), ((0, 0), (0, GPAD - GRID), (0, 0)))
+    pixels = pixels.reshape(images * GPAD, PIX)
+    (
+        sent,
+        patches,
+        state,
+        normed_one,
+        qkv,
+        mixed,
+        middle,
+        normed_two,
+        pre,
+        active,
+        last,
+        normed_last,
+        attend,
+    ) = encoder_forward(
+        pixels,
+        spots,
+        turn_table(scales, DE),
+        enc_vectors,
+        [pe_w, qkv_w, out_w, fc1_w, fc2_w, emb_w],
     )
-
-
-def bands(pixel_rows):
-    pixel_ids = jnp.arange(PIX, dtype=jnp.int32)
-    coarse = (
-        pixel_ids // (3 * PSIDE) // 2 * (PSIDE // 2) + pixel_ids // 3 % PSIDE // 2
-    ) * 3 + pixel_ids % 3
-    pool_table = (coarse[:, None] == jnp.arange(LOWPIX, dtype=jnp.int32)[None, :]).astype(F32)
-    low_band = jnp.dot(pixel_rows, pool_table, precision=HIGHEST) * 0.25
-    high_band = pixel_rows - jnp.dot(low_band, pool_table.T, precision=HIGHEST)
-    return (low_band, high_band)
-
-
-def linear(left, right):
-    return jnp.einsum("...k,kn->...n", left, right, preferred_element_type=F32)
-
-
-def input_grad(grad_rows, right):
-    return jnp.einsum("...n,kn->...k", grad_rows, right, preferred_element_type=F32)
-
-
-def norm_forward(state, gain, shift):
-    centered = state - jnp.mean(state, axis=-1, keepdims=True)
-    inverse = lax.rsqrt(jnp.mean(centered * centered, axis=-1, keepdims=True) + NORM_EPS)
-    unit_rows = centered * inverse
-    return (unit_rows * gain.astype(F32) + shift.astype(F32), unit_rows, inverse)
-
-
-def norm_backward(grad_out, unit_rows, inverse, gain):
-    grad_unit = grad_out * gain.astype(F32)
-    grad_in = inverse * (
-        grad_unit
-        - jnp.mean(grad_unit, axis=-1, keepdims=True)
-        - unit_rows * jnp.mean(grad_unit * unit_rows, axis=-1, keepdims=True)
+    *dec_factors, grad_sent, dec_sums, loss = decoder(
+        sent, pixels, spots, turn_table(scales, DD), masked_tile, dec_vectors, dec_weights
     )
-    return (grad_in, jnp.sum(grad_out * unit_rows, axis=(0, 1)), jnp.sum(grad_out, axis=(0, 1)))
-
-
-def attention_scores(query_part, key_part, bias):
-    head_dim = query_part.shape[-1]
-    return (
-        jnp.einsum("blhd,bmhd->bhlm", query_part, key_part, preferred_element_type=F32)
-        * head_dim ** (-0.5)
-        + bias
+    grad_state, grad_qkv, grad_middle, grad_pre, grad_out, enc_sums = encoder_backward(
+        grad_sent,
+        enc_vectors,
+        [state, qkv, middle, pre, last, attend],
+        [qkv_w, out_w, fc1_w, fc2_w, emb_w],
     )
-
-
-def gelu_exact(values):
-    return jax.nn.gelu(values, approximate=False)
-
-
-def block_forward(state, weights, heads, bias):
-    batch, length, width = state.shape
-    normed_one, unit_one, inverse_one = norm_forward(state, weights.ln1_g, weights.ln1_b)
-    normed_one = normed_one.astype(BF16)
-    qkv = (
-        linear(normed_one, weights.qkv_w)
-        .astype(BF16)
-        .reshape(batch, length, 3, heads, width // heads)
-    )
-    scores = attention_scores(qkv[:, :, 0], qkv[:, :, 1], bias)
-    row_max = jnp.max(scores, axis=-1, keepdims=True)
-    shifted = jnp.exp(scores - row_max)
-    totals = jnp.sum(shifted, axis=-1, keepdims=True)
-    attend = (shifted / totals).astype(BF16)
-    logsum = row_max + jnp.log(totals)
-    mixed = jnp.einsum("bhlm,bmhd->blhd", attend, qkv[:, :, 2], preferred_element_type=F32)
-    mixed = mixed.astype(BF16).reshape(batch, length, width)
-    middle = state + linear(mixed, weights.out_w)
-    normed_two, unit_two, inverse_two = norm_forward(middle, weights.ln2_g, weights.ln2_b)
-    normed_two = normed_two.astype(BF16)
-    pre_act = linear(normed_two, weights.fc1_w) + weights.fc1_b.astype(F32)
-    active = gelu_exact(pre_act).astype(BF16)
-    output = middle + linear(active, weights.fc2_w) + weights.fc2_b.astype(F32)
-    kept = Bag(
-        normed_one=normed_one,
-        unit_one=unit_one,
-        inverse_one=inverse_one,
-        qkv=qkv,
-        logsum=logsum,
-        mixed=mixed,
-        unit_two=unit_two,
-        inverse_two=inverse_two,
-        normed_two=normed_two,
-        active=active,
-        pre_act=pre_act,
-    )
-    return (output, kept)
-
-
-def block_backward(grad_out, kept, weights, heads, bias):
-    batch, length, width = grad_out.shape
-    grads = Bag()
-    pairs = Bag()
-    grad_low = grad_out.astype(BF16)
-    pairs.fc2_w = (kept.active, grad_low)
-    grads.fc2_b = jnp.sum(grad_out, axis=(0, 1))
-    _, gelu_back = jax.vjp(gelu_exact, kept.pre_act)
-    grad_pre = gelu_back(input_grad(grad_low, weights.fc2_w))[0]
-    grads.fc1_b = jnp.sum(grad_pre, axis=(0, 1))
-    grad_pre_low = grad_pre.astype(BF16)
-    pairs.fc1_w = (kept.normed_two, grad_pre_low)
-    grad_norm_in, grads.ln2_g, grads.ln2_b = norm_backward(
-        input_grad(grad_pre_low, weights.fc1_w),
-        kept.unit_two,
-        kept.inverse_two,
-        weights.ln2_g,
-    )
-    grad_mid = grad_out + grad_norm_in
-    grad_mid_low = grad_mid.astype(BF16)
-    pairs.out_w = (kept.mixed, grad_mid_low)
-    grad_mixed = (
-        input_grad(grad_mid_low, weights.out_w)
-        .astype(BF16)
-        .reshape(batch, length, heads, width // heads)
-    )
-    qkv = kept.qkv
-    query_part, key_part, value_part = (qkv[:, :, 0], qkv[:, :, 1], qkv[:, :, 2])
-    attend = jnp.exp(attention_scores(query_part, key_part, bias) - kept.logsum)
-    grad_value = jnp.einsum(
-        "bhlm,blhd->bmhd", attend.astype(BF16), grad_mixed, preferred_element_type=F32
-    )
-    grad_attend = jnp.einsum("blhd,bmhd->bhlm", grad_mixed, value_part, preferred_element_type=F32)
-    grad_scores = (
-        attend * (grad_attend - jnp.sum(grad_attend * attend, axis=-1, keepdims=True))
-    ).astype(BF16)
-    score_scale = (width // heads) ** (-0.5)
-    grad_query = (
-        jnp.einsum("bhlm,bmhd->blhd", grad_scores, key_part, preferred_element_type=F32)
-        * score_scale
-    )
-    grad_key = (
-        jnp.einsum("bhlm,blhd->bmhd", grad_scores, query_part, preferred_element_type=F32)
-        * score_scale
-    )
-    grad_qkv = (
-        jnp.stack([grad_query, grad_key, grad_value], axis=2)
-        .reshape(batch, length, 3 * width)
-        .astype(BF16)
-    )
-    pairs.qkv_w = (kept.normed_one, grad_qkv)
-    grad_norm_in, grads.ln1_g, grads.ln1_b = norm_backward(
-        input_grad(grad_qkv, weights.qkv_w),
-        kept.unit_one,
-        kept.inverse_one,
-        weights.ln1_g,
-    )
-    return (grad_mid + grad_norm_in, grads, pairs)
-
-
-def forward_backward(enc, dec, pixels, index_rows, counts, scales, masked_total):
-    images = counts.shape[0]
-    slots = jnp.arange(VMAX, dtype=jnp.int32)
-    valid = slots[None, :] < counts[:, None]
-    position = jnp.where(valid, index_rows, 0)
-    pixel_images = jnp.pad(pixels.reshape(images, GRID, PIX), ((0, 0), (0, GPAD - GRID), (0, 0)))
-    grid = jnp.arange(GPAD, dtype=jnp.int32)
-    chosen = ((position[:, :, None] == grid[None, None, :]) & valid[:, :, None]).astype(BF16)
-    patches = jnp.einsum("ivg,igp->ivp", chosen, pixel_images, preferred_element_type=F32)
-    patches = patches.astype(BF16)
-    enc_bias = jnp.where(valid, 0.0, MASK_FILL)[:, None, None, :]
-    state = (
-        linear(patches, enc.pe_w)
-        + enc.pe_b.astype(F32)
-        + position_code(position, scales[:, None], DE)
-    )
-    state, enc_kept = block_forward(state, enc, HE, enc_bias)
-    enc_normed, enc_unit, enc_inverse = norm_forward(state, enc.lnf_g, enc.lnf_b)
-    enc_normed = enc_normed.astype(BF16)
-    sent = (linear(enc_normed, enc.emb_w) + enc.emb_b.astype(F32)).astype(BF16)
-
-    placed = jnp.einsum("ivg,ivd->igd", chosen, sent, preferred_element_type=F32)
-    seen = jnp.sum(chosen.astype(F32), axis=1)
-    dec_bias = jnp.where(grid < GRID, 0.0, MASK_FILL)[None, None, None, :]
-    state = jnp.where(
-        seen[:, :, None] > 0.5, placed, dec.mask_tok.astype(F32)
-    ) + position_code(jnp.broadcast_to(grid[None], (images, GPAD)), scales[:, None], DD)
-    state, dec_kept = block_forward(state, dec, HD, dec_bias)
-    normed, unit_rows, inverse = norm_forward(state, dec.lnf_g, dec.lnf_b)
-    normed = normed.astype(BF16)
-    predicted = linear(normed, dec.head_w[:, :HEAD]) + dec.head_b[:HEAD].astype(F32)
-    low_band, high_band = bands(pixel_images.reshape(-1, PIX).astype(F32))
-    low_band = low_band.reshape(images, GPAD, -1)
-    high_band = high_band.reshape(images, GPAD, -1)
-    miss_low = predicted[..., :LOWPIX] - low_band
-    miss_high = predicted[..., LOWPIX:] - high_band
-    unseen = jnp.where(grid[None] < GRID, 1.0 - seen, 0.0)
-    per_patch = jnp.sum(miss_low * miss_low, axis=-1) + jnp.sum(
-        jnp.sqrt(miss_high * miss_high + 1.0) - 1.0, axis=-1
-    )
-    loss_local = jnp.sum(per_patch * unseen)
-    row_weight = unseen / masked_total
-    grad_pred = (
-        jnp.concatenate(
-            [2.0 * miss_low, miss_high * lax.rsqrt(miss_high * miss_high + 1.0)], axis=-1
-        )
-        * row_weight[:, :, None]
-    )
-    grad_low = jnp.pad(grad_pred, ((0, 0), (0, 0), (0, padded(HEAD) - HEAD))).astype(BF16)
-    dec_pairs = Bag(head_w=(normed, grad_low))
-    dec_grads = Bag(head_b=jnp.sum(grad_low.astype(F32), axis=(0, 1)))
-    grad_state, dec_grads.lnf_g, dec_grads.lnf_b = norm_backward(
-        input_grad(grad_low, dec.head_w), unit_rows, inverse, dec.lnf_g
-    )
-    grad_state, block_grads, block_pairs = block_backward(grad_state, dec_kept, dec, HD, dec_bias)
-    vars(dec_grads).update(vars(block_grads))
-    vars(dec_pairs).update(vars(block_pairs))
-    dec_grads.mask_tok = jnp.sum(grad_state * unseen[:, :, None], axis=(0, 1))
-    grad_sent = jnp.einsum(
-        "ivg,igd->ivd", chosen, grad_state.astype(BF16), preferred_element_type=F32
-    ).astype(BF16)
-
-    enc_pairs = Bag(emb_w=(enc_normed, grad_sent))
-    enc_grads = Bag(emb_b=jnp.sum(grad_sent.astype(F32), axis=(0, 1)))
-    grad_state, enc_grads.lnf_g, enc_grads.lnf_b = norm_backward(
-        input_grad(grad_sent, enc.emb_w), enc_unit, enc_inverse, enc.lnf_g
-    )
-    grad_state, block_grads, block_pairs = block_backward(grad_state, enc_kept, enc, HE, enc_bias)
-    vars(enc_grads).update(vars(block_grads))
-    vars(enc_pairs).update(vars(block_pairs))
-    enc_pairs.pe_w = (patches, grad_state.astype(BF16))
-    enc_grads.pe_b = jnp.sum(grad_state, axis=(0, 1))
-    return loss_local, enc_grads, enc_pairs, dec_grads, dec_pairs
-
-
-def vector_rows(vectors, columns):
-    rows = [jnp.pad(vector, (0, columns - vector.shape[0])) for vector in vectors]
-    rows += [jnp.zeros((columns,), F32)] * (VEC_ROWS - len(rows))
-    return jnp.stack(rows)
-
-
-def gradient_row(rows, enc_grads, enc_pairs, dec_grads, dec_pairs):
-    e, d = enc_grads, dec_grads
-    enc_vectors = vector_rows(
-        [e.pe_b, e.ln1_g, e.ln1_b, e.ln2_g, e.ln2_b, e.fc1_b, e.fc2_b, e.lnf_g, e.lnf_b, e.emb_b],
-        VEC_COLS[0],
-    )
-    dec_vectors = vector_rows(
-        [d.mask_tok, d.ln1_g, d.ln1_b, d.ln2_g, d.ln2_b]
-        + [d.fc1_b, d.fc2_b, d.lnf_g, d.lnf_b, d.head_b],
-        VEC_COLS[1],
-    )
-    e, d = enc_pairs, dec_pairs
-    pairs = [e.pe_w, e.qkv_w, e.fc1_w, e.emb_w, e.out_w, e.fc2_w]
-    pairs += [d.qkv_w, d.out_w, d.fc1_w, d.fc2_w, d.head_w]
-    factors = [factor.reshape(-1, factor.shape[-1]) for pair in pairs for factor in pair]
-    return flat_gradient(rows, factors, enc_vectors, dec_vectors)
-
-
-def bags(parts):
-    enc, dec = Bag(), Bag()
-    enc.pe_w, enc.qkv_w, enc.fc1_w, enc.emb_w, enc.out_w, enc.fc2_w = parts[:6]
-    dec.qkv_w, dec.out_w, dec.fc1_w, dec.fc2_w, dec.head_w = parts[6:11]
-    e, d = parts[11:]
-    enc.pe_b, enc.ln1_g, enc.ln1_b, enc.ln2_g, enc.ln2_b = [e[n, :DE] for n in range(5)]
-    enc.fc1_b = e[5]
-    enc.fc2_b, enc.lnf_g, enc.lnf_b = [e[n, :DE] for n in range(6, 9)]
-    enc.emb_b = e[9, :DD]
-    dec.mask_tok, dec.ln1_g, dec.ln1_b, dec.ln2_g, dec.ln2_b = [d[n, :DD] for n in range(5)]
-    dec.fc1_b = d[5]
-    dec.fc2_b, dec.lnf_g, dec.lnf_b = [d[n, :DD] for n in range(6, 9)]
-    dec.head_b = d[9, : padded(HEAD)]
-    return enc, dec
+    factors = [patches, grad_state, normed_one, grad_qkv, normed_two, grad_pre]
+    factors += [normed_last, grad_sent, mixed, grad_middle, active, grad_out]
+    return factors + dec_factors, enc_sums, dec_sums, loss[0, 0]
 
 
 def clip_scale(squares):
@@ -1431,12 +1901,11 @@
     if special:
         shards = [a.reshape(-1, 4, LANES) for a in (params, first_moment, second_moment, average)]
         copies, masked_tile = gather_rows(shards[0], jnp.full((8, LANES), masked))
-        masked_total = masked_tile[0, 0]
     else:
         copies = lax.all_gather(params.astype(BF16).reshape(-1, LANES), "dp", axis=0, tiled=True)
         copies = lax.all_gather(copies, "grp", axis=0, tiled=True)
-        masked_total = lax.psum(masked, "dp")
-    enc, dec = bags(weight_matrices(copies.reshape(-1, LANES)))
+        masked_tile = jnp.full((8, LANES), lax.psum(masked, "dp"))
+    parts = weight_matrices(copies.reshape(-1, LANES))
 
     half = visible_count.shape[0] // 2
     core = lax.axis_index("grp")
@@ -1445,16 +1914,15 @@
         return lax.dynamic_slice_in_dim(array, core * count, count, 0)
 
     scales = 0.5 + 0.25 * mine(gsd_id, half).astype(F32)
-    loss_local, enc_grads, enc_pairs, dec_grads, dec_pairs = forward_backward(
-        enc,
-        dec,
+    factors, enc_sums, dec_sums, loss_local = forward_backward(
+        parts,
         mine(pixels, half * GRID),
         mine(visible_index, half),
         mine(visible_count, half),
         scales,
-        masked_total,
+        masked_tile,
     )
-    gradient = gradient_row(chips * rows, enc_grads, enc_pairs, dec_grads, dec_pairs)
+    gradient = flat_gradient(chips * rows, factors, enc_sums, dec_sums)
     if special:
         owned, sums = scatter_sums(
             gradient.reshape(chips, rows // 4, 4, LANES), jnp.full((8, LANES), loss_local)
@@ -1468,7 +1936,7 @@
         owned = owned.reshape(params.shape)
         squares, loss_sum = lax.psum((jnp.sum(owned * owned), loss_local), ("grp", "dp"))
         outs = update_values(owned, clip_scale(squares), params, first_moment, second_moment, average)
-    return (*outs, loss_sum, masked_total, jnp.sqrt(squares))
+    return (*outs, loss_sum, masked_tile[0, 0], jnp.sqrt(squares))
 
 
 def solution(mesh):

time: 815 us -> 718 us (0.88)
  Pallas kernels: 543 us -> 693 us
  matrix products: 108 us -> 0 us
  local copies, waits for them, and re-layouts: 81.2 us -> 8.6 us
  other arithmetic: 69.6 us -> 8.57 us
    pallas_call x0 -> x3, Pallas kernels: none -> 151 us  [the longest x1 79.8 us: decoder(): pl.pallas_call(decoder_kernel, grid=(images // BATCH,), out_shape=out_sha...]
    dot_general x37 -> x0, matrix products: 108 us -> none  [the longest x10 36 us: input_grad(): jnp.einsum('...n,kn->...k', grad_rows, right, preferred_element_type=F32)]
    convert_element_type x16 -> x0, other arithmetic: 41.2 us -> none  [the longest x2 26.6 us: block_forward(): active = gelu_exact(pre_act).astype(BF16)]
    convert_element_type x11 -> x0, local copies, waits for them, and re-layouts: 31.7 us -> none  [the longest x7 24.8 us: block_backward(): grad_qkv = jnp.stack([grad_query, grad_key, grad_value], axis=2).reshape(...]
    unnamed x173 -> x2, local copies, waits for them, and re-layouts: 15.3 us -> 0.01 us
    slice x8 -> x1, local copies, waits for them, and re-layouts: 12.6 us -> 1.18 us  [body(): return (*outs, loss_sum, masked_tile[0, 0], jnp.sqrt(squares))]
    reduce_sum x15 -> x0, other arithmetic: 9.93 us -> none  [the longest x2 3.55 us: block_forward(): totals = jnp.sum(shifted, axis=-1, keepdims=True)]
    another operation x9 -> x0, local copies, waits for them, and re-layouts: 8.52 us -> none  [the longest x3 5.52 us: gradient_row(): factor.reshape(-1, factor.shape[-1])]
where the time goes in v3:
time: 718 us; the launch traced here: 714 us
  Pallas kernels  693 us (97%)
  local copies, waits for them, and re-layouts  8.6 us (1%)
  other arithmetic  8.57 us (1%)
    pallas_call x1, Pallas kernels, scatter_sums(): pl.pallas_call(scatter_kernel, out_shape=(jax.ShapeDtypeStruct((units, 4,...  289 us
    pallas_call x1, Pallas kernels, gather_rows(): pl.pallas_call(gather_kernel, out_shape=(jax.ShapeDtypeStruct((2, 16, uni...  149 us
    pallas_call x1, Pallas kernels, decoder(): pl.pallas_call(decoder_kernel, grid=(images // BATCH,), out_shape=out_sha...  79.8 us
    pallas_call x1, Pallas kernels, flat_gradient(): pl.pallas_call(functools.partial(product_kernel, rows, shapes), out_shape...  48 us
    pallas_call x1, Pallas kernels, weight_matrices(): pl.pallas_call(functools.partial(matrix_kernel, rows), out_shape=[jax.Sha...  44.8 us
    pallas_call x1, Pallas kernels, encoder_backward(): pl.pallas_call(encoder_backward_kernel, out_shape=out_shape, in_specs=[vm...  37.1 us
    pallas_call x1, Pallas kernels, encoder_forward(): pl.pallas_call(encoder_forward_kernel, out_shape=out_shape, in_specs=[vme...  33.6 us

profile of v3, /device:TPU:0, one launch (start us, length us, event | category | flops | bytes accessed | tf_op | source)
XLA Modules:
  0.0 713.9 jit_solution(9772495497915231894)
XLA Ops:
  0.6 0.7 multiply_add_fusion
  1.4 0.1 iota_multiply_fusion
  1.5 0.3 multiply_sine_fusion
  1.8 0.7 pad_maximum_fusion.table
  2.4 0.7 dynamic_slice.13
  3.2 0.8 dynamic-slice_select_fusion
  3.9 0.0 copy-start
  3.9 0.8 reshape.248.spot_columns
  4.7 1.3 subtract_reduce_fusion
  6.7 0.6 broadcast_in_dim.50.masked_ref
  7.3 149.0 %gather_rows.1 = (bf16[2,16,1085,4,128]{4,3,2,1,0:T(4,128)(2,1)}, f32[8,128]{1,0:T(8,128)}) custom-call(f32[1085,4,128]{2,1,0:T(4,128)} %bitcast.20, f32[8,128]{1,0:T(8,128)} %broadcast_in_dim.50.masked_ref), custom_call_target="tpu_custom_call" | custom-call | tf_op jit(solution)/shard_map/gather_rows/pallas_call | solution.py:326
  156.3 44.8 %weight_matrices.1 = (bf16[768,1024]{1,0:T(8,128)(2,1)}, bf16[1024,3072]{1,0:T(8,128)(2,1)}, bf16[1024,4096]{1,0:T(8,128)(2,1)}, bf16[1024,512]{1,0:T(8,128)(2,1...) custom-call(bf16[138880,128]{1,0:T(8,128)(2,1)} %bitcast.17), custom_call_target="tpu_custom_call" | custom-call | tf_op jit(solution)/shard_map/weight_matrices/pallas_call | solution.py:806
  201.1 0.0 copy-done
  201.1 1.4 constant_dynamic-slice_fusion
  202.5 0.3 reshape.233
  202.8 1.1 pad.4
  203.9 33.6 %encoder_forward.1 = (bf16[256,512]{1,0:T(8,128)(2,1)}, bf16[256,768]{1,0:T(8,128)(2,1)}, f32[256,1024]{1,0:T(8,128)}, bf16[256,1024]{1,0:T(8,128)(2,1)}, bf16[2...) custom-call(bf16[832,768]{1,0:T(8,128)(2,1)} %bitcast.18, ...), custom_call_target="tpu_custom_call" | custom-call | tf_op jit(solution)/shard_map/encoder_forward/pallas_call | solution.py:1694
  237.6 0.2 multiply_sine_fusion.1
  237.8 0.6 pad_maximum_fusion.1.table
  238.4 0.4 subtract_convert_fusion
  238.8 0.2 select_convert_fusion
  239.0 0.1 pad.7.clone
  239.1 2.0 maximum_maximum_fusion.bands_w
  241.1 79.8 %decoder.1 = (bf16[832,512]{1,0:T(8,128)(2,1)}, bf16[832,1536]{1,0:T(8,128)(2,1)}, bf16[832,512]{1,0:T(8,128)(2,1)}, bf16[832,512]{1,0:T(8,128)(2,1)}, bf16[832,...) custom-call(bf16[256,512]{1,0:T(8,128)(2,1)} %get-tuple-element.69.s, ...), custom_call_target="tpu_custom_call" | custom-call | tf_op jit(solution)/shard_map/decoder/pallas_call | solution.py:1547
  320.9 37.1 %encoder_backward.1 = (bf16[256,1024]{1,0:T(8,128)(2,1)}, bf16[256,3072]{1,0:T(8,128)(2,1)}, bf16[256,1024]{1,0:T(8,128)(2,1)}, bf16[256,4096]{1,0:T(8,128)(2,1)...) custom-call(bf16[256,512]{1,0:T(8,128)(2,1)} %get-tuple-element.77.grad_sent.refs_7_, ...), custom_call_target="tpu_custom_call" | custom-call | tf_op jit(solution)/shard_map/encoder_backward/pallas_call | solution.py:1807
  358.0 48.0 %flat_gradient.1 = f32[69440,128]{1,0:T(8,128)} custom-call(bf16[256,768]{1,0:T(8,128)(2,1)} %get-tuple-element.68.refs_0_, bf16[256,1024]{1,0:T(8,128)(2,1)} %get-tuple-element.84.refs_1_, bf16[256,1024]{1,0:T(8,128)(2,1)} %get-tuple-element.85.refs_2_, bf16[256,3072]{1,0:T(8,128)(2,1)} %get-tuple-element.86.refs_3_, ...), custom_call_target="tpu_custom_call" | custom-call | tf_op jit(solution)/shard_map/flat_gradient/pallas_call | solution.py:1119
  406.1 1.2 broadcast_in_dim.57.loss_ref
  407.3 289.1 %scatter_sums.1 = (f32[1085,4,128]{2,1,0:T(4,128)}, f32[8,128]{1,0:T(8,128)}) custom-call(f32[16,1085,4,128]{3,2,1,0:T(4,128)} %bitcast.16, f32[8,128]{1,0:T(8,128)} %broadcast_in_dim.57.loss_ref), custom_call_target="tpu_custom_call" | custom-call | tf_op jit(solution)/shard_map/scatter_sums/pallas_call | solution.py:556
  696.4 1.3 slice_reduce_fusion
  698.5 11.8 %update.1 = (f32[1085,4,128]{2,1,0:T(4,128)}, f32[1085,4,128]{2,1,0:T(4,128)}, f32[1085,4,128]{2,1,0:T(4,128)}, f32[1085,4,128]{2,1,0:T(4,128)}) custom-call(f32[1]{0:T(128)} %bitcast.6.scale_ref, f32[1085,4,128]{2,1,0:T(4,128)} %get-tuple-element.108.refs_0_, f32[1085,4,128]{2,1,0:T(4,128)} %bitcast.21, f32[1085,4,128]{2,1,0:T(4,128)} %bitcast.22, ...), custom_call_target="tpu_custom_call" | custom-call | tf_op jit(solution)/shard_map/update/pallas_call | solution.py:602
  710.2 1.2 slice.10
  711.4 1.2 slice.11
  (4 shorter events, 0.0 us)
Async XLA Ops:
  3.9 197.2 %copy-start = (s32[4,64]{1,0:T(4,128)}, s32[4,64]{1,0:T(4,128)S(1)}, u32[]{:S(2)}) copy-start(s32[4,64]{1,0:T(4,128)S(1)} %dynamic-slice_select_fusion) | copy-start | bytes 3076

commit v4 on v3

--- a/solution.py
+++ b/solution.py
@@ -41,7 +41,7 @@
 BF16 = jnp.bfloat16
 MESH = pl.DeviceIdType.MESH
 
-WIDTH = 256
+WIDTH = 512
 SUB = 64
 PIECE = 8192
 VEC_ROWS = 16
@@ -179,7 +179,9 @@
             return carry
 
         lax.fori_loop(1, 32, signal, 0)
-        pl.semaphore_wait(barrier, 31)
+
+    def await_all(self):
+        pl.semaphore_wait(pltpu.get_barrier_semaphore(), 31)
 
 
 def tell_all(spot, tiles, send_sem, recv_sem):
@@ -248,6 +250,7 @@
     lax.fori_loop(0, units // CHUNK, step, 0)
     if units % CHUNK:
         round_off(units - units % CHUNK, units % CHUNK)
+    spot.await_all()
 
     def copy(part, source, way, from_own):
         target = out_ref.at[spot.grp, source, pl.ds(*ranges[part])]
@@ -378,6 +381,7 @@
     stage, total, tiles, send_sem, recv_sem, stage_sem, out_sem, tile_send, tile_recv = refs[4 * PARTS :]
     spot = Spot()
     spot.greet()
+    spot.await_all()
 
     def slot(part, way, place, z):
         keys, depth = SLOTS[part][way]
@@ -609,6 +613,9 @@
     )(scale.reshape(1), *arrays)
 
 
+SLOTS_IN = 5
+
+
 def sections(layout, base):
     matrices, vectors = [], []
     offset = base
@@ -662,8 +669,8 @@
         end = -(-(first + length + (1 if shift else 0)) // 16) * 16
         copy = pltpu.make_async_copy(
             flat_ref.at[pl.ds(begin, end - begin)],
-            flat_in.at[index % 2, pl.ds(0, end - begin)],
-            in_sem.at[index % 2],
+            flat_in.at[index % SLOTS_IN, pl.ds(0, end - begin)],
+            in_sem.at[index % SLOTS_IN],
         )
         return copy, first - begin, end - begin
 
@@ -678,7 +685,7 @@
         step = 256
 
         def one(start, size):
-            wide[pl.ds(start, size)] = flat_in[index % 2, pl.ds(start, size)].astype(F32)
+            wide[pl.ds(start, size)] = flat_in[index % SLOTS_IN, pl.ds(start, size)].astype(F32)
 
         def loop(i, carry):
             one(pl.multiple_of(i * step, step), step)
@@ -699,8 +706,10 @@
 
         def plain(i, carry):
             row = pl.multiple_of(i * SUB, SUB)
+            packed = wide[pl.ds(phase + row * tiles, SUB * tiles)].reshape(SUB, tiles, LANES)
+            swapped = jnp.swapaxes(packed, 0, 1)
             for tile in range(tiles):
-                value = wide[pl.ds(phase + row * tiles + tile, SUB, stride=tiles)]
+                value = swapped[tile]
                 if shift:
                     after = wide[pl.ds(phase + row * tiles + tile + 1, SUB, stride=tiles)]
                     value = turned(value, after)
@@ -748,14 +757,15 @@
             vector_sem.at[n],
         )
 
-    load(0)[0].start()
+    for index in range(SLOTS_IN - 1):
+        load(index)[0].start()
     for n in range(len(windows)):
         vector_copy(n).start()
     for index, (number, start, depth, _, _) in enumerate(chunks):
         copy, phase, length = load(index)
         copy.wait()
-        if index + 1 < len(chunks):
-            load(index + 1)[0].start()
+        if index + SLOTS_IN - 1 < len(chunks):
+            load(index + SLOTS_IN - 1)[0].start()
         widen(index, length)
         if start // depth >= 2:
             store(index - 2).wait()
@@ -811,11 +821,11 @@
         out_specs=[anywhere] * len(shapes) + [vmem, vmem],
         scratch_shapes=buffers
         + [
-            pltpu.VMEM((2, PIECE + 32, LANES), BF16),
+            pltpu.VMEM((SLOTS_IN, PIECE + 32, LANES), BF16),
             pltpu.VMEM((PIECE + 32, LANES), F32),
             pltpu.VMEM((padded(HEAD) // LANES, SUB, LANES), F32),
             pltpu.VMEM((total, LANES), BF16),
-            dma((2,)),
+            dma((SLOTS_IN,)),
             dma((len(shapes), 2)),
             dma((windows,)),
         ],
@@ -844,6 +854,8 @@
     (DEC_LAYOUT, LENT, (6, 7, 8, 9, 10, 4, 5)),
 )
 PAIRS = 11
+FLIGHTS = 4
+DEPTH = 1024
 
 
 def factor_buffers(shapes):
@@ -1009,7 +1021,7 @@
 
                 lax.fori_loop(0, length // 64, turn, 0)
         length = lefts[number].shape[0]
-        sub = min(256, depth)
+        sub = min(DEPTH, depth)
 
         def loop(step, carry):
             k = pl.multiple_of(start + step * sub, sub)
@@ -1080,7 +1092,8 @@
         slot = number % 2
         buffer = rows_out.at[slot]
         if number >= 2:
-            flights[number - 2].wait()
+            for copy in flights[number - 2]:
+                copy.wait()
         first = group[0][5] // LANES if group else used // LANES
         begin = first // 8 * 8
         if tail is not None:
@@ -1100,13 +1113,22 @@
             end = groups[number + 1][0][5] if groups[number + 1] else used
             tail = (end // LANES - begin) // 8 * 8
             length = tail
-        flight = pltpu.make_async_copy(
-            buffer.at[pl.ds(0, length)], out_ref.at[pl.ds(begin, length)], out_sem.at[slot]
-        )
-        flight.start()
+        cuts = [length * n // FLIGHTS // 8 * 8 for n in range(FLIGHTS)] + [length]
+        flight = [
+            pltpu.make_async_copy(
+                buffer.at[pl.ds(lower, upper - lower)],
+                out_ref.at[pl.ds(begin + lower, upper - lower)],
+                out_sem.at[slot, n],
+            )
+            for n, (lower, upper) in enumerate(zip(cuts, cuts[1:]))
+            if upper > lower
+        ]
+        for copy in flight:
+            copy.start()
         flights.append(flight)
     for flight in flights[-2:]:
-        flight.wait()
+        for copy in flight:
+            copy.wait()
 
 
 def flat_gradient(rows, factors, enc_vectors, dec_vectors):
@@ -1125,13 +1147,13 @@
         + [
             pltpu.VMEM(enc_vectors.shape, F32),
             pltpu.VMEM(dec_vectors.shape, F32),
-            pltpu.VMEM((256, longest), BF16),
+            pltpu.VMEM((DEPTH, longest), BF16),
             pltpu.VMEM((padded(HEAD) // LANES, DD, LANES), F32),
             pltpu.VMEM((2, PIECE + 128, LANES), F32),
             dma((PAIRS, 2)),
             dma((PAIRS + 1, 2)),
             dma((PAIRS + 1, 2)),
-            dma((2,)),
+            dma((2, FLIGHTS)),
         ],
         compiler_params=pltpu.CompilerParams(
             collective_id=2, has_side_effects=True, vmem_limit_bytes=63 * 2**20

time: 718 us -> 685 us (0.954)
  Pallas kernels: 693 us -> 660 us
    pallas_call x1, Pallas kernels: 44.8 us -> 32.9 us  [weight_matrices(): pl.pallas_call(functools.partial(matrix_kernel, rows), out_shape=[jax.Sha...]
    pallas_call x1, Pallas kernels: 289 us -> 279 us  [scatter_sums(): pl.pallas_call(scatter_kernel, out_shape=(jax.ShapeDtypeStruct((units, 4,...]
    pallas_call x1, Pallas kernels: 48 us -> 38 us  [flat_gradient(): pl.pallas_call(functools.partial(product_kernel, rows, shapes), out_shape...]
where the time goes in v4:
time: 685 us; the launch traced here: 681 us
  Pallas kernels  660 us (96%)
  local copies, waits for them, and re-layouts  8.6 us (1%)
  other arithmetic  8.57 us (1%)
    pallas_call x1, Pallas kernels, scatter_sums(): pl.pallas_call(scatter_kernel, out_shape=(jax.ShapeDtypeStruct((units, 4,...  279 us
    pallas_call x1, Pallas kernels, gather_rows(): pl.pallas_call(gather_kernel, out_shape=(jax.ShapeDtypeStruct((2, 16, uni...  148 us
    pallas_call x1, Pallas kernels, decoder(): pl.pallas_call(decoder_kernel, grid=(images // BATCH,), out_shape=out_sha...  80 us
    pallas_call x1, Pallas kernels, flat_gradient(): pl.pallas_call(functools.partial(product_kernel, rows, shapes), out_shape...  38 us
    pallas_call x1, Pallas kernels, encoder_backward(): pl.pallas_call(encoder_backward_kernel, out_shape=out_shape, in_specs=[vm...  37.1 us
    pallas_call x1, Pallas kernels, encoder_forward(): pl.pallas_call(encoder_forward_kernel, out_shape=out_shape, in_specs=[vme...  33.6 us
    pallas_call x1, Pallas kernels, weight_matrices(): pl.pallas_call(functools.partial(matrix_kernel, rows), out_shape=[jax.Sha...  32.9 us

profile of v4, /device:TPU:0, one launch (start us, length us, event | category | flops | bytes accessed | tf_op | source)
XLA Modules:
  0.0 681.0 jit_solution(6104136802585608574)
XLA Ops:
  0.6 0.7 multiply_add_fusion
  1.4 0.1 iota_multiply_fusion
  1.5 0.3 multiply_sine_fusion
  1.8 0.7 pad_maximum_fusion.table
  2.4 0.7 dynamic_slice.13
  3.2 0.8 dynamic-slice_select_fusion
  3.9 0.0 copy-start
  3.9 0.8 reshape.248.spot_columns
  4.7 1.3 subtract_reduce_fusion
  6.7 0.6 broadcast_in_dim.50.masked_ref
  7.3 148.1 %gather_rows.1 = (bf16[2,16,1085,4,128]{4,3,2,1,0:T(4,128)(2,1)}, f32[8,128]{1,0:T(8,128)}) custom-call(f32[1085,4,128]{2,1,0:T(4,128)} %bitcast.20, f32[8,128]{1,0:T(8,128)} %broadcast_in_dim.50.masked_ref), custom_call_target="tpu_custom_call" | custom-call | tf_op jit(solution)/shard_map/gather_rows/pallas_call | solution.py:329
  155.4 32.9 %weight_matrices.1 = (bf16[768,1024]{1,0:T(8,128)(2,1)}, bf16[1024,3072]{1,0:T(8,128)(2,1)}, bf16[1024,4096]{1,0:T(8,128)(2,1)}, bf16[1024,512]{1,0:T(8,128)(2,1...) custom-call(bf16[138880,128]{1,0:T(8,128)(2,1)} %bitcast.17), custom_call_target="tpu_custom_call" | custom-call | tf_op jit(solution)/shard_map/weight_matrices/pallas_call | solution.py:816
  188.3 0.0 copy-done
  188.3 1.4 constant_dynamic-slice_fusion
  189.7 0.3 reshape.233
  190.0 1.1 pad.4
  191.1 33.6 %encoder_forward.1 = (bf16[256,512]{1,0:T(8,128)(2,1)}, bf16[256,768]{1,0:T(8,128)(2,1)}, f32[256,1024]{1,0:T(8,128)}, bf16[256,1024]{1,0:T(8,128)(2,1)}, bf16[2...) custom-call(bf16[832,768]{1,0:T(8,128)(2,1)} %bitcast.18, ...), custom_call_target="tpu_custom_call" | custom-call | tf_op jit(solution)/shard_map/encoder_forward/pallas_call | solution.py:1716
  224.8 0.2 multiply_sine_fusion.1
  225.0 0.6 pad_maximum_fusion.1.table
  225.6 0.4 subtract_convert_fusion
  226.0 0.2 select_convert_fusion
  226.2 0.1 pad.7.clone
  226.3 2.0 maximum_maximum_fusion.bands_w
  228.3 80.0 %decoder.1 = (bf16[832,512]{1,0:T(8,128)(2,1)}, bf16[832,1536]{1,0:T(8,128)(2,1)}, bf16[832,512]{1,0:T(8,128)(2,1)}, bf16[832,512]{1,0:T(8,128)(2,1)}, bf16[832,...) custom-call(bf16[256,512]{1,0:T(8,128)(2,1)} %get-tuple-element.69.s, ...), custom_call_target="tpu_custom_call" | custom-call | tf_op jit(solution)/shard_map/decoder/pallas_call | solution.py:1569
  308.3 37.1 %encoder_backward.1 = (bf16[256,1024]{1,0:T(8,128)(2,1)}, bf16[256,3072]{1,0:T(8,128)(2,1)}, bf16[256,1024]{1,0:T(8,128)(2,1)}, bf16[256,4096]{1,0:T(8,128)(2,1)...) custom-call(bf16[256,512]{1,0:T(8,128)(2,1)} %get-tuple-element.77.grad_sent.refs_7_, ...), custom_call_target="tpu_custom_call" | custom-call | tf_op jit(solution)/shard_map/encoder_backward/pallas_call | solution.py:1829
  345.3 38.0 %flat_gradient.1 = f32[69440,128]{1,0:T(8,128)} custom-call(bf16[256,768]{1,0:T(8,128)(2,1)} %get-tuple-element.68.refs_0_, bf16[256,1024]{1,0:T(8,128)(2,1)} %get-tuple-element.84.refs_1_, bf16[256,1024]{1,0:T(8,128)(2,1)} %get-tuple-element.85.refs_2_, bf16[256,3072]{1,0:T(8,128)(2,1)} %get-tuple-element.86.refs_3_, ...), custom_call_target="tpu_custom_call" | custom-call | tf_op jit(solution)/shard_map/flat_gradient/pallas_call | solution.py:1141
  383.4 1.2 broadcast_in_dim.57.loss_ref
  384.6 278.9 %scatter_sums.1 = (f32[1085,4,128]{2,1,0:T(4,128)}, f32[8,128]{1,0:T(8,128)}) custom-call(f32[16,1085,4,128]{3,2,1,0:T(4,128)} %bitcast.16, f32[8,128]{1,0:T(8,128)} %broadcast_in_dim.57.loss_ref), custom_call_target="tpu_custom_call" | custom-call | tf_op jit(solution)/shard_map/scatter_sums/pallas_call | solution.py:560
  663.5 1.3 slice_reduce_fusion
  665.5 11.8 %update.1 = (f32[1085,4,128]{2,1,0:T(4,128)}, f32[1085,4,128]{2,1,0:T(4,128)}, f32[1085,4,128]{2,1,0:T(4,128)}, f32[1085,4,128]{2,1,0:T(4,128)}) custom-call(f32[1]{0:T(128)} %bitcast.6.scale_ref, f32[1085,4,128]{2,1,0:T(4,128)} %get-tuple-element.108.refs_0_, f32[1085,4,128]{2,1,0:T(4,128)} %bitcast.21, f32[1085,4,128]{2,1,0:T(4,128)} %bitcast.22, ...), custom_call_target="tpu_custom_call" | custom-call | tf_op jit(solution)/shard_map/update/pallas_call | solution.py:606
  677.3 1.2 slice.10
  678.5 1.2 slice.11
  (4 shorter events, 0.0 us)
Async XLA Ops:
  3.9 184.4 %copy-start = (s32[4,64]{1,0:T(4,128)}, s32[4,64]{1,0:T(4,128)S(1)}, u32[]{:S(2)}) copy-start(s32[4,64]{1,0:T(4,128)S(1)} %dynamic-slice_select_fusion) | copy-start | bytes 3076

commit v5 on v4

--- a/solution.py
+++ b/solution.py
@@ -92,7 +92,8 @@
 OWN_FIRST = tuple(range(2 * SPLIT, 3 * SPLIT)) + tuple(range(2 * SPLIT))
 SHARES = (0.41, 0.26, 0.33)
 WAYS = ("x", "y", "up", "down")
-CHUNK = 16
+CHUNK = 64
+AXIS_SIZE = {"z": 4, "y": 2, "x": 2}
 OPPOSITE = {"x": "x", "y": "y", "up": "down", "down": "up"}
 
 
@@ -370,6 +371,14 @@
 
 SLOTS = slot_tables()
 STAGES = 4
+RING = 20
+MANY = 6
+
+
+def wide_shards(units):
+    shard = units * UNIT
+    last_matrix = sum(math.prod(shape) for shape in ENC_LAYOUT[:-2])
+    return ((last_matrix // shard, 16), (0, -(-NDEC // shard)))
 
 
 def scatter_kernel(grad_ref, loss_ref, out_ref, sums_ref, *refs):
@@ -378,10 +387,28 @@
     for part in range(PARTS):
         for number, way in enumerate(WAYS):
             landing[part, way] = refs[part * 4 + number]
-    stage, total, tiles, send_sem, recv_sem, stage_sem, out_sem, tile_send, tile_recv = refs[4 * PARTS :]
+    stage, ring, total, tiles, send_sem, recv_sem, stage_sem, out_sem, tile_send, tile_recv = refs[
+        4 * PARTS :
+    ]
     spot = Spot()
     spot.greet()
     spot.await_all()
+    bounds = wide_shards(grad_ref.shape[1])
+    z_here = spot.z
+
+    def is_wide(owner):
+        low = jnp.where(spot.grp == 0, bounds[0][0], bounds[1][0])
+        high = jnp.where(spot.grp == 0, bounds[0][1], bounds[1][1])
+        return (owner >= low) & (owner < high)
+
+    def is_split(part, way, z, owner):
+        axis = way if way in ("x", "y") else "z"
+        order = ORDERS[part]
+        chips = math.prod(AXIS_SIZE[later] for later in order[order.index(axis) + 1 :])
+        if axis != "z":
+            return True if chips >= MANY else is_wide(owner)
+        chips = chips * (z + 1 if way == "up" else DP_GRID[0] - z)
+        return is_wide(owner) | (chips >= MANY)
 
     def slot(part, way, place, z):
         keys, depth = SLOTS[part][way]
@@ -407,92 +434,159 @@
             return (dz, 0, dx)
         return (dz - 1 if way == "up" else dz + 1, dy, dx)
 
-    def send(part, place, origin):
+    def send(part, place, origin, half):
         z, owner, _ = spot.at(place)
         way = parent(part, place)
         back = OPPOSITE[way]
+        place_there = slot(part, back, seen_from_parent(part, place), z)
         return pltpu.make_async_remote_copy(
-            src_ref=origin,
-            dst_ref=landing[part, back].at[slot(part, back, seen_from_parent(part, place), z)],
-            send_sem=send_sem.at[part, owner],
-            recv_sem=recv_sem.at[part, owner, WAYS.index(back)],
+            src_ref=origin.at[half],
+            dst_ref=landing[part, back].at[place_there, half],
+            send_sem=send_sem.at[part, owner, half],
+            recv_sem=recv_sem.at[part, owner, WAYS.index(back), half],
             device_id=spot.neighbour[way],
             device_id_type=MESH,
         )
 
-    def own(part, owner):
-        return grad_ref.at[owner, pl.ds(*ranges[part])]
-
-    nodes = [(place, part) for place in relatives()[::-1] for part in range(PARTS)]
-    nodes += [((0, 0, 0), part) for part in range(PARTS)]
-    sent = []
-    inner = []
-    for place, part in nodes:
-        z, owner, inside = spot.at(place)
-        ways = onward(ORDERS[part], place)
-        if place != (0, 0, 0):
-            sent.append((part, place, owner, inside))
-        inner.append((part, place, ways, z, owner, inside))
-    staged_nodes = [node for node in inner if node[2]]
+    nodes = []
+    for place in relatives()[::-1] + [(0, 0, 0)]:
+        for part in range(PARTS):
+            z, owner, inside = spot.at(place)
+            nodes.append((part, place, onward(ORDERS[part], place), z, owner, inside))
 
     def staged(number):
-        part, _, _, _, owner, _ = staged_nodes[number]
+        part, _, _, _, owner, _ = nodes[number]
         return pltpu.make_async_copy(
-            own(part, owner),
+            grad_ref.at[owner, pl.ds(*ranges[part])],
             stage.at[number % STAGES, pl.ds(0, ranges[part][1])],
             stage_sem.at[number % STAGES],
         )
 
+    def ring_part(index, part):
+        return ring.at[index % RING, :, pl.ds(0, ranges[part][1])]
+
+    def finish_send(number):
+        part, place, _, _, owner, inside = nodes[number]
+        split = is_split(part, parent(part, place), spot.z, owner)
+
+        def finish():
+            source = ring_part(0, part)
+            send(part, place, source, 0).wait_send()
+            when(
+                None if split is True else split,
+                lambda: send(part, place, source, 1).wait_send(),
+            )
+
+        when(inside, finish)
+
     for number in range(STAGES - 1):
-        when(staged_nodes[number][5], lambda: staged(number).start())
-    number = -1
-    for part, place, ways, z, owner, inside in inner:
-        if not ways:
-            when(inside, lambda: send(part, place, own(part, owner)).start())
-            continue
-        number += 1
+        when(nodes[number][5], lambda: staged(number).start())
+    ringed = []
+    for number, (part, place, ways, z, owner, inside) in enumerate(nodes):
         ahead = number + STAGES - 1
-        if ahead < len(staged_nodes):
-            when(staged_nodes[ahead][5], lambda: staged(ahead).start())
+        if ahead < len(nodes):
+            when(nodes[ahead][5], lambda: staged(ahead).start())
         length = ranges[part][1]
         root = place == (0, 0, 0)
+        flat = [way for way in ways if way in ("x", "y")]
+        along = [way for way in ways if way in ("up", "down")]
+        if not flat:
+            if len(ringed) >= RING:
+                finish_send(ringed[-RING])
+            ringed.append(number)
+        ring_index = len(ringed) - 1
 
         def combine(arriving, number=number, part=part, place=place, z=z, owner=owner):
-            slots = []
-            for way in arriving:
-                spot_of = landing[part, way].at[slot(part, way, place, z)]
+            slots = [landing[part, way].at[slot(part, way, place, z)] for way in arriving]
+            target = slots[0] if slots else ring_part(ring_index, part)
+
+            def arrived(way, item, half):
                 pltpu.make_async_remote_copy(
-                    src_ref=spot_of,
-                    dst_ref=spot_of,
-                    send_sem=send_sem.at[part, owner],
-                    recv_sem=recv_sem.at[part, owner, WAYS.index(way)],
+                    src_ref=item.at[half],
+                    dst_ref=item.at[half],
+                    send_sem=send_sem.at[part, owner, half],
+                    recv_sem=recv_sem.at[part, owner, WAYS.index(way), half],
                     device_id=spot.neighbour[way],
                     device_id_type=MESH,
                 ).wait_recv()
-                slots.append(spot_of)
+
+            def lines(ref):
+                return ref.reshape(ref.shape[0] * 4, LANES)
+
+            mine = lines(stage.at[number % STAGES, pl.ds(0, length)])
+
+            def every(action):
+                count = 4 * length
+                some = 4 * CHUNK
+
+                def step(index, carry):
+                    action(pl.ds(pl.multiple_of(index * some, some), some))
+                    return carry
+
+                lax.fori_loop(0, count // some, step, 0)
+                if count % some:
+                    action(pl.ds(count - count % some, count % some))
+
+            def put(rows, value, split):
+                if root:
+                    lines(total.at[pl.ds(*ranges[part])])[rows] = value
+                    return
+                high = value.astype(BF16)
+                lines(target.at[0])[rows] = high
+                if split:
+                    lines(target.at[1])[rows] = (value - high.astype(F32)).astype(BF16)
+
+            def summed(rows):
+                value = mine[rows]
+                for item in slots:
+                    value = value + lines(item.at[0])[rows].astype(F32)
+                return value
+
+            for way, item in zip(arriving, slots):
+                arrived(way, item, 0)
             staged(number).wait()
-            if slots:
-                target = total.at[pl.ds(*ranges[part])] if root else slots[0]
-
-                def add(start, count):
-                    value = stage[number % STAGES, pl.ds(start, count)]
-                    for item in slots:
-                        value = value + item[pl.ds(start, count)]
-                    target[pl.ds(start, count)] = value
-
-                def step(index, carry):
-                    add(index * CHUNK, CHUNK)
-                    return carry
-
-                lax.fori_loop(0, length // CHUNK, step, 0)
-                if length % CHUNK:
-                    add(length - length % CHUNK, length % CHUNK)
+            theirs = []
+            for way in arriving:
+                there = {"up": z_here + 1, "down": z_here - 1}.get(way, z_here)
+                theirs.append(is_split(part, OPPOSITE[way], there, owner))
+            ours = False if root else is_split(part, parent(part, place), z_here, owner)
+            some_split = functools.reduce(lambda a, b: a | b, theirs + [ours])
+
+            def short():
+                every(lambda rows: put(rows, summed(rows), False))
+
+            def long():
+                def first(rows):
+                    mine[rows] = summed(rows)
+
+                if slots:
+                    every(first)
+                for way, item, split in zip(arriving, slots, theirs):
+
+                    def rest(way=way, item=item):
+                        arrived(way, item, 1)
+
+                        def one(rows):
+                            mine[rows] = mine[rows] + lines(item.at[1])[rows].astype(F32)
+
+                        every(one)
+
+                    when(None if split is True else split, rest)
+                every(lambda rows: put(rows, mine[rows], True))
+
+            if some_split is True:
+                long()
+            else:
+                pl.when(some_split)(long)
+                pl.when(jnp.logical_not(some_split))(short)
             if not root:
-                send(part, place, slots[0] if slots else own(part, owner)).start()
-
-        def choose(ways=ways, combine=combine):
-            flat = [way for way in ways if way in ("x", "y")]
-            along = [way for way in ways if way in ("up", "down")]
+                send(part, place, target, 0).start()
+                when(
+                    None if ours is True else ours,
+                    lambda: send(part, place, target, 1).start(),
+                )
+
+        def choose(flat=flat, along=along, combine=combine):
             if not along:
                 combine(flat)
             elif len(along) == 1:
@@ -527,8 +621,10 @@
     tiles[me, pl.ds(4, 4)] = loss_ref[pl.ds(4, 4)]
     tell, told = tell_all(spot, tiles, tile_send, tile_recv)
     tell()
-    for part, place, owner, inside in sent:
-        when(inside, lambda: send(part, place, own(part, owner)).wait_send())
+    done = set(ringed[:-RING])
+    for number, node in enumerate(nodes):
+        if number not in done and node[1] != (0, 0, 0):
+            finish_send(number)
     told()
     sums_ref[...] = jnp.sum(tiles[...], axis=0)
     out.wait()
@@ -541,15 +637,17 @@
     for part in range(PARTS):
         for way in WAYS:
             keys, depth = SLOTS[part][way]
-            scratch.append(pltpu.VMEM((len(keys) * depth, ranges[part][1], 4, LANES), F32))
+            shape = (len(keys) * depth, 2, ranges[part][1], 4, LANES)
+            scratch.append(pltpu.VMEM(shape, BF16))
     largest = max(length for _, length in ranges)
     dma = pltpu.SemaphoreType.DMA
     scratch += [
         pltpu.VMEM((STAGES, largest, 4, LANES), F32),
+        pltpu.VMEM((RING, 2, largest, 4, LANES), BF16),
         pltpu.VMEM((units, 4, LANES), F32),
         pltpu.VMEM((32, 8, LANES), F32),
-        dma((PARTS, 16)),
-        dma((PARTS, 16, 4)),
+        dma((PARTS, 16, 2)),
+        dma((PARTS, 16, 4, 2)),
         dma((STAGES,)),
         dma,
         dma((32,)),

time: 685 us -> 622 us (0.908)
  Pallas kernels: 660 us -> 598 us
    pallas_call x1, Pallas kernels: 279 us -> 216 us  [scatter_sums(): pl.pallas_call(scatter_kernel, out_shape=(jax.ShapeDtypeStruct((units, 4,...]
where the time goes in v5:
time: 622 us; the launch traced here: 618 us
  Pallas kernels  598 us (96%)
  local copies, waits for them, and re-layouts  8.6 us (1%)
  other arithmetic  8.57 us (1%)
    pallas_call x1, Pallas kernels, scatter_sums(): pl.pallas_call(scatter_kernel, out_shape=(jax.ShapeDtypeStruct((units, 4,...  216 us
    pallas_call x1, Pallas kernels, gather_rows(): pl.pallas_call(gather_kernel, out_shape=(jax.ShapeDtypeStruct((2, 16, uni...  148 us
    pallas_call x1, Pallas kernels, decoder(): pl.pallas_call(decoder_kernel, grid=(images // BATCH,), out_shape=out_sha...  79.9 us
    pallas_call x1, Pallas kernels, flat_gradient(): pl.pallas_call(functools.partial(product_kernel, rows, shapes), out_shape...  38.1 us
    pallas_call x1, Pallas kernels, encoder_backward(): pl.pallas_call(encoder_backward_kernel, out_shape=out_shape, in_specs=[vm...  37.1 us
    pallas_call x1, Pallas kernels, encoder_forward(): pl.pallas_call(encoder_forward_kernel, out_shape=out_shape, in_specs=[vme...  33.6 us
    pallas_call x1, Pallas kernels, weight_matrices(): pl.pallas_call(functools.partial(matrix_kernel, rows), out_shape=[jax.Sha...  32.9 us

profile of v5, /device:TPU:0, one launch (start us, length us, event | category | flops | bytes accessed | tf_op | source)
XLA Modules:
  0.0 618.2 jit_solution(15225554641685245432)
XLA Ops:
  0.6 0.7 multiply_add_fusion
  1.4 0.1 iota_multiply_fusion
  1.5 0.3 multiply_sine_fusion
  1.8 0.7 pad_maximum_fusion.table
  2.4 0.7 dynamic_slice.13
  3.2 0.8 dynamic-slice_select_fusion
  3.9 0.0 copy-start
  3.9 0.8 reshape.248.spot_columns
  4.7 1.3 subtract_reduce_fusion
  6.7 0.6 broadcast_in_dim.50.masked_ref
  7.3 148.1 %gather_rows.1 = (bf16[2,16,1085,4,128]{4,3,2,1,0:T(4,128)(2,1)}, f32[8,128]{1,0:T(8,128)}) custom-call(f32[1085,4,128]{2,1,0:T(4,128)} %bitcast.20, f32[8,128]{1,0:T(8,128)} %broadcast_in_dim.50.masked_ref), custom_call_target="tpu_custom_call" | custom-call | tf_op jit(solution)/shard_map/gather_rows/pallas_call | solution.py:330
  155.4 32.9 %weight_matrices.1 = (bf16[768,1024]{1,0:T(8,128)(2,1)}, bf16[1024,3072]{1,0:T(8,128)(2,1)}, bf16[1024,4096]{1,0:T(8,128)(2,1)}, bf16[1024,512]{1,0:T(8,128)(2,1...) custom-call(bf16[138880,128]{1,0:T(8,128)(2,1)} %bitcast.17), custom_call_target="tpu_custom_call" | custom-call | tf_op jit(solution)/shard_map/weight_matrices/pallas_call | solution.py:914
  188.3 0.0 copy-done
  188.3 1.4 constant_dynamic-slice_fusion
  189.7 0.3 reshape.233
  190.0 1.1 pad.4
  191.1 33.6 %encoder_forward.1 = (bf16[256,512]{1,0:T(8,128)(2,1)}, bf16[256,768]{1,0:T(8,128)(2,1)}, f32[256,1024]{1,0:T(8,128)}, bf16[256,1024]{1,0:T(8,128)(2,1)}, bf16[2...) custom-call(bf16[832,768]{1,0:T(8,128)(2,1)} %bitcast.18, ...), custom_call_target="tpu_custom_call" | custom-call | tf_op jit(solution)/shard_map/encoder_forward/pallas_call | solution.py:1814
  224.8 0.2 multiply_sine_fusion.1
  225.0 0.6 pad_maximum_fusion.1.table
  225.6 0.4 subtract_convert_fusion
  226.0 0.2 select_convert_fusion
  226.2 0.1 pad.7.clone
  226.3 2.0 maximum_maximum_fusion.bands_w
  228.3 79.9 %decoder.1 = (bf16[832,512]{1,0:T(8,128)(2,1)}, bf16[832,1536]{1,0:T(8,128)(2,1)}, bf16[832,512]{1,0:T(8,128)(2,1)}, bf16[832,512]{1,0:T(8,128)(2,1)}, bf16[832,...) custom-call(bf16[256,512]{1,0:T(8,128)(2,1)} %get-tuple-element.69.s, ...), custom_call_target="tpu_custom_call" | custom-call | tf_op jit(solution)/shard_map/decoder/pallas_call | solution.py:1667
  308.2 37.1 %encoder_backward.1 = (bf16[256,1024]{1,0:T(8,128)(2,1)}, bf16[256,3072]{1,0:T(8,128)(2,1)}, bf16[256,1024]{1,0:T(8,128)(2,1)}, bf16[256,4096]{1,0:T(8,128)(2,1)...) custom-call(bf16[256,512]{1,0:T(8,128)(2,1)} %get-tuple-element.77.grad_sent.refs_7_, ...), custom_call_target="tpu_custom_call" | custom-call | tf_op jit(solution)/shard_map/encoder_backward/pallas_call | solution.py:1927
  345.3 38.1 %flat_gradient.1 = f32[69440,128]{1,0:T(8,128)} custom-call(bf16[256,768]{1,0:T(8,128)(2,1)} %get-tuple-element.68.refs_0_, bf16[256,1024]{1,0:T(8,128)(2,1)} %get-tuple-element.84.refs_1_, bf16[256,1024]{1,0:T(8,128)(2,1)} %get-tuple-element.85.refs_2_, bf16[256,3072]{1,0:T(8,128)(2,1)} %get-tuple-element.86.refs_3_, ...), custom_call_target="tpu_custom_call" | custom-call | tf_op jit(solution)/shard_map/flat_gradient/pallas_call | solution.py:1239
  383.3 1.2 broadcast_in_dim.57.loss_ref
  384.6 216.1 %scatter_sums.1 = (f32[1085,4,128]{2,1,0:T(4,128)}, f32[8,128]{1,0:T(8,128)}) custom-call(f32[16,1085,4,128]{3,2,1,0:T(4,128)} %bitcast.16, f32[8,128]{1,0:T(8,128)} %broadcast_in_dim.57.loss_ref), custom_call_target="tpu_custom_call" | custom-call | tf_op jit(solution)/shard_map/scatter_sums/pallas_call | solution.py:658
  600.7 1.3 slice_reduce_fusion
  602.7 11.8 %update.1 = (f32[1085,4,128]{2,1,0:T(4,128)}, f32[1085,4,128]{2,1,0:T(4,128)}, f32[1085,4,128]{2,1,0:T(4,128)}, f32[1085,4,128]{2,1,0:T(4,128)}) custom-call(f32[1]{0:T(128)} %bitcast.6.scale_ref, f32[1085,4,128]{2,1,0:T(4,128)} %get-tuple-element.108.refs_0_, f32[1085,4,128]{2,1,0:T(4,128)} %bitcast.21, f32[1085,4,128]{2,1,0:T(4,128)} %bitcast.22, ...), custom_call_target="tpu_custom_call" | custom-call | tf_op jit(solution)/shard_map/update/pallas_call | solution.py:704
  614.5 1.2 slice.10
  615.7 1.2 slice.11
  (4 shorter events, 0.0 us)
Async XLA Ops:
  3.9 184.4 %copy-start = (s32[4,64]{1,0:T(4,128)}, s32[4,64]{1,0:T(4,128)S(1)}, u32[]{:S(2)}) copy-start(s32[4,64]{1,0:T(4,128)S(1)} %dynamic-slice_select_fusion) | copy-start | bytes 3076

commit v6 on v5

--- a/solution.py
+++ b/solution.py
@@ -3,6 +3,8 @@
 
 import jax
 import jax.numpy as jnp
+import ml_dtypes
+import numpy as np
 from jax import lax
 from jax.experimental import pallas as pl
 from jax.experimental.pallas import tpu as pltpu
@@ -168,49 +170,60 @@
         inside = None if place[0] == 0 else (z >= 0) & (z <= 3)
         return z, self.index(z, y, x), inside
 
-    def greet(self):
+    def greet(self, everyone):
         barrier = pltpu.get_barrier_semaphore()
-        me = self.grp * 16 + self.dp
 
         def signal(step, carry):
-            other = (me + step) % 32
             pl.semaphore_signal(
-                barrier, inc=1, device_id=(other // 16, other % 16), device_id_type=MESH
+                barrier, inc=1, device_id=self.partner(step, everyone), device_id_type=MESH
             )
             return carry
 
-        lax.fori_loop(1, 32, signal, 0)
-
-    def await_all(self):
-        pl.semaphore_wait(pltpu.get_barrier_semaphore(), 31)
-
-
-def tell_all(spot, tiles, send_sem, recv_sem):
-    me = spot.grp * 16 + spot.dp
-
-    def copy(number, other):
+        lax.fori_loop(1, 32 if everyone else 16, signal, 0)
+        if not everyone:
+            sibling = self.neighbour["core"]
+            pl.semaphore_signal(barrier, inc=1, device_id=sibling, device_id_type=MESH)
+
+    def await_all(self, everyone):
+        pl.semaphore_wait(pltpu.get_barrier_semaphore(), 31 if everyone else 16)
+
+    def number(self, everyone):
+        return self.grp * 16 + self.dp if everyone else self.dp
+
+    def partner(self, step, everyone):
+        if everyone:
+            other = (self.number(True) + step) % 32
+            return (other // 16, other % 16)
+        return (self.grp, (self.dp + step) % 16)
+
+
+def tell_all(spot, tiles, send_sem, recv_sem, everyone):
+    me = spot.number(everyone)
+    count = 32 if everyone else 16
+
+    def copy(number, other, target):
         return pltpu.make_async_remote_copy(
             src_ref=tiles.at[number],
             dst_ref=tiles.at[number],
             send_sem=send_sem.at[other],
             recv_sem=recv_sem.at[number],
-            device_id=(other // 16, other % 16),
+            device_id=target,
             device_id_type=MESH,
         )
 
     def start(step, carry):
-        copy(me, (me + step) % 32).start()
+        copy(me, (me + step) % count, spot.partner(step, everyone)).start()
         return carry
 
     def finish(step, carry):
-        other = (me + step) % 32
-        copy(other, other).wait_recv()
-        copy(me, other).wait_send()
+        other = (me + step) % count
+        copy(other, other, spot.partner(step, everyone)).wait_recv()
+        copy(me, other, spot.partner(step, everyone)).wait_send()
         return carry
 
     return (
-        lambda: lax.fori_loop(1, 32, start, 0),
-        lambda: lax.fori_loop(1, 32, finish, 0),
+        lambda: lax.fori_loop(1, count, start, 0),
+        lambda: lax.fori_loop(1, count, finish, 0),
     )
 
 
@@ -233,25 +246,24 @@
     spot = Spot()
     read = pltpu.make_async_copy(master_ref, master, local_sem)
     read.start()
-    tiles[spot.grp * 16 + spot.dp] = masked_ref[...]
-    spot.greet()
-    tell, told = tell_all(spot, tiles, tile_send, tile_recv)
+    tiles[spot.dp] = masked_ref[...]
+    spot.greet(False)
+    tell, told = tell_all(spot, tiles, tile_send, tile_recv, False)
     ranges = part_ranges(own_ref.shape[0])
     read.wait()
 
     def round_off(start, length):
-        block = pl.ds(start, length)
-        own_ref[block] = master[block].astype(BF16)
-
-    def step(index, carry):
-        round_off(index * CHUNK, CHUNK)
-        return carry
-
-    units = own_ref.shape[0]
-    lax.fori_loop(0, units // CHUNK, step, 0)
-    if units % CHUNK:
-        round_off(units - units % CHUNK, units % CHUNK)
-    spot.await_all()
+        def one(first, count):
+            block = pl.ds(first, count)
+            own_ref[block] = master[block].astype(BF16)
+
+        def step(index, carry):
+            one(start + index * CHUNK, CHUNK)
+            return carry
+
+        lax.fori_loop(0, length // CHUNK, step, 0)
+        if length % CHUNK:
+            one(start + length - length % CHUNK, length % CHUNK)
 
     def copy(part, source, way, from_own):
         target = out_ref.at[spot.grp, source, pl.ds(*ranges[part])]
@@ -271,6 +283,9 @@
 
     sent = []
     for part in OWN_FIRST:
+        round_off(*ranges[part])
+        if part == OWN_FIRST[0]:
+            spot.await_all(False)
         for way in onward(ORDERS[part], (0, 0, 0)):
             when(
                 spot.exists[way],
@@ -318,7 +333,7 @@
 
     lax.fori_loop(0, 16, await_core, 0)
     told()
-    masked_out[...] = jnp.sum(tiles[pl.ds(0, 16)], axis=0)
+    masked_out[...] = jnp.sum(tiles[...], axis=0)
     local.wait()
 
 
@@ -338,14 +353,14 @@
         scratch_shapes=[
             pltpu.VMEM((units, 4, LANES), F32),
             pltpu.VMEM((units, 4, LANES), BF16),
-            pltpu.VMEM((32, 8, LANES), F32),
+            pltpu.VMEM((16, 8, LANES), F32),
             dma,
             dma((PARTS, 16, 4)),
             dma((PARTS, 16)),
             dma((PARTS, 16)),
             dma((PARTS, 16)),
-            dma((32,)),
-            dma((32,)),
+            dma((16,)),
+            dma((16,)),
         ],
         compiler_params=pltpu.CompilerParams(collective_id=0, has_side_effects=True),
         name="gather_rows",
@@ -391,8 +406,8 @@
         4 * PARTS :
     ]
     spot = Spot()
-    spot.greet()
-    spot.await_all()
+    spot.greet(True)
+    spot.await_all(True)
     bounds = wide_shards(grad_ref.shape[1])
     z_here = spot.z
 
@@ -619,7 +634,7 @@
     me = spot.grp * 16 + spot.dp
     tiles[me, pl.ds(0, 4)] = squares
     tiles[me, pl.ds(4, 4)] = loss_ref[pl.ds(4, 4)]
-    tell, told = tell_all(spot, tiles, tile_send, tile_recv)
+    tell, told = tell_all(spot, tiles, tile_send, tile_recv, True)
     tell()
     done = set(ringed[:-RING])
     for number, node in enumerate(nodes):
@@ -682,33 +697,42 @@
     return new_params, new_first, new_second, new_average
 
 
-def update_kernel(scale_ref, *refs):
-    scale = scale_ref[0]
+def update_kernel(sums_ref, masked_ref, *refs):
+    squares = jnp.sum(sums_ref[pl.ds(0, 4)], axis=0, keepdims=True)
+    norm = jnp.sqrt(jnp.sum(squares, axis=1, keepdims=True))
+    scale = jnp.minimum(1.0, CLIP / norm)
     step = 31
 
     def one(index, carry):
         block = pl.ds(index * step, step)
         owned, params, first, second, average = [ref[block] for ref in refs[:5]]
-        values = update_values(owned, scale, params, first, second, average)
-        for out, value in zip(refs[5:], values):
+        values = update_values(owned, scale[None], params, first, second, average)
+        for out, value in zip(refs[5:9], values):
             out[block] = value
         return carry
 
     lax.fori_loop(0, refs[0].shape[0] // step, one, 0)
-
-
-def update(scale, arrays):
+    loss_ref, total_ref, norm_ref = refs[9:]
+    loss_ref[...] = sums_ref[pl.ds(4, 1), pl.ds(0, 1)]
+    total_ref[...] = masked_ref[pl.ds(0, 1), pl.ds(0, 1)]
+    norm_ref[...] = norm
+
+
+def update(sums, masked, arrays):
     units = arrays[0].shape[0]
     depth = 155
     spec = pl.BlockSpec((depth, 4, LANES), lambda i: (i, 0, 0))
+    tile = pl.BlockSpec((8, LANES), lambda i: (0, 0))
+    scalar = pl.BlockSpec((1, 1), lambda i: (0, 0))
     return pl.pallas_call(
         update_kernel,
         grid=(units // depth,),
-        out_shape=[jax.ShapeDtypeStruct((units, 4, LANES), F32)] * 4,
-        in_specs=[pl.BlockSpec(memory_space=pltpu.SMEM)] + [spec] * 5,
-        out_specs=[spec] * 4,
+        out_shape=[jax.ShapeDtypeStruct((units, 4, LANES), F32)] * 4
+        + [jax.ShapeDtypeStruct((1, 1), F32)] * 3,
+        in_specs=[tile, tile] + [spec] * 5,
+        out_specs=[spec] * 4 + [scalar] * 3,
         name="update",
-    )(scale.reshape(1), *arrays)
+    )(sums, masked, *arrays)
 
 
 SLOTS_IN = 5
@@ -789,7 +813,7 @@
             one(pl.multiple_of(i * step, step), step)
             return carry
 
-        lax.fori_loop(0, length // step, loop, 0)
+        lax.fori_loop(0, length // step, loop, 0, unroll=2)
         if length % step:
             one(length - length % step, length % step)
 
@@ -833,7 +857,7 @@
                 block[pl.ds(pl.multiple_of(i * SUB, SUB), SUB), lanes] = pairs[tile].astype(BF16)
             return carry
 
-        lax.fori_loop(0, depth // SUB, paired if columns % LANES else plain, 0)
+        lax.fori_loop(0, depth // SUB, paired if columns % LANES else plain, 0, unroll=4)
 
     windows = []
     wanted = [(0, n, v) for n, v in enumerate(enc_vectors)]
@@ -1158,7 +1182,8 @@
                         buffer[pl.ds(row + tile, sub, stride=tiles)] = part
                 return carry
 
-            lax.fori_loop(0, tiles * LANES // width, across, 0)
+            count = tiles * LANES // width
+            lax.fori_loop(0, count, across, 0, unroll=2 if count % 2 == 0 else 1)
             return carry
 
         lax.fori_loop(0, depth // sub, loop, 0)
@@ -1283,7 +1308,8 @@
         action(pl.ds(pl.multiple_of(index * size, size), size))
         return carry
 
-    lax.fori_loop(0, length // size, step, 0)
+    count = length // size
+    lax.fori_loop(0, count, step, 0, unroll=2 if count % 2 == 0 else 1)
 
 
 def row_step(length):
@@ -1380,7 +1406,7 @@
         mixed[rows, lanes(0)] = total.astype(BF16)
         return carry
 
-    lax.fori_loop(0, images * groups, one, 0)
+    lax.fori_loop(0, images * groups, one, 0, unroll=4)
 
 
 def attention_backward(
@@ -1420,11 +1446,11 @@
         out[rows, lanes(0)] = (total * scale).astype(BF16)
         return carry
 
-    lax.fori_loop(0, images * groups, one, 0)
+    lax.fori_loop(0, images * groups, one, 0, unroll=4)
 
 
 def columns_loop(columns, size, action):
-    blocks(columns, min(size, columns), action)
+    blocks(columns, min(2 * size, columns), action)
 
 
 def feed_forward(normed_two, fc1_w, fc2_w, vectors, middle, pre, active, state):
@@ -1565,13 +1591,13 @@
         square = miss * miss
         root = jnp.sqrt(square + 1.0)
         unseen = 1.0 - seen[...]
-        loss[...] += jnp.sum(jnp.where(low, square, root - 1.0) * unseen).reshape(1, 1)
+        loss[...] += jnp.sum(jnp.where(low, square, root - 1.0) * unseen)
         slope = jnp.where(low, 2.0 * miss, miss / root) * (unseen * weight)
         rounded = slope.astype(BF16)
         grad_predicted[:, part] = rounded
         sums[pl.ds(LAST_B, 1), part] += jnp.sum(rounded.astype(F32), axis=0, keepdims=True)
 
-    columns_loop(head_w.shape[1], GROUP, predict)
+    blocks(head_w.shape[1], GROUP, predict)
 
     def head_back(part):
         spare[:, part] = dot_nt(grad_predicted[...], head_w[part])
@@ -1660,7 +1686,7 @@
     out_shape = [jax.ShapeDtypeStruct((images * GPAD, columns), BF16) for columns in widths]
     out_shape.append(jax.ShapeDtypeStruct((images * VMAX, DD), BF16))
     out_shape.append(jax.ShapeDtypeStruct((VEC_ROWS, VEC_COLS[1]), F32))
-    out_shape.append(jax.ShapeDtypeStruct((1, 1), F32))
+    out_shape.append(jax.ShapeDtypeStruct((8, LANES), F32))
     operands = [masked_tile, bands_w, vectors, *weights]
     f32 = lambda *shape: pltpu.VMEM(shape, F32)
     b16 = lambda *shape: pltpu.VMEM(shape, BF16)
@@ -1947,13 +1973,12 @@
 
 
 def band_matrix():
-    ids = jnp.arange(PIX, dtype=jnp.int32)
+    ids = np.arange(PIX)
     coarse = (ids // (3 * PSIDE) // 2 * (PSIDE // 2) + ids // 3 % PSIDE // 2) * 3 + ids % 3
-    low = jnp.where(coarse[:, None] == jnp.arange(LOWPIX, dtype=jnp.int32)[None], 0.25, 0.0)
-    same = jnp.where(coarse[:, None] == coarse[None], 0.25, 0.0)
-    high = jnp.where(ids[:, None] == ids[None], 1.0, 0.0) - same
-    rest = jnp.zeros((PIX, padded(HEAD) - HEAD), F32)
-    return jnp.concatenate([low, high, rest], axis=1).astype(BF16)
+    low = np.where(coarse[:, None] == np.arange(LOWPIX)[None], 0.25, 0.0)
+    high = np.eye(PIX) - np.where(coarse[:, None] == coarse[None], 0.25, 0.0)
+    rest = np.zeros((PIX, padded(HEAD) - HEAD))
+    return jnp.asarray(np.concatenate([low, high, rest], axis=1).astype(ml_dtypes.bfloat16))
 
 
 def turn_table(scales, width):
@@ -2004,11 +2029,7 @@
     )
     factors = [patches, grad_state, normed_one, grad_qkv, normed_two, grad_pre]
     factors += [normed_last, grad_sent, mixed, grad_middle, active, grad_out]
-    return factors + dec_factors, enc_sums, dec_sums, loss[0, 0]
-
-
-def clip_scale(squares):
-    return jnp.minimum(1.0, CLIP / jnp.sqrt(squares))
+    return factors + dec_factors, enc_sums, dec_sums, loss
 
 
 def body(
@@ -2034,7 +2055,7 @@
         return lax.dynamic_slice_in_dim(array, core * count, count, 0)
 
     scales = 0.5 + 0.25 * mine(gsd_id, half).astype(F32)
-    factors, enc_sums, dec_sums, loss_local = forward_backward(
+    factors, enc_sums, dec_sums, loss_tile = forward_backward(
         parts,
         mine(pixels, half * GRID),
         mine(visible_index, half),
@@ -2044,19 +2065,17 @@
     )
     gradient = flat_gradient(chips * rows, factors, enc_sums, dec_sums)
     if special:
-        owned, sums = scatter_sums(
-            gradient.reshape(chips, rows // 4, 4, LANES), jnp.full((8, LANES), loss_local)
-        )
-        squares = jnp.sum(sums[:4])
-        loss_sum = sums[4, 0]
-        outs = update(clip_scale(squares), [owned] + shards)
-        outs = [out.reshape(params.shape) for out in outs]
-    else:
-        owned = lax.psum_scatter(gradient, "dp", scatter_dimension=0, tiled=True)
-        owned = owned.reshape(params.shape)
-        squares, loss_sum = lax.psum((jnp.sum(owned * owned), loss_local), ("grp", "dp"))
-        outs = update_values(owned, clip_scale(squares), params, first_moment, second_moment, average)
-    return (*outs, loss_sum, masked_tile[0, 0], jnp.sqrt(squares))
+        owned, sums = scatter_sums(gradient.reshape(chips, rows // 4, 4, LANES), loss_tile)
+        outs = update(sums, masked_tile, [owned] + shards)
+        outs = [out.reshape(params.shape) for out in outs[:4]] + [out.reshape(()) for out in outs[4:]]
+        return tuple(outs)
+    owned = lax.psum_scatter(gradient, "dp", scatter_dimension=0, tiled=True)
+    owned = owned.reshape(params.shape)
+    squares, loss_sum = lax.psum((jnp.sum(owned * owned), loss_tile[0, 0]), ("grp", "dp"))
+    norm = jnp.sqrt(squares)
+    scale = jnp.minimum(1.0, CLIP / norm)
+    outs = update_values(owned, scale, params, first_moment, second_moment, average)
+    return (*outs, loss_sum, masked_tile[0, 0], norm)
 
 
 def solution(mesh):

time: 622 us -> 560 us (0.900)
  Pallas kernels: 598 us -> 545 us
    pallas_call x1, Pallas kernels: 79.9 us -> 54.4 us  [decoder(): pl.pallas_call(decoder_kernel, grid=(images // BATCH,), out_shape=out_sha...]
    pallas_call x1, Pallas kernels: 216 us -> 205 us  [scatter_sums(): pl.pallas_call(scatter_kernel, out_shape=(jax.ShapeDtypeStruct((units, 4,...]
    pallas_call x1, Pallas kernels: 33.6 us -> 24.5 us  [encoder_forward(): pl.pallas_call(encoder_forward_kernel, out_shape=out_shape, in_specs=[vme...]
    pallas_call x1, Pallas kernels: 38.1 us -> 45.6 us  [flat_gradient(): pl.pallas_call(functools.partial(product_kernel, rows, shapes), out_shape...]
    pallas_call x1, Pallas kernels: 37.1 us -> 29.7 us  [encoder_backward(): pl.pallas_call(encoder_backward_kernel, out_shape=out_shape, in_specs=[vm...]
where the time goes in v6:
time: 560 us; the launch traced here: 556 us
  Pallas kernels  545 us (97%)
    pallas_call x1, Pallas kernels, scatter_sums(): pl.pallas_call(scatter_kernel, out_shape=(jax.ShapeDtypeStruct((units, 4,...  205 us
    pallas_call x1, Pallas kernels, gather_rows(): pl.pallas_call(gather_kernel, out_shape=(jax.ShapeDtypeStruct((2, 16, uni...  146 us
    pallas_call x1, Pallas kernels, decoder(): pl.pallas_call(decoder_kernel, grid=(images // BATCH,), out_shape=out_sha...  54.4 us
    pallas_call x1, Pallas kernels, flat_gradient(): pl.pallas_call(functools.partial(product_kernel, rows, shapes), out_shape...  45.6 us
    pallas_call x1, Pallas kernels, encoder_backward(): pl.pallas_call(encoder_backward_kernel, out_shape=out_shape, in_specs=[vm...  29.7 us
    pallas_call x1, Pallas kernels, weight_matrices(): pl.pallas_call(functools.partial(matrix_kernel, rows), out_shape=[jax.Sha...  27.5 us
    pallas_call x1, Pallas kernels, encoder_forward(): pl.pallas_call(encoder_forward_kernel, out_shape=out_shape, in_specs=[vme...  24.5 us
    pallas_call x1, Pallas kernels, update(): pl.pallas_call(update_kernel, grid=(units // depth,), out_shape=[jax.Shap...  12.2 us

profile of v6, /device:TPU:0, one launch (start us, length us, event | category | flops | bytes accessed | tf_op | source)
XLA Modules:
  0.0 556.0 jit_solution(799591239032340629)
XLA Ops:
  0.6 0.7 multiply_add_fusion
  1.4 0.1 iota_multiply_fusion
  1.5 0.3 multiply_sine_fusion
  1.8 0.7 pad_maximum_fusion.table
  2.4 0.7 dynamic_slice.13
  3.2 0.8 dynamic-slice_select_fusion
  3.9 0.0 copy-start
  3.9 0.8 reshape.116.spot_columns
  4.7 1.3 subtract_reduce_fusion
  6.6 0.6 broadcast_in_dim.7.masked_ref
  7.2 146.0 %gather_rows.1 = (bf16[2,16,1085,4,128]{4,3,2,1,0:T(4,128)(2,1)}, f32[8,128]{1,0:T(8,128)}) custom-call(f32[1085,4,128]{2,1,0:T(4,128)} %bitcast.19, f32[8,128]{1,0:T(8,128)} %broadcast_in_dim.7.masked_ref), custom_call_target="tpu_custom_call" | custom-call | tf_op jit(solution)/shard_map/gather_rows/pallas_call | solution.py:345
  153.3 27.5 %weight_matrices.1 = (bf16[768,1024]{1,0:T(8,128)(2,1)}, bf16[1024,3072]{1,0:T(8,128)(2,1)}, bf16[1024,4096]{1,0:T(8,128)(2,1)}, bf16[1024,512]{1,0:T(8,128)(2,1...) custom-call(bf16[138880,128]{1,0:T(8,128)(2,1)} %bitcast.16), custom_call_target="tpu_custom_call" | custom-call | tf_op jit(solution)/shard_map/weight_matrices/pallas_call | solution.py:938
  180.8 0.0 copy-done
  180.8 1.4 constant_dynamic-slice_fusion
  182.1 0.3 reshape.99
  182.4 1.2 pad.4
  183.7 24.5 %encoder_forward.1 = (bf16[256,512]{1,0:T(8,128)(2,1)}, bf16[256,768]{1,0:T(8,128)(2,1)}, f32[256,1024]{1,0:T(8,128)}, bf16[256,1024]{1,0:T(8,128)(2,1)}, bf16[2...) custom-call(bf16[832,768]{1,0:T(8,128)(2,1)} %bitcast.17, ...), custom_call_target="tpu_custom_call" | custom-call | tf_op jit(solution)/shard_map/encoder_forward/pallas_call | solution.py:1840
  208.1 0.2 multiply_sine_fusion.1
  208.3 0.6 pad_maximum_fusion.1.table
  209.0 54.4 %decoder.1 = (bf16[832,512]{1,0:T(8,128)(2,1)}, bf16[832,1536]{1,0:T(8,128)(2,1)}, bf16[832,512]{1,0:T(8,128)(2,1)}, bf16[832,512]{1,0:T(8,128)(2,1)}, bf16[832,...) custom-call(bf16[256,512]{1,0:T(8,128)(2,1)} %get-tuple-element.72.s, ...), custom_call_target="tpu_custom_call" | custom-call | tf_op jit(solution)/shard_map/decoder/pallas_call | solution.py:1693
  263.4 29.7 %encoder_backward.1 = (bf16[256,1024]{1,0:T(8,128)(2,1)}, bf16[256,3072]{1,0:T(8,128)(2,1)}, bf16[256,1024]{1,0:T(8,128)(2,1)}, bf16[256,4096]{1,0:T(8,128)(2,1)...) custom-call(bf16[256,512]{1,0:T(8,128)(2,1)} %get-tuple-element.80.grad_sent.refs_7_, ...), custom_call_target="tpu_custom_call" | custom-call | tf_op jit(solution)/shard_map/encoder_backward/pallas_call | solution.py:1953
  293.1 45.6 %flat_gradient.1 = f32[69440,128]{1,0:T(8,128)} custom-call(bf16[256,768]{1,0:T(8,128)(2,1)} %get-tuple-element.71.refs_0_, bf16[256,1024]{1,0:T(8,128)(2,1)} %get-tuple-element.87.refs_1_, bf16[256,1024]{1,0:T(8,128)(2,1)} %get-tuple-element.88.refs_2_, bf16[256,3072]{1,0:T(8,128)(2,1)} %get-tuple-element.89.refs_3_, ...), custom_call_target="tpu_custom_call" | custom-call | tf_op jit(solution)/shard_map/flat_gradient/pallas_call | solution.py:1264
  338.7 204.9 %scatter_sums.1 = (f32[1085,4,128]{2,1,0:T(4,128)}, f32[8,128]{1,0:T(8,128)}) custom-call(f32[16,1085,4,128]{3,2,1,0:T(4,128)} %bitcast.15, f32[8,128]{1,0:T(8,128)} %get-tuple-element.109.loss_ref), custom_call_target="tpu_custom_call" | custom-call | tf_op jit(solution)/shard_map/scatter_sums/pallas_call | solution.py:673
  543.6 12.2 %update.1 = (f32[1085,4,128]{2,1,0:T(4,128)}, f32[1085,4,128]{2,1,0:T(4,128)}, f32[1085,4,128]{2,1,0:T(4,128)}, f32[1085,4,128]{2,1,0:T(4,128)}, f32[1,1]{1,0:T(1,128)}, /*index=5*/f32[1,1]{1,0:T(1,128)}, f32[1,1]{1,0:T(1,128)}) custom-call(f32[8,128]{1,0:T(8,128)} %get-tuple-element.110.sums_ref, f32[8,128]{1,0:T(8,128)} %get-tuple-element.73.masked_ref, ...), custom_call_target="tpu_custom_call" | custom-call | tf_op jit(solution)/shard_map/update/pallas_call | solution.py:727
  (2 shorter events, 0.0 us)
Async XLA Ops:
  3.9 176.9 %copy-start = (s32[4,64]{1,0:T(4,128)}, s32[4,64]{1,0:T(4,128)S(1)}, u32[]{:S(2)}) copy-start(s32[4,64]{1,0:T(4,128)S(1)} %dynamic-slice_select_fusion) | copy-start | bytes 3076

commit v7 on v6

--- a/solution.py
+++ b/solution.py
@@ -385,8 +385,8 @@
 
 
 SLOTS = slot_tables()
-STAGES = 4
-RING = 20
+STAGES = 3
+RING = 28
 MANY = 6
 
 
@@ -1309,7 +1309,8 @@
         return carry
 
     count = length // size
-    lax.fori_loop(0, count, step, 0, unroll=2 if count % 2 == 0 else 1)
+    unroll = 4 if count % 4 == 0 else 2 if count % 2 == 0 else 1
+    lax.fori_loop(0, count, step, 0, unroll=unroll)
 
 
 def row_step(length):

time: 560 us -> 540 us (0.964)
  Pallas kernels: 545 us -> 524 us
    pallas_call x1, Pallas kernels: 205 us -> 190 us  [scatter_sums(): pl.pallas_call(scatter_kernel, out_shape=(jax.ShapeDtypeStruct((units, 4,...]
where the time goes in v7:
time: 540 us; the launch traced here: 535 us
  Pallas kernels  524 us (97%)
    pallas_call x1, Pallas kernels, scatter_sums(): pl.pallas_call(scatter_kernel, out_shape=(jax.ShapeDtypeStruct((units, 4,...  190 us
    pallas_call x1, Pallas kernels, gather_rows(): pl.pallas_call(gather_kernel, out_shape=(jax.ShapeDtypeStruct((2, 16, uni...  146 us
    pallas_call x1, Pallas kernels, decoder(): pl.pallas_call(decoder_kernel, grid=(images // BATCH,), out_shape=out_sha...  49 us
    pallas_call x1, Pallas kernels, flat_gradient(): pl.pallas_call(functools.partial(product_kernel, rows, shapes), out_shape...  45.6 us
    pallas_call x1, Pallas kernels, encoder_backward(): pl.pallas_call(encoder_backward_kernel, out_shape=out_shape, in_specs=[vm...  29.3 us
    pallas_call x1, Pallas kernels, weight_matrices(): pl.pallas_call(functools.partial(matrix_kernel, rows), out_shape=[jax.Sha...  27.5 us
    pallas_call x1, Pallas kernels, encoder_forward(): pl.pallas_call(encoder_forward_kernel, out_shape=out_shape, in_specs=[vme...  24.1 us
    pallas_call x1, Pallas kernels, update(): pl.pallas_call(update_kernel, grid=(units // depth,), out_shape=[jax.Shap...  12.2 us

profile of v7, /device:TPU:0, one launch (start us, length us, event | category | flops | bytes accessed | tf_op | source)
XLA Modules:
  0.0 535.4 jit_solution(1658703010743530386)
XLA Ops:
  0.6 0.7 multiply_add_fusion
  1.4 0.1 iota_multiply_fusion
  1.5 0.3 multiply_sine_fusion
  1.8 0.7 pad_maximum_fusion.table
  2.4 0.7 dynamic_slice.13
  3.2 0.8 dynamic-slice_select_fusion
  3.9 0.0 copy-start
  3.9 0.8 reshape.116.spot_columns
  4.7 1.3 subtract_reduce_fusion
  6.6 0.6 broadcast_in_dim.7.masked_ref
  7.2 146.0 %gather_rows.1 = (bf16[2,16,1085,4,128]{4,3,2,1,0:T(4,128)(2,1)}, f32[8,128]{1,0:T(8,128)}) custom-call(f32[1085,4,128]{2,1,0:T(4,128)} %bitcast.19, f32[8,128]{1,0:T(8,128)} %broadcast_in_dim.7.masked_ref), custom_call_target="tpu_custom_call" | custom-call | tf_op jit(solution)/shard_map/gather_rows/pallas_call | solution.py:345
  153.3 27.5 %weight_matrices.1 = (bf16[768,1024]{1,0:T(8,128)(2,1)}, bf16[1024,3072]{1,0:T(8,128)(2,1)}, bf16[1024,4096]{1,0:T(8,128)(2,1)}, bf16[1024,512]{1,0:T(8,128)(2,1...) custom-call(bf16[138880,128]{1,0:T(8,128)(2,1)} %bitcast.16), custom_call_target="tpu_custom_call" | custom-call | tf_op jit(solution)/shard_map/weight_matrices/pallas_call | solution.py:938
  180.8 0.0 copy-done
  180.8 1.4 constant_dynamic-slice_fusion
  182.1 0.3 reshape.99
  182.4 1.2 pad.4
  183.7 24.1 %encoder_forward.1 = (bf16[256,512]{1,0:T(8,128)(2,1)}, bf16[256,768]{1,0:T(8,128)(2,1)}, f32[256,1024]{1,0:T(8,128)}, bf16[256,1024]{1,0:T(8,128)(2,1)}, bf16[2...) custom-call(bf16[832,768]{1,0:T(8,128)(2,1)} %bitcast.17, ...), custom_call_target="tpu_custom_call" | custom-call | tf_op jit(solution)/shard_map/encoder_forward/pallas_call | solution.py:1841
  207.8 0.2 multiply_sine_fusion.1
  208.0 0.6 pad_maximum_fusion.1.table
  208.6 49.0 %decoder.1 = (bf16[832,512]{1,0:T(8,128)(2,1)}, bf16[832,1536]{1,0:T(8,128)(2,1)}, bf16[832,512]{1,0:T(8,128)(2,1)}, bf16[832,512]{1,0:T(8,128)(2,1)}, bf16[832,...) custom-call(bf16[256,512]{1,0:T(8,128)(2,1)} %get-tuple-element.72.s, ...), custom_call_target="tpu_custom_call" | custom-call | tf_op jit(solution)/shard_map/decoder/pallas_call | solution.py:1694
  257.7 29.3 %encoder_backward.1 = (bf16[256,1024]{1,0:T(8,128)(2,1)}, bf16[256,3072]{1,0:T(8,128)(2,1)}, bf16[256,1024]{1,0:T(8,128)(2,1)}, bf16[256,4096]{1,0:T(8,128)(2,1)...) custom-call(bf16[256,512]{1,0:T(8,128)(2,1)} %get-tuple-element.80.grad_sent.refs_7_, ...), custom_call_target="tpu_custom_call" | custom-call | tf_op jit(solution)/shard_map/encoder_backward/pallas_call | solution.py:1954
  287.0 45.6 %flat_gradient.1 = f32[69440,128]{1,0:T(8,128)} custom-call(bf16[256,768]{1,0:T(8,128)(2,1)} %get-tuple-element.71.refs_0_, bf16[256,1024]{1,0:T(8,128)(2,1)} %get-tuple-element.87.refs_1_, bf16[256,1024]{1,0:T(8,128)(2,1)} %get-tuple-element.88.refs_2_, bf16[256,3072]{1,0:T(8,128)(2,1)} %get-tuple-element.89.refs_3_, ...), custom_call_target="tpu_custom_call" | custom-call | tf_op jit(solution)/shard_map/flat_gradient/pallas_call | solution.py:1264
  332.6 190.4 %scatter_sums.1 = (f32[1085,4,128]{2,1,0:T(4,128)}, f32[8,128]{1,0:T(8,128)}) custom-call(f32[16,1085,4,128]{3,2,1,0:T(4,128)} %bitcast.15, f32[8,128]{1,0:T(8,128)} %get-tuple-element.109.loss_ref), custom_call_target="tpu_custom_call" | custom-call | tf_op jit(solution)/shard_map/scatter_sums/pallas_call | solution.py:673
  523.0 12.2 %update.1 = (f32[1085,4,128]{2,1,0:T(4,128)}, f32[1085,4,128]{2,1,0:T(4,128)}, f32[1085,4,128]{2,1,0:T(4,128)}, f32[1085,4,128]{2,1,0:T(4,128)}, f32[1,1]{1,0:T(1,128)}, /*index=5*/f32[1,1]{1,0:T(1,128)}, f32[1,1]{1,0:T(1,128)}) custom-call(f32[8,128]{1,0:T(8,128)} %get-tuple-element.110.sums_ref, f32[8,128]{1,0:T(8,128)} %get-tuple-element.73.masked_ref, ...), custom_call_target="tpu_custom_call" | custom-call | tf_op jit(solution)/shard_map/update/pallas_call | solution.py:727
  (2 shorter events, 0.0 us)
Async XLA Ops:
  3.9 176.9 %copy-start = (s32[4,64]{1,0:T(4,128)}, s32[4,64]{1,0:T(4,128)S(1)}, u32[]{:S(2)}) copy-start(s32[4,64]{1,0:T(4,128)S(1)} %dynamic-slice_select_fusion) | copy-start | bytes 3076

commit v8 on v7

--- a/solution.py
+++ b/solution.py
@@ -386,7 +386,7 @@
 
 SLOTS = slot_tables()
 STAGES = 3
-RING = 28
+RING = 30
 MANY = 6
 
 
@@ -720,7 +720,7 @@
 
 def update(sums, masked, arrays):
     units = arrays[0].shape[0]
-    depth = 155
+    depth = 217
     spec = pl.BlockSpec((depth, 4, LANES), lambda i: (i, 0, 0))
     tile = pl.BlockSpec((8, LANES), lambda i: (0, 0))
     scalar = pl.BlockSpec((1, 1), lambda i: (0, 0))
@@ -1049,11 +1049,11 @@
     def act(role):
         remote_vectors(1 - role).start()
         pending = [(number, side) for number in ROLES[role][2] for side in range(2)]
-        for number, side in pending:
-            local(role, number, side).start()
         given = [(number, side) for number in ROLES[1 - role][2] for side in range(2)]
         for number, side in given:
             remote(1 - role, number, side).start()
+        for number, side in pending:
+            local(role, number, side).start()
         remote_vectors(role).wait_recv()
 
         def ready(number):

time: 540 us -> 539 us (level)
  no operation moved by 1% of the time
where the time goes in v8:
time: 539 us; the launch traced here: 535 us
  Pallas kernels  523 us (97%)
    pallas_call x1, Pallas kernels, scatter_sums(): pl.pallas_call(scatter_kernel, out_shape=(jax.ShapeDtypeStruct((units, 4,...  190 us
    pallas_call x1, Pallas kernels, gather_rows(): pl.pallas_call(gather_kernel, out_shape=(jax.ShapeDtypeStruct((2, 16, uni...  146 us
    pallas_call x1, Pallas kernels, decoder(): pl.pallas_call(decoder_kernel, grid=(images // BATCH,), out_shape=out_sha...  49 us
    pallas_call x1, Pallas kernels, flat_gradient(): pl.pallas_call(functools.partial(product_kernel, rows, shapes), out_shape...  45.5 us
    pallas_call x1, Pallas kernels, encoder_backward(): pl.pallas_call(encoder_backward_kernel, out_shape=out_shape, in_specs=[vm...  29.3 us
    pallas_call x1, Pallas kernels, weight_matrices(): pl.pallas_call(functools.partial(matrix_kernel, rows), out_shape=[jax.Sha...  27.5 us
    pallas_call x1, Pallas kernels, encoder_forward(): pl.pallas_call(encoder_forward_kernel, out_shape=out_shape, in_specs=[vme...  24.1 us
    pallas_call x1, Pallas kernels, update(): pl.pallas_call(update_kernel, grid=(units // depth,), out_shape=[jax.Shap...  11.5 us

profile of v8, /device:TPU:0, one launch (start us, length us, event | category | flops | bytes accessed | tf_op | source)
XLA Modules:
  0.0 534.6 jit_solution(1665690405662263272)
XLA Ops:
  0.6 0.7 multiply_add_fusion
  1.4 0.1 iota_multiply_fusion
  1.5 0.3 multiply_sine_fusion
  1.8 0.7 pad_maximum_fusion.table
  2.4 0.7 dynamic_slice.13
  3.2 0.8 dynamic-slice_select_fusion
  3.9 0.0 copy-start
  3.9 0.8 reshape.116.spot_columns
  4.7 1.3 subtract_reduce_fusion
  6.6 0.6 broadcast_in_dim.7.masked_ref
  7.2 146.0 %gather_rows.1 = (bf16[2,16,1085,4,128]{4,3,2,1,0:T(4,128)(2,1)}, f32[8,128]{1,0:T(8,128)}) custom-call(f32[1085,4,128]{2,1,0:T(4,128)} %bitcast.19, f32[8,128]{1,0:T(8,128)} %broadcast_in_dim.7.masked_ref), custom_call_target="tpu_custom_call" | custom-call | tf_op jit(solution)/shard_map/gather_rows/pallas_call | solution.py:345
  153.3 27.5 %weight_matrices.1 = (bf16[768,1024]{1,0:T(8,128)(2,1)}, bf16[1024,3072]{1,0:T(8,128)(2,1)}, bf16[1024,4096]{1,0:T(8,128)(2,1)}, bf16[1024,512]{1,0:T(8,128)(2,1...) custom-call(bf16[138880,128]{1,0:T(8,128)(2,1)} %bitcast.16), custom_call_target="tpu_custom_call" | custom-call | tf_op jit(solution)/shard_map/weight_matrices/pallas_call | solution.py:938
  180.8 0.0 copy-done
  180.8 1.4 constant_dynamic-slice_fusion
  182.1 0.3 reshape.99
  182.4 1.2 pad.4
  183.7 24.1 %encoder_forward.1 = (bf16[256,512]{1,0:T(8,128)(2,1)}, bf16[256,768]{1,0:T(8,128)(2,1)}, f32[256,1024]{1,0:T(8,128)}, bf16[256,1024]{1,0:T(8,128)(2,1)}, bf16[2...) custom-call(bf16[832,768]{1,0:T(8,128)(2,1)} %bitcast.17, ...), custom_call_target="tpu_custom_call" | custom-call | tf_op jit(solution)/shard_map/encoder_forward/pallas_call | solution.py:1841
  207.8 0.2 multiply_sine_fusion.1
  208.0 0.6 pad_maximum_fusion.1.table
  208.6 49.0 %decoder.1 = (bf16[832,512]{1,0:T(8,128)(2,1)}, bf16[832,1536]{1,0:T(8,128)(2,1)}, bf16[832,512]{1,0:T(8,128)(2,1)}, bf16[832,512]{1,0:T(8,128)(2,1)}, bf16[832,...) custom-call(bf16[256,512]{1,0:T(8,128)(2,1)} %get-tuple-element.72.s, ...), custom_call_target="tpu_custom_call" | custom-call | tf_op jit(solution)/shard_map/decoder/pallas_call | solution.py:1694
  257.7 29.3 %encoder_backward.1 = (bf16[256,1024]{1,0:T(8,128)(2,1)}, bf16[256,3072]{1,0:T(8,128)(2,1)}, bf16[256,1024]{1,0:T(8,128)(2,1)}, bf16[256,4096]{1,0:T(8,128)(2,1)...) custom-call(bf16[256,512]{1,0:T(8,128)(2,1)} %get-tuple-element.80.grad_sent.refs_7_, ...), custom_call_target="tpu_custom_call" | custom-call | tf_op jit(solution)/shard_map/encoder_backward/pallas_call | solution.py:1954
  287.0 45.5 %flat_gradient.1 = f32[69440,128]{1,0:T(8,128)} custom-call(bf16[256,768]{1,0:T(8,128)(2,1)} %get-tuple-element.71.refs_0_, bf16[256,1024]{1,0:T(8,128)(2,1)} %get-tuple-element.87.refs_1_, bf16[256,1024]{1,0:T(8,128)(2,1)} %get-tuple-element.88.refs_2_, bf16[256,3072]{1,0:T(8,128)(2,1)} %get-tuple-element.89.refs_3_, ...), custom_call_target="tpu_custom_call" | custom-call | tf_op jit(solution)/shard_map/flat_gradient/pallas_call | solution.py:1264
  332.6 190.3 %scatter_sums.1 = (f32[1085,4,128]{2,1,0:T(4,128)}, f32[8,128]{1,0:T(8,128)}) custom-call(f32[16,1085,4,128]{3,2,1,0:T(4,128)} %bitcast.15, f32[8,128]{1,0:T(8,128)} %get-tuple-element.109.loss_ref), custom_call_target="tpu_custom_call" | custom-call | tf_op jit(solution)/shard_map/scatter_sums/pallas_call | solution.py:673
  522.9 11.5 %update.1 = (f32[1085,4,128]{2,1,0:T(4,128)}, f32[1085,4,128]{2,1,0:T(4,128)}, f32[1085,4,128]{2,1,0:T(4,128)}, f32[1085,4,128]{2,1,0:T(4,128)}, f32[1,1]{1,0:T(1,128)}, /*index=5*/f32[1,1]{1,0:T(1,128)}, f32[1,1]{1,0:T(1,128)}) custom-call(f32[8,128]{1,0:T(8,128)} %get-tuple-element.110.sums_ref, f32[8,128]{1,0:T(8,128)} %get-tuple-element.73.masked_ref, ...), custom_call_target="tpu_custom_call" | custom-call | tf_op jit(solution)/shard_map/update/pallas_call | solution.py:727
  (2 shorter events, 0.0 us)
Async XLA Ops:
  3.9 176.9 %copy-start = (s32[4,64]{1,0:T(4,128)}, s32[4,64]{1,0:T(4,128)S(1)}, u32[]{:S(2)}) copy-start(s32[4,64]{1,0:T(4,128)S(1)} %dynamic-slice_select_fusion) | copy-start | bytes 3076
